TPU v7x, 32 devices: a whole 2x2x4 slice. The times are simulated.
32 devices in a mesh: ctx: 16 (over z, y, core), fsdp: 2 (over x).
Axes of the slice: x: 2, y: 2, z: 4, core: 2. Of those that a mesh axis runs over, the one named last changes fastest.
Arguments:
- tokens: bfloat16 [2, 2048, 2048], P('fsdp', 'ctx'), may hold values from -6 to 6
- cotangent: float32 [2, 2048, 2048], P('fsdp', 'ctx'), may hold values from -6 to 6
- lengths: int32 [2, 4], P('fsdp'), may hold values from 1 to 1024, 2048 in all within a row
- token_order: int32 [2, 2048], P('fsdp'), may hold values from 0 to 2047, as said below
- routes: int32 [2, 2048, 6], P('fsdp', 'ctx'), may hold values from 0 to 15, all different within a row; in each aligned block of 128 rows (0 to 127, 128 to 255, ..., all dimensions but the last counted through in order) at most 64 rows name the same one
- first_gain: float32 [2048], P(('ctx', 'fsdp')), may hold values from 0.1 to 1.9
- latent_gain: float32 [512], P(('ctx', 'fsdp')), may hold values from 0.1 to 1.9
- query_weight: float32 [2048, 3072], P(('ctx', 'fsdp')), may hold values from -0.125 to 0.125
- compress_weight: float32 [2048, 576], P(('ctx', 'fsdp')), may hold values from -0.125 to 0.125
- expand_weight: float32 [512, 4096], P(('ctx', 'fsdp')), may hold values from -0.25 to 0.25
- output_weight: float32 [2048, 2048], P(('ctx', 'fsdp')), may hold values from -0.75 to 0.75
- second_gain: float32 [2048], P(('ctx', 'fsdp')), may hold values from 0.1 to 1.9
- router_weight: float32 [2048, 16], P(('ctx', 'fsdp')), may hold values from -0.0625 to 0.0625
- shared_gate: float32 [2048, 2816], P(('ctx', 'fsdp')), may hold values from -0.125 to 0.125
- shared_up: float32 [2048, 2816], P(('ctx', 'fsdp')), may hold values from -0.125 to 0.125
- shared_down: float32 [2048, 2816], P(('ctx', 'fsdp')), may hold values from -0.109375 to 0.109375
- expert_gate: float32 [16, 2048, 1408], P('ctx', 'fsdp'), may hold values from -0.125 to 0.125
- expert_up: float32 [16, 2048, 1408], P('ctx', 'fsdp'), may hold values from -0.125 to 0.125
- expert_down: float32 [16, 2048, 1408], P('ctx', 'fsdp'), may hold values from -1.25 to 1.25
Outputs:
- output: float32 [2, 2048, 2048], P('fsdp', 'ctx')
- grad_tokens: float32 [2, 2048, 2048], P('fsdp', 'ctx')
- grad_first_gain: float32 [2048], P(('ctx', 'fsdp'))
- grad_latent_gain: float32 [512], P(('ctx', 'fsdp'))
- grad_query_weight: float32 [2048, 3072], P(('ctx', 'fsdp'))
- grad_compress_weight: float32 [2048, 576], P(('ctx', 'fsdp'))
- grad_expand_weight: float32 [512, 4096], P(('ctx', 'fsdp'))
- grad_output_weight: float32 [2048, 2048], P(('ctx', 'fsdp'))
- grad_second_gain: float32 [2048], P(('ctx', 'fsdp'))
- grad_router_weight: float32 [2048, 16], P(('ctx', 'fsdp'))
- grad_shared_gate: float32 [2048, 2816], P(('ctx', 'fsdp'))
- grad_shared_up: float32 [2048, 2816], P(('ctx', 'fsdp'))
- grad_shared_down: float32 [2048, 2816], P(('ctx', 'fsdp'))
- grad_expert_gate: float32 [16, 2048, 1408], P('ctx', 'fsdp')
- grad_expert_up: float32 [16, 2048, 1408], P('ctx', 'fsdp')
- grad_expert_down: float32 [16, 2048, 1408], P('ctx', 'fsdp')
Inputs may be any that keep to these rules, and one draw needn't show every extreme that they name: `token_order`: each row holds every number below 2048 exactly once. The lengths of a row add up to 2048; the largest is exactly 1024. `routes`: each token names 6 different experts; among the 128 tokens of one device no expert is named more than 64 times, and in every draw some device names some expert exactly 64 times.
All inputs are finite; a program needn't handle non-finite values.
Results may differ from a plain program's by a relative error of at most 0.035.
Values may be sent and summed in bfloat16 or wider, within the bound.
A program may use at most 448 MiB of HBM per device.

v0:
```python
import jax
import jax.numpy as jnp
from jax import lax
from jax.sharding import PartitionSpec as P

D = 2048
HEADS = 16
NOPE = 128
ROPE = 64
VDIM = 128
LATENT = 512
TOP = 6


EPS = 1e-06
NEGATIVE = -1e30


def shifted(shard, axis, by):
    devices = lax.axis_size(axis)
    return lax.ppermute(shard, axis, [(i, (i + by) % devices) for i in range(devices)])


def matmul(left, right):
    return jnp.dot(left, right, preferred_element_type=jnp.float32)


def contract_last(left, right):
    return lax.dot_general(
        left, right, (((1,), (1,)), ((), ())), preferred_element_type=jnp.float32
    )


def leading_contraction(left, right):
    return lax.dot_general(
        left, right, (((0,), (0,)), ((), ())), preferred_element_type=jnp.float32
    )


def rms_norm(value, gain):
    return value * lax.rsqrt(jnp.mean(value * value, -1, keepdims=True) + EPS) * gain


def rotate(value, position):
    half = value.shape[-1] // 2
    freq = 10000.0 ** (-jnp.arange(half, dtype=jnp.float32) / half)
    angle = position.astype(jnp.float32)[:, None] * freq[None, :]
    cosine = jnp.cos(angle)[:, None, :]
    sine = jnp.sin(angle)[:, None, :]
    first = value[..., :half]
    second = value[..., half:]
    return jnp.concatenate([first * cosine - second * sine, first * sine + second * cosine], -1)


def placement(lengths_row, order_row):
    ends = jnp.cumsum(lengths_row)
    starts = ends - lengths_row
    sequence = jnp.sum((order_row[:, None] >= ends[None, :]).astype(jnp.int32), 1)
    chosen = sequence[:, None] == jnp.arange(lengths_row.shape[0], dtype=jnp.int32)[None, :]
    offset = jnp.sum(jnp.where(chosen, starts[None, :], 0), 1)
    return (sequence, order_row - offset)


def expert_slots(route_rows, experts):
    flat = route_rows.reshape(-1)
    onehot = (flat[:, None] == jnp.arange(experts, dtype=jnp.int32)[None, :]).astype(jnp.int32)
    before = jnp.cumsum(onehot, 0) - onehot
    return (flat, jnp.sum(before * onehot, 1))


def swiglu(gate_value, up_value):
    return jax.nn.silu(gate_value) * up_value


def softmax_last(value):
    return jax.nn.softmax(value, -1)


def local(
    tokens,
    cotangent,
    lengths,
    token_order,
    routes,
    first_gain,
    latent_gain,
    query_weight,
    compress_weight,
    expand_weight,
    output_weight,
    second_gain,
    router_weight,
    shared_gate,
    shared_up,
    shared_down,
    expert_gate,
    expert_up,
    expert_down,
):
    (
        gain_first,
        gain_latent,
        query_full,
        compress_full,
        expand_full,
        output_full,
        gain_second,
        router_full,
        shared_gate_full,
        shared_up_full,
        shared_down_full,
    ) = (
        lax.all_gather(first_gain.astype(jnp.bfloat16), ("ctx", "fsdp"), axis=0, tiled=True),
        lax.all_gather(latent_gain.astype(jnp.bfloat16), ("ctx", "fsdp"), axis=0, tiled=True),
        lax.all_gather(query_weight.astype(jnp.bfloat16), ("ctx", "fsdp"), axis=0, tiled=True),
        lax.all_gather(compress_weight.astype(jnp.bfloat16), ("ctx", "fsdp"), axis=0, tiled=True),
        lax.all_gather(expand_weight.astype(jnp.bfloat16), ("ctx", "fsdp"), axis=0, tiled=True),
        lax.all_gather(output_weight.astype(jnp.bfloat16), ("ctx", "fsdp"), axis=0, tiled=True),
        lax.all_gather(second_gain.astype(jnp.bfloat16), ("ctx", "fsdp"), axis=0, tiled=True),
        lax.all_gather(router_weight.astype(jnp.bfloat16), ("ctx", "fsdp"), axis=0, tiled=True),
        lax.all_gather(shared_gate.astype(jnp.bfloat16), ("ctx", "fsdp"), axis=0, tiled=True),
        lax.all_gather(shared_up.astype(jnp.bfloat16), ("ctx", "fsdp"), axis=0, tiled=True),
        lax.all_gather(shared_down.astype(jnp.bfloat16), ("ctx", "fsdp"), axis=0, tiled=True),
    )
    gate_expert, up_expert, down_expert = (
        lax.all_gather(expert_gate.astype(jnp.bfloat16), "fsdp", axis=1, tiled=True),
        lax.all_gather(expert_up.astype(jnp.bfloat16), "fsdp", axis=1, tiled=True),
        lax.all_gather(expert_down.astype(jnp.bfloat16), "fsdp", axis=1, tiled=True),
    )
    gate_expert = gate_expert[0]
    up_expert = up_expert[0]
    down_expert = down_expert[0]
    rows = tokens.shape[1]
    place = lax.axis_index("ctx")
    devices = lax.axis_size("ctx")
    query_width = NOPE + ROPE
    sequence, position = placement(lengths[0], token_order[0])
    own_seq = lax.dynamic_slice_in_dim(sequence, place * rows, rows)
    own_pos = lax.dynamic_slice_in_dim(position, place * rows, rows)

    def visible_mask(start, count):
        key_seq = lax.dynamic_slice_in_dim(sequence, start, count)
        key_pos = lax.dynamic_slice_in_dim(position, start, count)
        return (own_seq[:, None] == key_seq[None, :]) & (key_pos[None, :] <= own_pos[:, None])

    def turn_query(part):
        return rotate(part, own_pos)

    def turn_key(part):
        return rotate(part[:, None, :], own_pos)[:, 0, :]

    hidden = tokens[0].astype(jnp.float32)
    normed_f, norm_pull = jax.vjp(rms_norm, hidden, gain_first.astype(jnp.float32))
    normed = normed_f.astype(jnp.bfloat16)
    query_raw = matmul(normed, query_full).reshape(rows, HEADS, query_width)
    query_rotated, query_pull = jax.vjp(turn_query, query_raw[..., NOPE:])
    query = jnp.concatenate([query_raw[..., :NOPE], query_rotated], -1).astype(jnp.bfloat16)
    compressed = matmul(normed, compress_full)
    latent_f, latent_pull = jax.vjp(
        rms_norm, compressed[:, :LATENT], gain_latent.astype(jnp.float32)
    )
    latent = latent_f.astype(jnp.bfloat16)
    expanded = matmul(latent, expand_full).reshape(rows, HEADS, NOPE + VDIM)
    key_rot, key_pull = jax.vjp(turn_key, compressed[:, LATENT:])
    keys = jnp.concatenate(
        [expanded[..., :NOPE], jnp.broadcast_to(key_rot[:, None, :], (rows, HEADS, ROPE))], -1
    )
    keys = keys.astype(jnp.bfloat16).reshape(rows, HEADS * query_width)
    values = expanded[..., NOPE:].astype(jnp.bfloat16).reshape(rows, HEADS * VDIM)
    scale = query_width ** (-0.5)
    running = jnp.full((HEADS, rows), NEGATIVE, jnp.float32)
    key_piece = lax.all_gather(keys, "ctx", axis=0, tiled=True)
    value_piece = lax.all_gather(values, "ctx", axis=0, tiled=True)
    count = key_piece.shape[0]
    scores = (
        jnp.einsum(
            "qhd,khd->hqk",
            query,
            key_piece.reshape(count, HEADS, query_width),
            preferred_element_type=jnp.float32,
        )
        * scale
    )
    visible = visible_mask(jnp.int32(0), count)[None]
    masked = jnp.where(visible, scores, NEGATIVE)
    newest = jnp.maximum(running, jnp.max(masked, -1))
    weights = jnp.where(visible, jnp.exp(masked - newest[..., None]), 0.0)
    total = jnp.sum(weights, -1)
    summed = jnp.einsum(
        "hqk,khd->qhd",
        weights.astype(jnp.bfloat16),
        value_piece.reshape(count, HEADS, VDIM),
        preferred_element_type=jnp.float32,
    )
    running, total, summed = (newest, total, summed)
    mixed_f = summed / jnp.transpose(total)[:, :, None]
    logsum = running + jnp.log(total)
    mixed = mixed_f.astype(jnp.bfloat16).reshape(rows, HEADS * VDIM)
    residual = hidden + contract_last(mixed, output_full)
    normed_two_f, norm_two_pull = jax.vjp(rms_norm, residual, gain_second.astype(jnp.float32))
    normed_two = normed_two_f.astype(jnp.bfloat16)
    logits = matmul(normed_two, router_full)
    experts = router_full.shape[1]
    route_rows = routes[0]
    pick = (route_rows[:, :, None] == jnp.arange(experts, dtype=jnp.int32)[None, None, :]).astype(
        jnp.float32
    )
    router_probs, gate_pull = jax.vjp(softmax_last, logits)
    gates = jnp.sum(pick * router_probs[:, None, :], -1)
    shared_gate_val = matmul(normed_two, shared_gate_full)
    shared_up_val = matmul(normed_two, shared_up_full)
    shared_hidden = swiglu(shared_gate_val, shared_up_val).astype(jnp.bfloat16)
    shared_out = contract_last(shared_hidden, shared_down_full)
    capacity = rows * TOP * 4 // (3 * experts)
    flat, slot = expert_slots(route_rows, experts)
    anchor = jnp.arange(rows * TOP, dtype=jnp.int32) // TOP
    outgoing = (
        jnp.zeros((experts, capacity, D), jnp.bfloat16).at[flat, slot].set(normed_two[anchor])
    )
    arrived = lax.all_to_all(outgoing, "ctx", split_axis=0, concat_axis=0, tiled=True)
    received_rows = arrived.reshape(-1, D)
    gate_val = matmul(received_rows, gate_expert)
    up_val = matmul(received_rows, up_expert)
    expert_hidden = swiglu(gate_val, up_val).astype(jnp.bfloat16)
    produced = contract_last(expert_hidden, down_expert).astype(jnp.bfloat16).reshape(arrived.shape)
    returned = lax.all_to_all(produced, "ctx", split_axis=0, concat_axis=0, tiled=True)
    route_out = returned[flat, slot].astype(jnp.float32).reshape(rows, TOP, D)
    routed = jnp.sum(gates[:, :, None] * route_out, 1)
    output = residual + routed + shared_out
    grad_out = cotangent[0]
    grad_low = grad_out.astype(jnp.bfloat16)
    grad_shared_hidden = matmul(grad_low, shared_down_full)
    grad_sdown = leading_contraction(grad_low, shared_hidden)
    grad_sg, grad_su = jax.vjp(swiglu, shared_gate_val, shared_up_val)[1](grad_shared_hidden)
    grad_sg = grad_sg.astype(jnp.bfloat16)
    grad_su = grad_su.astype(jnp.bfloat16)
    grad_sgate = leading_contraction(normed_two, grad_sg)
    grad_sup = leading_contraction(normed_two, grad_su)
    grad_normed_two = contract_last(grad_sg, shared_gate_full) + contract_last(
        grad_su, shared_up_full
    )
    grad_gates = jnp.sum(grad_out[:, None, :] * route_out, -1)
    grad_route = (
        (gates[:, :, None] * grad_out[:, None, :]).astype(jnp.bfloat16).reshape(rows * TOP, D)
    )
    grad_outgoing = jnp.zeros((experts, capacity, D), jnp.bfloat16).at[flat, slot].set(grad_route)
    grad_arrived = lax.all_to_all(
        grad_outgoing, "ctx", split_axis=0, concat_axis=0, tiled=True
    ).reshape(-1, D)
    grad_expert_hidden = matmul(grad_arrived, down_expert)
    grad_edown = leading_contraction(grad_arrived, expert_hidden)
    grad_eg, grad_expert_up_value = jax.vjp(swiglu, gate_val, up_val)[1](grad_expert_hidden)
    grad_eg = grad_eg.astype(jnp.bfloat16)
    grad_expert_up_value = grad_expert_up_value.astype(jnp.bfloat16)
    grad_egate = leading_contraction(received_rows, grad_eg)
    grad_expert_up_partial = leading_contraction(received_rows, grad_expert_up_value)
    grad_rows = (
        contract_last(grad_eg, gate_expert) + contract_last(grad_expert_up_value, up_expert)
    ).astype(jnp.bfloat16)
    grad_back = lax.all_to_all(
        grad_rows.reshape(arrived.shape), "ctx", split_axis=0, concat_axis=0, tiled=True
    )
    grad_normed_two = grad_normed_two + jnp.sum(
        grad_back[flat, slot].astype(jnp.float32).reshape(rows, TOP, D), 1
    )
    expert_parts = (
        lax.psum_scatter(
            grad_egate[None].astype(jnp.bfloat16), "fsdp", scatter_dimension=1, tiled=True
        ).astype(jnp.float32),
        lax.psum_scatter(
            grad_expert_up_partial[None].astype(jnp.bfloat16),
            "fsdp",
            scatter_dimension=1,
            tiled=True,
        ).astype(jnp.float32),
        lax.psum_scatter(
            grad_edown[None].astype(jnp.bfloat16), "fsdp", scatter_dimension=1, tiled=True
        ).astype(jnp.float32),
    )
    grad_router_probs = jnp.sum(pick * grad_gates[:, :, None], 1)
    grad_logits = gate_pull(grad_router_probs)[0].astype(jnp.bfloat16)
    grad_normed_two = grad_normed_two + contract_last(grad_logits, router_full)
    grad_router = leading_contraction(normed_two, grad_logits)
    grad_residual_norm, grad_gain_second = norm_two_pull(grad_normed_two)
    grad_residual = grad_out + grad_residual_norm
    grad_attended = grad_residual.astype(jnp.bfloat16)
    grad_mixed = matmul(grad_attended, output_full).astype(jnp.bfloat16).reshape(rows, HEADS, VDIM)
    grad_output_w = leading_contraction(grad_attended, mixed)
    delta = jnp.transpose(jnp.sum(grad_mixed.astype(jnp.float32) * mixed_f, -1))

    def rotation_loop_step(step, carry):
        key_block, value_block, grad_key, grad_value, grad_query = carry
        start = (place - step) % devices * rows
        keyed = key_block.reshape(rows, HEADS, query_width)
        valued = value_block.reshape(rows, HEADS, VDIM)
        scores = (
            jnp.einsum("qhd,khd->hqk", query, keyed, preferred_element_type=jnp.float32) * scale
        )
        visible = visible_mask(start, rows)[None]
        weights = jnp.where(visible, jnp.exp(scores - logsum[:, :, None]), 0.0)
        weights_low = weights.astype(jnp.bfloat16)
        grad_weights = jnp.einsum(
            "qhd,khd->hqk", grad_mixed, valued, preferred_element_type=jnp.float32
        )
        grad_scores = (weights * (grad_weights - delta[:, :, None])).astype(jnp.bfloat16)
        grad_query = grad_query + scale * jnp.einsum(
            "hqk,khd->qhd", grad_scores, keyed, preferred_element_type=jnp.float32
        )
        grad_key = grad_key + scale * jnp.einsum(
            "hqk,qhd->khd", grad_scores, query, preferred_element_type=jnp.float32
        )
        grad_value = grad_value + jnp.einsum(
            "hqk,qhd->khd", weights_low, grad_mixed, preferred_element_type=jnp.float32
        )
        grad_key, grad_value = (
            shifted(grad_key.astype(jnp.bfloat16), "ctx", 1).astype(grad_key.dtype),
            shifted(grad_value.astype(jnp.bfloat16), "ctx", 1).astype(grad_value.dtype),
        )
        key_block, value_block = shifted((key_block, value_block), "ctx", 1)
        return (key_block, value_block, grad_key, grad_value, grad_query)

    cycle_start = (
        keys,
        values,
        jnp.zeros((rows, HEADS, query_width), jnp.float32),
        jnp.zeros((rows, HEADS, VDIM), jnp.float32),
        jnp.zeros((rows, HEADS, query_width), jnp.float32),
    )
    cycle_end = lax.fori_loop(0, devices, rotation_loop_step, cycle_start)
    grad_key = cycle_end[2]
    grad_value = cycle_end[3]
    grad_query = cycle_end[4]
    grad_key_rotary = jnp.sum(grad_key[..., NOPE:], 1)
    grad_expanded_latent = jnp.concatenate([grad_key[..., :NOPE], grad_value], -1)
    grad_expanded_latent = grad_expanded_latent.reshape(rows, HEADS * (NOPE + VDIM)).astype(
        jnp.bfloat16
    )
    grad_latent = contract_last(grad_expanded_latent, expand_full)
    grad_expand_w = leading_contraction(latent, grad_expanded_latent)
    grad_comp_latent, grad_gain_latent = latent_pull(grad_latent)
    grad_comp_rope = key_pull(grad_key_rotary)[0]
    grad_compressed = jnp.concatenate([grad_comp_latent, grad_comp_rope], -1).astype(jnp.bfloat16)
    grad_query_rope = query_pull(grad_query[..., NOPE:])[0]
    grad_query_raw = jnp.concatenate([grad_query[..., :NOPE], grad_query_rope], -1)
    grad_query_raw = grad_query_raw.reshape(rows, HEADS * query_width).astype(jnp.bfloat16)
    grad_normed = contract_last(grad_query_raw, query_full) + contract_last(
        grad_compressed, compress_full
    )
    grad_query_w = leading_contraction(normed, grad_query_raw)
    grad_compress_w = leading_contraction(normed, grad_compressed)
    grad_hidden_norm, grad_gain_first = norm_pull(grad_normed)
    grad_input = grad_residual + grad_hidden_norm
    dense_parts = (
        lax.psum_scatter(grad_gain_first, ("ctx", "fsdp"), scatter_dimension=0, tiled=True),
        lax.psum_scatter(grad_gain_latent, ("ctx", "fsdp"), scatter_dimension=0, tiled=True),
        lax.psum_scatter(grad_query_w, ("ctx", "fsdp"), scatter_dimension=0, tiled=True),
        lax.psum_scatter(grad_compress_w, ("ctx", "fsdp"), scatter_dimension=0, tiled=True),
        lax.psum_scatter(grad_expand_w, ("ctx", "fsdp"), scatter_dimension=0, tiled=True),
        lax.psum_scatter(grad_output_w, ("ctx", "fsdp"), scatter_dimension=0, tiled=True),
        lax.psum_scatter(grad_gain_second, ("ctx", "fsdp"), scatter_dimension=0, tiled=True),
        lax.psum_scatter(grad_router, ("ctx", "fsdp"), scatter_dimension=0, tiled=True),
        lax.psum_scatter(grad_sgate, ("ctx", "fsdp"), scatter_dimension=0, tiled=True),
        lax.psum_scatter(grad_sup, ("ctx", "fsdp"), scatter_dimension=0, tiled=True),
        lax.psum_scatter(grad_sdown, ("ctx", "fsdp"), scatter_dimension=0, tiled=True),
    )
    return (
        output[None],
        grad_input[None],
        dense_parts[0],
        dense_parts[1],
        dense_parts[2],
        dense_parts[3],
        dense_parts[4],
        dense_parts[5],
        dense_parts[6],
        dense_parts[7],
        dense_parts[8],
        dense_parts[9],
        dense_parts[10],
        expert_parts[0],
        expert_parts[1],
        expert_parts[2],
    )


def solution(mesh):
    in_specs = (
        P("fsdp", "ctx", None),
        P("fsdp", "ctx", None),
        P("fsdp", None),
        P("fsdp", None),
        P("fsdp", "ctx", None),
        P(("ctx", "fsdp")),
        P(("ctx", "fsdp")),
        P(("ctx", "fsdp"), None),
        P(("ctx", "fsdp"), None),
        P(("ctx", "fsdp"), None),
        P(("ctx", "fsdp"), None),
        P(("ctx", "fsdp")),
        P(("ctx", "fsdp"), None),
        P(("ctx", "fsdp"), None),
        P(("ctx", "fsdp"), None),
        P(("ctx", "fsdp"), None),
        P("ctx", "fsdp", None),
        P("ctx", "fsdp", None),
        P("ctx", "fsdp", None),
    )
    out_specs = (
        P("fsdp", "ctx", None),
        P("fsdp", "ctx", None),
        P(("ctx", "fsdp")),
        P(("ctx", "fsdp")),
        P(("ctx", "fsdp"), None),
        P(("ctx", "fsdp"), None),
        P(("ctx", "fsdp"), None),
        P(("ctx", "fsdp"), None),
        P(("ctx", "fsdp")),
        P(("ctx", "fsdp"), None),
        P(("ctx", "fsdp"), None),
        P(("ctx", "fsdp"), None),
        P(("ctx", "fsdp"), None),
        P("ctx", "fsdp", None),
        P("ctx", "fsdp", None),
        P("ctx", "fsdp", None),
    )
    return jax.shard_map(local, mesh=mesh, in_specs=in_specs, out_specs=out_specs, check_vma=False)
```

profile of v0, /device:TPU:0, one launch (start us, length us, event | category | flops | bytes accessed | tf_op | source)
XLA Modules:
  0.0 4329.1 jit_solution(870965542376122503)
XLA Ops:
  13.2 42.4 all-reduce.11
  57.0 15.3 all-gather.14.cloned.1.call-done
  75.5 61.4 %all-gather.16.cloned.1.call-done = bf16[512,4096]{1,0:T(8,128)(2,1)} async-done(((bf16[16,4096]{1,0:T(8,128)(2,1)}), bf16[512,4096]{1,0:T(8,128)(2,1)}) %all-gather.16.cloned.1.call-update) | async-done | bytes 4194320 | tf_op jit(solution)/shard_map/all_gather | solution.py:117
  163.4 68.0 %all-gather = bf16[32,64,16]{1,2,0:T(8,128)(2,1)S(1)} all-gather(bf16[1,64,16]{1,2,0:T(8,128)(2,1)S(1)} %convert_bitcast_fusion.1), channel_id=1, replica_groups=mesh['ctx'=16,'fsdp'=2] {'ctx','fsdp'}, dimensions={0}, use_global_device_ids=true | all-gather | bytes 67584 | tf_op jit(solution)/shard_map/all_gather | solution.py:120
  247.5 12.3 copy.108
  259.8 53.4 %all-gather.20.cloned.1.call-done = bf16[2048,3072]{1,0:T(8,128)(2,1)} async-done(((bf16[64,3072]{1,0:T(8,128)(2,1)}), bf16[2048,3072]{1,0:T(8,128)(2,1)}) %all-gather.20.cloned.1.call-update) | async-done | bytes 12582928 | tf_op jit(solution)/shard_map/all_gather | solution.py:115
  313.1 16.9 copy.109
  336.9 80.5 %all-gather.22.cloned.1.call-done = bf16[2048,3072]{0,1:T(8,128)(2,1)} async-done(((bf16[128,3072]{0,1:T(8,128)(2,1)}), bf16[2048,3072]{0,1:T(8,128)(2,1)}) %all-gather.22.cloned.1.call-update) | async-done | bytes 12582928 | tf_op jit(solution)/shard_map/all_gather | solution.py:172
  417.4 14.6 fusion.11
  440.6 14.3 fusion.126
  454.9 41.4 all-gather.24.cloned.1.call-done
  512.7 137.6 %scatter_fusion.1 = bf16[16,64,2048]{2,1,0:T(8,128)(2,1)} fusion(bf16[16,64,2048]{2,1,0:T(8,128)(2,1)} %broadcast.453.clone, s32[768]{0:T(1024)S(1)} %get-tuple-element.586, bf16[768,2048]{1,0:T(8,128)(2,1)} %multiply_convert_fusion), kind=kCustom, calls=%fused_computation.4 | custom fusion | bytes 9443328 | tf_op jit(solution)/shard_map/scatter | solution.py:246
  661.7 137.9 %scatter_fusion = bf16[16,64,2048]{2,1,0:T(8,128)(2,1)} fusion(bf16[16,64,2048]{2,1,0:T(8,128)(2,1)} %broadcast.453.clone.1, s32[768]{0:T(1024)S(1)} %get-tuple-element.586, bf16[768,2048]{1,0:T(8,128)(2,1)} %gather_fusion), kind=kCustom, calls=%fused_computation.3 | custom fusion | bytes 9443328 | tf_op jit(solution)/shard_map/scatter | solution.py:218
  807.0 12.0 fusion.23
  819.0 82.4 %all-to-all-done = bf16[16,64,2048]{2,1,0:T(8,128)(2,1)} async-done(((bf16[16,64,2048]{2,1,0:T(8,128)(2,1)}), bf16[16,64,2048]{2,1,0:T(8,128)(2,1)}, u32[]{:S(2)}, u32[]{:S(2)}) %all-to-all-start) | async-done | bytes 4194336 | tf_op jit(solution)/shard_map/all_to_all | solution.py:220
  901.5 12.0 fusion.29
  913.5 16.4 fusion.22
  941.8 35.2 all-to-all-start.1
  977.3 100.6 %all-to-all-done.1 = bf16[16,64,2048]{2,1,0:T(8,128)(2,1)} async-done(((bf16[16,64,2048]{2,1,0:T(8,128)(2,1)}), bf16[16,64,2048]{2,1,0:T(8,128)(2,1)}, u32[]{:S(2)}, u32[]{:S(2)}) %all-to-all-start.1) | async-done | bytes 4194336 | tf_op jit(solution)/shard_map/all_to_all | solution.py:226
  1077.9 14.8 gather_fusion.1
  1151.4 46.6 %all-to-all-start.3 = ((bf16[16,64,2048]{2,1,0:T(8,128)(2,1)}), bf16[16,64,2048]{2,1,0:T(8,128)(2,1)}, u32[]{:S(2)}, u32[]{:S(2)}) async-start(bf16[16,64,2048]{2,1,0:T(8,128)(2,1)} %bitcast.295), calls=%async_computation.3 | async-start | bytes 8388608 | tf_op jit(solution)/shard_map/all_to_all | solution.py:260
  1242.7 34.0 all-to-all-done.3
  1276.7 14.7 gather_fusion.2
  1318.9 575.0 %while.24 = (s32[]{:T(128)}, bf16[128,3072]{0,1:T(8,128)(2,1)}, bf16[128,2048]{1,0:T(8,128)(2,1)S(1)}, f32[128,16,192]{0,2,1:T(8,128)}, f32[128,16,128]{2,0,1:T(...) while((s32[]{:T(128)}, bf16[128,3072]{0,1:T(8,128)(2,1)}, ...), condition=%wide.region_24.25_spmd.clone, body=%wide.region_23.24_spmd.clone.sunk | while | flops 442286080 | bytes 47239776 | solution.py:329
  1347.6 17.1 collective-permute-done.3
  1382.2 17.4 collective-permute-done.3
  1416.1 18.4 collective-permute-done.3
  1450.9 18.5 collective-permute-done.3
  1485.8 18.5 collective-permute-done.3
  1520.8 18.5 collective-permute-done.3
  1555.7 18.5 collective-permute-done.3
  1590.6 18.5 collective-permute-done.3
  1625.5 18.4 collective-permute-done.3
  1660.4 18.5 collective-permute-done.3
  1695.3 18.5 collective-permute-done.3
  1730.2 18.5 collective-permute-done.3
  1765.1 18.5 collective-permute-done.3
  1800.0 18.5 collective-permute-done.3
  1835.0 18.5 collective-permute-done.3
  1869.9 18.5 collective-permute-done.3
  1942.2 23.4 copy.130
  1998.6 38.4 all-reduce.10
  2066.2 162.8 %reduce-scatter.20.cloned.1.call-done = f32[16,4096]{1,0:T(8,128)} async-done(((f32[512,4096]{1,0:T(8,128)}), f32[16,4096]{1,0:T(8,128)}) %reduce-scatter.20.cloned.1.call-update) | async-done | bytes 262160 | tf_op jit(solution)/shard_map/reduce_scatter | solution.py:358
  2229.0 491.9 %reduce-scatter.24.cloned.1.call-done = f32[64,2816]{1,0:T(8,128)} async-done(((f32[2048,2816]{1,0:T(8,128)}), f32[64,2816]{1,0:T(8,128)}) %reduce-scatter.24.cloned.1.call-update) | async-done | bytes 720912 | tf_op jit(solution)/shard_map/reduce_scatter | solution.py:362
  2720.9 492.6 %reduce-scatter.26.cloned.1.call-done = f32[64,2816]{1,0:T(8,128)} async-done(((f32[2048,2816]{1,0:T(8,128)}), f32[64,2816]{1,0:T(8,128)}) %reduce-scatter.26.cloned.1.call-update) | async-done | bytes 720912 | tf_op jit(solution)/shard_map/reduce_scatter | solution.py:363
  3213.5 492.7 %reduce-scatter.36.cloned.1.call-done = f32[64,2816]{1,0:T(8,128)} async-done(((f32[2048,2816]{1,0:T(8,128)}), f32[64,2816]{1,0:T(8,128)}) %reduce-scatter.36.cloned.1.call-update) | async-done | bytes 720912
  3706.3 362.0 %reduce-scatter.22.cloned.1.call-done = f32[64,2048]{1,0:T(8,128)} async-done(((f32[2048,2048]{1,0:T(8,128)}), f32[64,2048]{1,0:T(8,128)}) %reduce-scatter.22.cloned.1.call-update) | async-done | bytes 524304 | tf_op jit(solution)/shard_map/reduce_scatter | solution.py:359
  4068.3 253.7 %reduce-scatter.16.cloned.1.call-done = f32[64,3072]{1,0:T(8,128)} async-done(((f32[2048,3072]{1,0:T(8,128)}), f32[64,3072]{1,0:T(8,128)}) %reduce-scatter.16.cloned.1.call-update) | async-done | bytes 786448 | tf_op jit(solution)/shard_map/reduce_scatter | solution.py:356
  (779 shorter events, 636.8 us)
Async XLA Ops:
  7.2 65.1 %all-gather.14.cloned.1.call-start = ((), (), s32[]{:S(2)}) async-start(), calls=%async_computation.15 | async-start | bytes 2703360 | tf_op jit(solution)/shard_map/all_gather | solution.py:116
  8.8 128.1 %all-gather.16.cloned.1.call-start = ((), (), s32[]{:S(2)}) async-start(), calls=%async_computation.16 | async-start | bytes 4325376 | tf_op jit(solution)/shard_map/all_gather | solution.py:117
  10.5 237.0 %all-gather.18.cloned.1.call-start = ((), (), s32[]{:S(2)}) async-start(), calls=%async_computation.17 | async-start | bytes 8912896 | tf_op jit(solution)/shard_map/all_gather | solution.py:173
  141.4 171.8 %all-gather.20.cloned.1.call-start = ((), (), s32[]{:S(2)}) async-start(), calls=%async_computation.18 | async-start | bytes 12976128 | tf_op jit(solution)/shard_map/all_gather | solution.py:115
  142.2 275.1 %all-gather.22.cloned.1.call-start = ((), (), s32[]{:S(2)}) async-start(), calls=%async_computation.19 | async-start | bytes 13369344 | tf_op jit(solution)/shard_map/all_gather | solution.py:172
  145.7 350.6 %all-gather.24.cloned.1.call-start = ((), (), s32[]{:S(2)}) async-start(), calls=%async_computation.20 | async-start | bytes 8650752 | tf_op jit(solution)/shard_map/all_gather | solution.py:118
  146.5 660.5 %all-gather.30.cloned.1.call-start = ((), (), s32[]{:S(2)}) async-start(), calls=%async_computation.23 | async-start | bytes 8650752 | tf_op jit(solution)/shard_map/all_gather | solution.py:128
  151.4 667.6 %all-gather.28.cloned.1.call-start = ((), (), s32[]{:S(2)}) async-start(), calls=%async_computation.22 | async-start | bytes 8650752 | tf_op jit(solution)/shard_map/all_gather | solution.py:127
  156.1 757.4 %all-gather.26.cloned.1.call-start = ((), (), s32[]{:S(2)}) async-start(), calls=%async_computation.21 | async-start | bytes 8650752 | tf_op jit(solution)/shard_map/all_gather | solution.py:126
  160.7 1038.9 %all-gather.32.cloned.1.call-start = ((), (), s32[]{:S(2)}) async-start(), calls=%async_computation.24 | async-start | bytes 11894784 | tf_op jit(solution)/shard_map/all_gather | solution.py:121
  161.6 1045.1 %all-gather.34.cloned.1.call-start = ((), (), s32[]{:S(2)}) async-start(), calls=%async_computation.25 | async-start | bytes 11894784 | tf_op jit(solution)/shard_map/all_gather | solution.py:122
  650.3 149.3 %all-to-all-start.2 = ((bf16[16,64,2048]{2,1,0:T(8,128)(2,1)}), bf16[16,64,2048]{2,1,0:T(8,128)(2,1)}, u32[]{:S(2)}, u32[]{:S(2)}) async-start(bf16[16,64,2048]{2,1,0:T(8,128)(2,1)} %scatter_fusion.1), calls=%async_computation.2 | async-start | bytes 8388608 | tf_op jit(solution)/shard_map/all_to_all | solution.py:247
  799.6 101.9 %all-to-all-start = ((bf16[16,64,2048]{2,1,0:T(8,128)(2,1)}), bf16[16,64,2048]{2,1,0:T(8,128)(2,1)}, u32[]{:S(2)}, u32[]{:S(2)}) async-start(bf16[16,64,2048]{2,1,0:T(8,128)(2,1)} %scatter_fusion), calls=%async_computation | async-start | bytes 8388608 | tf_op jit(solution)/shard_map/all_to_all | solution.py:220
  805.7 408.1 %all-gather.36.cloned.1.call-start = ((), (), s32[]{:S(2)}) async-start(), calls=%async_computation.26 | async-start | bytes 11894784 | tf_op jit(solution)/shard_map/all_gather | solution.py:123
  941.8 136.1 %all-to-all-start.1 = ((bf16[16,64,2048]{2,1,0:T(8,128)(2,1)}), bf16[16,64,2048]{2,1,0:T(8,128)(2,1)}, u32[]{:S(2)}, u32[]{:S(2)}) async-start(bf16[16,64,2048]{2,1,0:T(8,128)(2,1)} %bitcast.296), calls=%async_computation.1 | async-start | bytes 8388608 | tf_op jit(solution)/shard_map/all_to_all | solution.py:226
  977.1 1073.5 %reduce-scatter.34.cloned.1.call-start = ((), (), s32[]{:S(2)}) async-start(), calls=%async_computation.36 | async-start | bytes 1081344
  1108.3 943.7 %reduce-scatter.32.cloned.1.call-start = ((), (), s32[]{:S(2)}) async-start(), calls=%async_computation.35 | async-start | bytes 8650752 | tf_op jit(solution)/shard_map/reduce_scatter | solution.py:276
  1119.3 937.4 %reduce-scatter.28.cloned.1.call-start = ((), (), s32[]{:S(2)}) async-start(), calls=%async_computation.33 | async-start | bytes 8650752 | tf_op jit(solution)/shard_map/reduce_scatter | solution.py:267
  1151.4 125.3 %all-to-all-start.3 = ((bf16[16,64,2048]{2,1,0:T(8,128)(2,1)}), bf16[16,64,2048]{2,1,0:T(8,128)(2,1)}, u32[]{:S(2)}, u32[]{:S(2)}) async-start(bf16[16,64,2048]{2,1,0:T(8,128)(2,1)} %bitcast.295), calls=%async_computation.3 | async-start | bytes 8388608 | tf_op jit(solution)/shard_map/all_to_all | solution.py:260
  1198.1 863.4 %reduce-scatter.30.cloned.1.call-start = ((), (), s32[]{:S(2)}) async-start(), calls=%async_computation.34 | async-start | bytes 8650752 | tf_op jit(solution)/shard_map/reduce_scatter | solution.py:270
  1242.5 823.7 %reduce-scatter.18.cloned.1.call-start = ((), (), s32[]{:S(2)}) async-start(), calls=%async_computation.28 | async-start | bytes 5406720 | tf_op jit(solution)/shard_map/reduce_scatter | solution.py:357
  1320.2 49.9 %collective-permute-start = (bf16[128,3072]{0,1:T(8,128)(2,1)S(1)}, bf16[128,3072]{0,1:T(8,128)(2,1)}, u32[]{:S(2)}, u32[]{:S(2)}) collective-permute-start(bf16[128,3072]{0,1:T(8,128)(2,1)S(1)} %copy.160), channel_id=1, source_target_pairs={{0,2},{2,4},{4,6},{6,8},{8,10},{10,12},{12,14},{14,16},{16,18},{18... | collective-permute-start | bytes 2359304 | tf_op jit(solution)/shard_map/while/body/eval_jaxpr/ppermute | solution.py:21
  1326.2 40.6 collective-permute-start.2
  1334.5 30.2 collective-permute-start.3
  1335.3 34.8 collective-permute-start.1
  1371.3 33.8 collective-permute-start
  1406.2 33.8 collective-permute-start
  1441.1 33.8 collective-permute-start
  1476.0 33.8 collective-permute-start
  1510.9 33.8 collective-permute-start
  1545.9 33.8 collective-permute-start
  1580.8 33.8 collective-permute-start
  1615.7 33.8 collective-permute-start
  1650.6 33.8 collective-permute-start
  1657.3 27.1 collective-permute-start.1
  1685.5 33.8 collective-permute-start
  1720.4 33.8 collective-permute-start
  1755.3 33.8 collective-permute-start
  1790.3 33.8 collective-permute-start
  1825.2 33.8 collective-permute-start
  1860.1 33.8 collective-permute-start
  1866.8 27.1 collective-permute-start.1
  1905.2 323.8 %reduce-scatter.20.cloned.1.call-start = ((), (), s32[]{:S(2)}) async-start(), calls=%async_computation.29 | async-start | bytes 8650752 | tf_op jit(solution)/shard_map/reduce_scatter | solution.py:358
  1909.9 811.0 %reduce-scatter.24.cloned.1.call-start = ((), (), s32[]{:S(2)}) async-start(), calls=%async_computation.31 | async-start | bytes 23789568 | tf_op jit(solution)/shard_map/reduce_scatter | solution.py:362
  1920.5 1293.0 %reduce-scatter.26.cloned.1.call-start = ((), (), s32[]{:S(2)}) async-start(), calls=%async_computation.32 | async-start | bytes 23789568 | tf_op jit(solution)/shard_map/reduce_scatter | solution.py:363
  1931.1 1775.2 %reduce-scatter.36.cloned.1.call-start = ((), (), s32[]{:S(2)}) async-start(), calls=%async_computation.37 | async-start | bytes 23789568
  1965.6 2102.7 %reduce-scatter.22.cloned.1.call-start = ((), (), s32[]{:S(2)}) async-start(), calls=%async_computation.30 | async-start | bytes 17301504 | tf_op jit(solution)/shard_map/reduce_scatter | solution.py:359
  1975.2 2346.8 %reduce-scatter.16.cloned.1.call-start = ((), (), s32[]{:S(2)}) async-start(), calls=%async_computation.27 | async-start | bytes 25952256 | tf_op jit(solution)/shard_map/reduce_scatter | solution.py:356
  (174 other events, 5833.9 us)
Sparse Core Ops, SparseCore 0:
  11.5 60.7 all-gather.13
  75.8 60.9 all-gather.15
  141.5 73.9 all-gather.17
  218.8 94.2 all-gather.19
  315.1 102.1 all-gather.21
  420.8 75.4 all-gather.23
  497.8 73.0 all-gather.29
  572.4 74.4 all-gather.27
  648.5 74.4 all-gather.25
  726.3 124.8 all-gather.31
  854.5 118.4 all-gather.33
  975.7 151.7 all-gather.35
  1129.7 161.3 reduce-scatter.33
  1293.9 77.5 reduce-scatter.31
  1374.2 71.3 reduce-scatter.27
  1447.9 71.3 reduce-scatter.29
  1905.3 140.0 reduce-scatter.17
  2048.1 180.8 reduce-scatter.19
  2231.9 489.0 reduce-scatter.23
  2723.6 489.8 reduce-scatter.25
  3216.4 489.8 reduce-scatter.35
  3709.1 359.1 reduce-scatter.21
  4075.3 246.6 reduce-scatter.15
where the time goes:
time: 4350 us; the launch traced here: 4330 us
  waiting for transfers between devices  3030 us (70%)
  local copies, waits for them, and re-layouts  458 us (11%)
  matrix products  404 us (9%)
  other arithmetic  153 us (4%)
  blocking collectives  149 us (3%)
  starting transfers between devices  115 us (3%)
    unnamed x25, waiting for transfers between devices  493 us
    reduce_scatter x1, waiting for transfers between devices, local(): lax.psum_scatter(grad_sup, ('ctx', 'fsdp'), scatter_dimension=0, tiled=True)  493 us
    reduce_scatter x1, waiting for transfers between devices, local(): lax.psum_scatter(grad_sgate, ('ctx', 'fsdp'), scatter_dimension=0, tiled=...  492 us
    reduce_scatter x1, waiting for transfers between devices, local(): lax.psum_scatter(grad_output_w, ('ctx', 'fsdp'), scatter_dimension=0, til...  362 us
    ppermute x64, waiting for transfers between devices, shifted(): lax.ppermute(shard, axis, [(i, (i + by) % devices) for i in range(devices)])  308 us
    scatter x2, local copies, waits for them, and re-layouts, local(): jnp.zeros((experts, capacity, D), jnp.bfloat16).at[flat, slot]  276 us
    reduce_scatter x1, waiting for transfers between devices, local(): lax.psum_scatter(grad_query_w, ('ctx', 'fsdp'), scatter_dimension=0, tile...  254 us
    reduce_scatter x1, waiting for transfers between devices, local(): lax.psum_scatter(grad_expand_w, ('ctx', 'fsdp'), scatter_dimension=0, til...  163 us
  transfers between devices with their start and end apart: 91, of which 46 were waited for; matrix products, arithmetic and copies ran while one was open for 23% of the time, Pallas kernels for 0%

commit v1 on v0

--- a/solution.py
+++ b/solution.py
@@ -1,6 +1,10 @@
+import functools
+
 import jax
 import jax.numpy as jnp
 from jax import lax
+from jax.experimental import pallas as pl
+from jax.experimental.pallas import tpu as pltpu
 from jax.sharding import PartitionSpec as P
 
 D = 2048
@@ -10,31 +14,908 @@
 VDIM = 128
 LATENT = 512
 TOP = 6
-
-
 EPS = 1e-06
 NEGATIVE = -1e30
+BF = jnp.bfloat16
+F32 = jnp.float32
+
+
+def matmul(left, right):
+    return jnp.dot(left, right, preferred_element_type=F32)
+
+
+def contract_last(left, right):
+    return lax.dot_general(left, right, (((1,), (1,)), ((), ())), preferred_element_type=F32)
+
+
+def leading_contraction(left, right):
+    return lax.dot_general(left, right, (((0,), (0,)), ((), ())), preferred_element_type=F32)
+
+
+def norm_scale(value):
+    return lax.rsqrt(jnp.mean(value * value, -1, keepdims=True) + EPS)
+
+
+def norm_back(value, scale, gain, grad):
+    lifted = grad * gain
+    return scale * lifted - value * (scale**3 * jnp.mean(lifted * value, -1, keepdims=True))
+
+
+def turn(value, cosine, sine):
+    half = value.shape[-1] // 2
+    first, second = value[..., :half], value[..., half:]
+    return jnp.concatenate([first * cosine - second * sine, first * sine + second * cosine], -1)
+
+
+def swiglu_parts(gate, up):
+    sigmoid = 1.0 / (1.0 + jnp.exp(-gate))
+    act = gate * sigmoid
+    return act, sigmoid * (1.0 + gate * (1.0 - sigmoid))
+
+
+def box_of(count):
+    dims = [2, 2]
+    count //= 4
+    while count > 1:
+        side = 4 if count % 4 == 0 else 2
+        dims.insert(0, side)
+        count //= side
+    return dims
+
+
+class Box:
+    def __init__(self):
+        self.count = lax.axis_size("ctx")
+        self.dims = box_of(self.count)
+        self.strides = []
+        stride = self.count
+        for side in self.dims:
+            stride //= side
+            self.strides.append(stride)
+
+    def shift(self, value, dim, by):
+        side, stride = self.dims[dim], self.strides[dim]
+
+        def target(i):
+            here = i // stride % side
+            return i + ((here + by) % side - here) * stride
+
+        return lax.ppermute(value, "ctx", [(i, target(i)) for i in range(self.count)])
+
+    def owners(self):
+        me = lax.axis_index("ctx")
+        owner = jnp.zeros((1,), jnp.int32)
+        for side, stride in zip(self.dims, self.strides):
+            here = me // stride % side
+            offset = (here - jnp.arange(side, dtype=jnp.int32)) % side * stride
+            owner = (offset[:, None] + owner[None, :]).reshape(-1)
+        return owner
+
+    def gather_step(self, held, dim):
+        shifted = [self.shift(held, dim, k) for k in range(1, self.dims[dim])]
+        return jnp.concatenate([held] + shifted, 0)
+
+    def gather(self, held):
+        for dim in range(len(self.dims)):
+            held = self.gather_step(held, dim)
+        return held
+
+    def scatter_step(self, held, dim):
+        parts = jnp.split(held, self.dims[dim], 0)
+        total = parts[0].astype(F32)
+        for k in range(1, self.dims[dim]):
+            total = total + self.shift(parts[k], dim, -k).astype(F32)
+        return total if dim == 0 else total.astype(held.dtype)
+
+    def scatter(self, held):
+        for dim in reversed(range(len(self.dims))):
+            held = self.scatter_step(held, dim)
+        return held
+
+
+def after(event, *values):
+    return lax.optimization_barrier((event,) + values)[1:]
+
+
+def meet(*values):
+    return lax.optimization_barrier(values)
+
+
+MESH = pl.DeviceIdType.MESH
+DMA = pltpu.SemaphoreType.DMA
+
+
+def sides(count, both=False):
+    found, stride, held = [], count, 1
+    for side in box_of(count):
+        stride //= side
+        found.append(("ctx", side, stride, held))
+        held *= side
+    return found + ([("fsdp", 2, 1, held)] if both else [])
+
+
+def moved(me, side, stride, by):
+    here = me // stride % side
+    return me + ((here + by) % side - here) * stride
+
+
+def offset_of(count, me, owner):
+    total = 0
+    for _, side, stride, held in sides(count):
+        total = total + (me // stride % side + side - owner // stride % side) % side * held
+    return total
+
+
+def remote(src, dst, send, recv, axis, target):
+    return pltpu.make_async_remote_copy(
+        src_ref=src,
+        dst_ref=dst,
+        send_sem=send,
+        recv_sem=recv,
+        device_id={axis: target},
+        device_id_type=MESH,
+    )
+
+
+class Gather:
+    def __init__(self, count, value, chunks):
+        self.count, self.chunks = count, chunks
+        self.out = jax.ShapeDtypeStruct((count,) + value.shape, value.dtype)
+        self.scratch = [DMA, DMA((count, chunks)), DMA((count, chunks))]
+        self.space, self.out_space = pl.ANY, pl.ANY
+        self.reach = "box"
+
+    def bind(self, me, half, x_ref, out_ref, own_sem, send_sem, recv_sem):
+        self.me, self.x, self.o = me, x_ref, out_ref
+        self.sems = (send_sem, recv_sem)
+        self.own = pltpu.make_async_copy(x_ref, out_ref.at[0], own_sem)
+        self.sent = []
+        self.dims = sides(self.count)
+
+    def copy(self, block, chunk, dim, by):
+        _, side, stride, held = self.dims[dim]
+        step = self.x.shape[0] // self.chunks
+        part = pl.ds(chunk * step, step)
+        src = self.x.at[part] if block == 0 else self.o.at[block, part]
+        to = by * held + block
+        return remote(
+            src,
+            self.o.at[to, part],
+            self.sems[0].at[to, chunk],
+            self.sems[1].at[to, chunk],
+            "ctx",
+            moved(self.me, side, stride, by),
+        )
+
+    def forward(self, block, chunk, first):
+        for dim in range(first, len(self.dims)):
+            for by in range(1, self.dims[dim][1]):
+                copy = self.copy(block, chunk, dim, by)
+                copy.start()
+                self.sent.append(copy)
+
+    def start(self):
+        self.own.start()
+        for chunk in range(self.chunks):
+            self.forward(0, chunk, 0)
+
+    def arrive(self, chunk, dim):
+        _, side, _, held = self.dims[dim]
+        for by in range(1, side):
+            for block in range(held):
+                self.copy(block, chunk, dim, by).wait_recv()
+                self.forward(by * held + block, chunk, dim + 1)
+
+    def steps(self):
+        found, last = [], len(self.dims)
+        for wave in range(self.chunks + last - 1):
+            for dim in range(last):
+                if 0 <= wave - dim < self.chunks:
+                    found.append(functools.partial(self.arrive, wave - dim, dim))
+        return found
+
+    def finish(self):
+        for copy in self.sent:
+            copy.wait_send()
+        self.own.wait()
+
+
+class GatherAll:
+    def __init__(self, count, value):
+        self.count = count
+        self.out = jax.ShapeDtypeStruct((count, 2) + value.shape, value.dtype)
+        self.scratch = [DMA, DMA((count, 2)), DMA((count, 2))]
+        self.space, self.out_space = pl.ANY, pl.ANY
+        self.reach = "box+half"
+
+    def bind(self, me, half, x_ref, out_ref, own_sem, send_sem, recv_sem):
+        self.me, self.half, self.x, self.o = me, half, x_ref, out_ref
+        self.sems = (send_sem, recv_sem)
+        self.own = pltpu.make_async_copy(x_ref, out_ref.at[me, half], own_sem)
+        self.sent = []
+        self.dims = sides(self.count)
+
+    def owner(self, block):
+        owner = self.me
+        for _, side, stride, held in self.dims:
+            owner = moved(owner, side, stride, -(block // held % side))
+        return owner
+
+    def copy(self, block, other, dim, by):
+        _, side, stride, held = self.dims[dim]
+        owner = self.owner(block)
+        half = 1 - self.half if other else self.half
+        src = self.x if block == 0 and not other else self.o.at[owner, half]
+        to = by * held + block
+        return remote(
+            src,
+            self.o.at[owner, half],
+            self.sems[0].at[to, other],
+            self.sems[1].at[to, other],
+            "ctx",
+            moved(self.me, side, stride, by),
+        )
+
+    def arrived(self, block, other, dim, by):
+        _, side, stride, held = self.dims[dim]
+        to = by * held + block
+        half = 1 - self.half if other else self.half
+        here = self.o.at[self.owner(to), half]
+        return remote(
+            here, here, self.sems[0].at[to, other], self.sems[1].at[to, other], "ctx",
+            moved(self.me, side, stride, by),
+        )
+
+    def across(self, half):
+        return remote(
+            self.x, self.o.at[self.me, half], self.sems[0].at[0, 0], self.sems[1].at[0, 0],
+            "fsdp", 1 - self.half,
+        )
+
+    def forward(self, block, other, first):
+        for dim in range(first, len(self.dims)):
+            for by in range(1, self.dims[dim][1]):
+                copy = self.copy(block, other, dim, by)
+                copy.start()
+                self.sent.append(copy)
+
+    def start(self):
+        self.own.start()
+        self.cross = self.across(self.half)
+        self.cross.start()
+        self.forward(0, 0, 0)
+
+    def meet(self):
+        self.across(1 - self.half).wait_recv()
+        self.forward(0, 1, 0)
+
+    def arrive(self, dim):
+        _, side, _, held = self.dims[dim]
+        for other in range(2):
+            for by in range(1, side):
+                for block in range(held):
+                    self.arrived(block, other, dim, by).wait_recv()
+                    self.forward(by * held + block, other, dim + 1)
+
+    def steps(self):
+        return [self.meet] + [functools.partial(self.arrive, d) for d in range(len(self.dims))]
+
+    def finish(self):
+        for copy in self.sent:
+            copy.wait_send()
+        self.cross.wait_send()
+        self.own.wait()
+
+
+class Deal:
+    def __init__(self, count, value, both=False, pick=None, place=None):
+        self.count, self.both = count, both
+        self.pick = pick or (lambda me, to: to)
+        self.place = place or (lambda me, to: me)
+        shape = value.shape[:1] + ((2,) if both else ()) + value.shape[1:]
+        self.out = jax.ShapeDtypeStruct(shape, value.dtype)
+        self.scratch = [DMA, DMA((count, 2)), DMA((count, 2))]
+        self.space, self.out_space = pl.ANY, pl.ANY
+        self.reach = "all+half" if both else "all"
+
+    def bind(self, me, half, x_ref, out_ref, own_sem, send_sem, recv_sem):
+        self.me, self.half, self.x, self.o = me, half, x_ref, out_ref
+        self.send, self.recv = send_sem, recv_sem
+        self.sent = []
+        self.own = pltpu.make_async_copy(
+            x_ref.at[self.pick(me, me)], self.here(self.place(me, me), half), own_sem
+        )
+
+    def here(self, slot, half):
+        return self.o.at[slot, half] if self.both else self.o.at[slot]
+
+    def copy(self, by):
+        to = (self.me + by) % self.count
+        return remote(
+            self.x.at[self.pick(self.me, to)],
+            self.here(self.place(self.me, to), self.half),
+            self.send.at[by, 0],
+            self.recv.at[by, 0],
+            "ctx",
+            to,
+        )
+
+    def arrived(self, by):
+        source = (self.me + self.count - by) % self.count
+        slot = self.here(self.place(source, self.me), self.half)
+        return remote(
+            slot, slot, self.send.at[by, 0], self.recv.at[by, 0], "ctx", (self.me + by) % self.count
+        )
+
+    def across(self, by, half):
+        source = (self.me + self.count - by) % self.count
+        slot = self.here(self.place(source, self.me), half)
+        src = self.x.at[self.pick(self.me, self.me)] if by == 0 else slot
+        return remote(
+            src, slot, self.send.at[by, 1], self.recv.at[by, 1], "fsdp", 1 - self.half
+        )
+
+    def start(self):
+        self.own.start()
+        for by in range(1, self.count):
+            copy = self.copy(by)
+            copy.start()
+            self.sent.append(copy)
+        if self.both:
+            self.pass_on(0)
+
+    def pass_on(self, by):
+        copy = self.across(by, self.half)
+        copy.start()
+        self.sent.append(copy)
+
+    def arrive(self, by):
+        self.arrived(by).wait_recv()
+        if self.both:
+            self.pass_on(by)
+
+    def rest(self):
+        for by in range(self.count):
+            self.across(by, 1 - self.half).wait_recv()
+
+    def steps(self):
+        return [functools.partial(self.arrive, by) for by in range(1, self.count)]
+
+    def finish(self):
+        if self.both:
+            self.rest()
+        for copy in self.sent:
+            copy.wait_send()
+        self.own.wait()
+
+
+class Scatter:
+    def __init__(self, count, value, chunks, both=False):
+        self.count, self.chunks, self.both = count, chunks, both
+        tail = value.shape[1:]
+        self.out = jax.ShapeDtypeStruct(tail, F32)
+        dims = sides(count, both)
+        blocks = value.shape[0]
+        self.scratch = [
+            pltpu.VMEM(((side - 1) * held,) + tail, value.dtype) for _, side, _, held in dims
+        ]
+        self.scratch += [pltpu.VMEM((held,) + tail, value.dtype) for _, _, _, held in dims[1:]]
+        self.scratch += [DMA((blocks, chunks)), DMA((blocks, chunks))]
+        self.space, self.out_space = pltpu.VMEM, pltpu.VMEM
+        self.reach = "box+half" if both else "box"
+
+    def bind(self, me, half, x_ref, out_ref, *scratch):
+        self.me, self.half, self.o = me, half, out_ref
+        self.blocks = x_ref.shape[0]
+        self.dims = sides(self.count, self.both)
+        levels = len(self.dims)
+        self.landed = scratch[:levels]
+        self.held = scratch[levels : 2 * levels - 1] + (x_ref,)
+        self.send, self.recv = scratch[2 * levels - 1 :]
+        self.sent = []
+
+    def part(self, chunk):
+        step = self.o.shape[0] // self.chunks
+        return pl.ds(chunk * step, step)
+
+    def copy(self, dim, block, chunk):
+        axis, side, stride, held = self.dims[dim]
+        part = self.part(chunk)
+        here = self.me if axis == "ctx" else self.half
+        return remote(
+            self.held[dim].at[block, part],
+            self.landed[dim].at[block - held, part],
+            self.send.at[block, chunk],
+            self.recv.at[block, chunk],
+            axis,
+            moved(here, side, stride, -(block // held)),
+        )
+
+    def ready(self, dim, block, chunk):
+        if block >= self.dims[dim][3]:
+            copy = self.copy(dim, block, chunk)
+            copy.start()
+            self.sent.append(copy)
+
+    def add(self, dim, chunk):
+        _, side, _, held = self.dims[dim]
+        part = self.part(chunk)
+        for block in reversed(range(held)):
+            total = self.held[dim][block, part].astype(F32)
+            for by in range(1, side):
+                self.copy(dim, by * held + block, chunk).wait_recv()
+                total = total + self.landed[dim][(by - 1) * held + block, part].astype(F32)
+            if dim == 0:
+                self.o[part] = total
+            else:
+                self.held[dim - 1][block, part] = total.astype(self.held[dim - 1].dtype)
+                self.ready(dim - 1, block, chunk)
+
+    def start(self):
+        last = len(self.dims) - 1
+        for chunk in range(self.chunks):
+            for block in reversed(range(self.dims[last][3], self.blocks)):
+                self.ready(last, block, chunk)
+
+    def steps(self):
+        found, levels = [], len(self.dims)
+        for wave in range(self.chunks + levels - 1):
+            for dim in reversed(range(levels)):
+                chunk = wave - (levels - 1 - dim)
+                if 0 <= chunk < self.chunks:
+                    found.append(functools.partial(self.add, dim, chunk))
+        return found
+
+    def finish(self):
+        for copy in self.sent:
+            copy.wait_send()
+
+
+def exchange_kernel(count, plans, early, *refs):
+    me, half = lax.axis_index("ctx"), lax.axis_index("fsdp")
+    ins, refs = refs[: len(plans)], refs[len(plans) :]
+    outs, refs = refs[: len(plans)], refs[len(plans) :]
+    barrier = pltpu.get_barrier_semaphore()
+    peers = []
+    if any("all" in plan.reach for plan in plans):
+        peers = [("ctx", (me + by) % count) for by in range(1, count)]
+    else:
+        for _, side, stride, _ in sides(count):
+            peers += [("ctx", moved(me, side, stride, by)) for by in range(1, side)]
+    if any("half" in plan.reach for plan in plans):
+        peers.append(("fsdp", 1 - half))
+    for axis, target in peers:
+        pl.semaphore_signal(barrier, inc=1, device_id={axis: target}, device_id_type=MESH)
+    pl.semaphore_wait(barrier, len(peers))
+    for plan, x_ref, out_ref in zip(plans, ins, outs):
+        mine, refs = refs[: len(plan.scratch)], refs[len(plan.scratch) :]
+        plan.bind(me, half, x_ref, out_ref, *mine)
+        plan.start()
+    for plan in plans[:early]:
+        for step in plan.steps():
+            step()
+    queues = [plan.steps() for plan in plans[early:]]
+    longest = max(len(queue) for queue in queues)
+    done = [0] * len(queues)
+    for turn in range(longest):
+        for i, queue in enumerate(queues):
+            upto = (turn + 1) * len(queue) // longest
+            for step in queue[done[i] : upto]:
+                step()
+            done[i] = upto
+    for plan in plans:
+        plan.finish()
+
+
+def exchange(count, collective, values, plans, early=0):
+    scratch = [ref for plan in plans for ref in plan.scratch]
+    return pl.pallas_call(
+        functools.partial(exchange_kernel, count, plans, early),
+        out_shape=tuple(plan.out for plan in plans),
+        in_specs=[pl.BlockSpec(memory_space=plan.space) for plan in plans],
+        out_specs=tuple(pl.BlockSpec(memory_space=plan.out_space) for plan in plans),
+        scratch_shapes=scratch,
+        compiler_params=pltpu.CompilerParams(
+            collective_id=collective, has_side_effects=True, vmem_limit_bytes=56 << 20
+        ),
+        cost_estimate=pl.CostEstimate(flops=0, bytes_accessed=100 << 20, transcendentals=0),
+    )(*values)
+
+
+def placement(lengths_row, order_row):
+    ends = jnp.cumsum(lengths_row)
+    starts = ends - lengths_row
+    sequence = jnp.sum((order_row[:, None] >= ends[None, :]).astype(jnp.int32), 1)
+    chosen = sequence[:, None] == jnp.arange(lengths_row.shape[0], dtype=jnp.int32)[None, :]
+    offset = jnp.sum(jnp.where(chosen, starts[None, :], 0), 1)
+    return (sequence, order_row - offset)
+
+
+def spread(weight, count, repeat):
+    rows = weight.shape[0]
+    parts = jnp.transpose(weight.astype(BF).reshape(rows, count // repeat, -1), (1, 0, 2))
+    return jnp.repeat(parts, repeat, 0) if repeat > 1 else parts
+
+
+def pad_last(value, width):
+    return jnp.pad(value, [(0, 0)] * (value.ndim - 1) + [(0, width - value.shape[-1])])
+
+
+def up_to(width, unit=128):
+    return -(-width // unit) * unit
+
+
+def local(
+    tokens,
+    cotangent,
+    lengths,
+    token_order,
+    routes,
+    first_gain,
+    latent_gain,
+    query_weight,
+    compress_weight,
+    expand_weight,
+    output_weight,
+    second_gain,
+    router_weight,
+    shared_gate,
+    shared_up,
+    shared_down,
+    expert_gate,
+    expert_up,
+    expert_down,
+):
+    box = Box()
+    count = box.count
+    repeat = max(1, count // HEADS)
+    rows = tokens.shape[1]
+    group = rows * count
+    asked = group // repeat
+    experts = router_weight.shape[1]
+    shard = query_weight.shape[0]
+    width = NOPE + ROPE
+    me = lax.axis_index("ctx")
+    both = ("ctx", "fsdp")
+    all_devices = count * lax.axis_size("fsdp")
+
+    half = lax.axis_index("fsdp")
+    small_vmem = count * rows * D * 2 <= 12 << 20
+
+    def reduce_blocks(collective, value, *more):
+        if small_vmem:
+            plans = [plan for _, plan in more] + [Scatter(count, value, 4)]
+            got = exchange(count, collective, [v for v, _ in more] + [value], plans)
+            return (got[-1],) + tuple(got[:-1])
+        rest = exchange(count, collective, [v for v, _ in more], [p for _, p in more]) if more else ()
+        return (box.scatter(value)[0],) + tuple(rest)
+
+    def across(value):
+        return lax.ppermute(value, "fsdp", [(0, 1), (1, 0)])
+
+    def both_halves(value):
+        other = across(value)
+        first, second = jnp.where(half == 0, value, other), jnp.where(half == 0, other, value)
+        return jnp.stack([first, second], 1)
+
+    def halves_sent(parts):
+        own = lax.dynamic_index_in_dim(parts, half, 1, keepdims=False)
+        other = lax.dynamic_index_in_dim(parts, 1 - half, 1, keepdims=False)
+        return own, across(other.astype(BF))
+
+    def halves_summed(parts):
+        own, got = halves_sent(parts)
+        return own.astype(F32) + got.astype(F32)
+
+    owners = box.owners()
+
+    small_cols = compress_weight.shape[1] + experts + 3
+    lat_rows = latent_gain.shape[0]
+    small = jnp.concatenate(
+        [
+            compress_weight,
+            router_weight,
+            first_gain[:, None],
+            second_gain[:, None],
+            jnp.pad(latent_gain, (0, shard - lat_rows))[:, None],
+        ],
+        1,
+    ).astype(BF)
+    small = pad_last(small, up_to(small_cols))
+    query_parts = spread(query_weight, count, repeat)
+    expand_parts = spread(expand_weight, count, repeat)
+    small_all = lax.all_gather(small, both, axis=0, tiled=True)
+    gate_expert = lax.all_gather(expert_gate[0].astype(BF), "fsdp", axis=0, tiled=True)
+    query_own, expand_own, token_all = exchange(
+        count,
+        0,
+        [query_parts, expand_parts, tokens[0]],
+        [
+            Deal(count, query_parts, both=True),
+            Deal(count, expand_parts, both=True),
+            Gather(count, tokens[0], 4),
+        ],
+        early=2,
+    )
+    token_all = token_all.reshape(group, D)
+    query_own = query_own.reshape(D, -1)
+    expand_own = expand_own.reshape(LATENT, -1)
+    edge = compress_weight.shape[1]
+    compress_full = small_all[:, :edge]
+    router_full = small_all[:, edge : edge + experts]
+    gain_first = small_all[:, edge + experts].astype(F32)
+    gain_second = small_all[:, edge + experts + 1].astype(F32)
+    gain_latent = small_all[:, edge + experts + 2].reshape(all_devices, shard)[:, :lat_rows]
+    gain_latent = gain_latent.reshape(-1).astype(F32)
+
+    output_cast, up_cast, down_cast = after(
+        token_all, output_weight, expert_up[0], expert_down[0]
+    )
+    output_full = lax.all_gather(output_cast.astype(BF), both, axis=0, tiled=True)
+    up_expert = lax.all_gather(up_cast.astype(BF), "fsdp", axis=0, tiled=True)
+    down_expert = lax.all_gather(down_cast.astype(BF), "fsdp", axis=0, tiled=True)
+
+    cot_low, route_own, gate_cols, up_cols, down_cols = after(
+        token_all, cotangent[0].astype(BF), routes[0], shared_gate, shared_up, shared_down
+    )
+    fs = shared_gate.shape[1] // count
+    fp = up_to(fs)
+    rest = jnp.concatenate(
+        [spread(gate_cols, count, 1), spread(up_cols, count, 1), spread(down_cols, count, 1)], -1
+    )
+    rest = pad_last(rest, up_to(3 * fs))
+    rest = lax.all_to_all(rest, "ctx", split_axis=0, concat_axis=0, tiled=True)
+    order_all = jnp.take(token_order[0].reshape(count, rows), owners, axis=0).reshape(-1)
+    sequence, position = placement(lengths[0], order_all)
+    turns = ROPE // 2
+    freq = 10000.0 ** (-jnp.arange(turns, dtype=F32) / turns)
+    angle = position.astype(F32)[:, None] * freq[None, :]
+    cosine, sine = jnp.cos(angle), jnp.sin(angle)
+
+    hidden_all = token_all.astype(F32)
+    normed_all = (hidden_all * norm_scale(hidden_all) * gain_first).astype(BF)
+    query_raw = matmul(normed_all[:asked], query_own)
+    query = jnp.concatenate(
+        [query_raw[:, :NOPE], turn(query_raw[:, NOPE:], cosine[:asked], sine[:asked])], -1
+    ).astype(BF)
+    compressed = matmul(normed_all, compress_full)
+    compressed, rest = meet(compressed, rest)
+    rest = both_halves(rest).reshape(D, -1)
+    rest_own = rest
+    sgate_own = pad_last(rest_own[:, :fs], fp)
+    sup_own = pad_last(rest_own[:, fs : 2 * fs], fp)
+    sdown_own = pad_last(rest_own[:, 2 * fs : 3 * fs], fp)
+    low_part = compressed[:, :LATENT]
+    latent_scale = norm_scale(low_part)
+    latent = (low_part * latent_scale * gain_latent).astype(BF)
+    expanded = matmul(latent, expand_own)
+    keys = jnp.concatenate(
+        [expanded[:, :NOPE], turn(compressed[:, LATENT:], cosine, sine)], -1
+    ).astype(BF)
+    values = expanded[:, NOPE:].astype(BF)
+    keys, gate_expert = meet(keys, gate_expert)
+    scale = width ** (-0.5)
+    visible = (sequence[:asked, None] == sequence[None, :]) & (
+        position[None, :] <= position[:asked, None]
+    )
+    scores = jnp.where(visible, contract_last(query, keys) * scale, NEGATIVE)
+    peak = jnp.max(scores, -1, keepdims=True)
+    weights = jnp.where(visible, jnp.exp(scores - peak), 0.0)
+    total = jnp.sum(weights, -1, keepdims=True)
+    mixed_f = matmul(weights.astype(BF), values) / total
+    logsum = peak + jnp.log(total)
+
+    def to_owner(value):
+        if repeat > 1:
+            value = jnp.pad(value, ((0, group - asked), (0, 0)))
+        value = value.reshape(count, rows, -1)
+        plan = Deal(count, value, pick=lambda me, to: offset_of(count, me, to))
+        (got,) = exchange(count, 1, [value], [plan])
+        if repeat > 1:
+            got = jnp.sum(got.reshape(HEADS, repeat, rows, -1).astype(F32), 1).astype(BF)
+        return jnp.transpose(got, (1, 0, 2)).reshape(rows, -1)
+
+    def to_head(value):
+        value = jnp.transpose(value.reshape(rows, HEADS, -1), (1, 0, 2))
+        if repeat > 1:
+            value = jnp.repeat(value, repeat, 0)
+        plan = Deal(count, value, place=lambda me, to: offset_of(count, to, me))
+        (got,) = exchange(count, 4, [value], [plan])
+        return got.reshape(group, -1)[:asked]
+
+    mixed = to_owner(mixed_f.astype(BF))
+    hidden = tokens[0].astype(F32)
+    residual = hidden + contract_last(mixed, output_full)
+
+    residual_scale = norm_scale(residual)
+    normed_two = (residual * residual_scale * gain_second).astype(BF)
+    (two_all,) = exchange(count, 2, [normed_two], [Gather(count, normed_two, 4)])
+    two_all = two_all.reshape(group, D)
+    route_all = box.gather(route_own)
+    two_all, up_expert, cot_low = meet(two_all, up_expert, cot_low)
+    cot_held = box.gather_step(cot_low, 0)
+    probs_all = jax.nn.softmax(matmul(two_all, router_full), -1)
+    mine = jnp.any(route_all == me, -1)
+    capacity = rows * TOP * 4 // (3 * experts) * count
+    slot = jnp.where(mine, jnp.cumsum(mine.astype(jnp.int32)) - 1, -1)
+    slots = jnp.arange(capacity, dtype=jnp.int32)
+    chosen = slots[:, None] == slot[None, :]
+    pick = chosen.astype(BF)
+    column = jnp.arange(experts, dtype=jnp.int32)[None, :] == me
+    gate_tok = jnp.where(mine, jnp.sum(jnp.where(column, probs_all, 0.0), -1), 0.0)
+    gate_row = jnp.sum(jnp.where(chosen, gate_tok[None, :], 0.0), 1)
+    rows_in = matmul(pick, two_all).astype(BF)
+
+    gate_val = matmul(rows_in, gate_expert)
+    up_val = matmul(rows_in, up_expert)
+    gate_val, cot_held = meet(gate_val, cot_held)
+    for dim in range(1, len(box.dims) - 1):
+        cot_held = box.gather_step(cot_held, dim)
+    act, slope = swiglu_parts(gate_val, up_val)
+    expert_hidden = (act * up_val).astype(BF)
+    produced = contract_last(expert_hidden, down_expert).astype(BF)
+    sg = matmul(two_all, sgate_own)
+    su = matmul(two_all, sup_own)
+    sact, sslope = swiglu_parts(sg, su)
+    shared_hidden = (sact * su).astype(BF)
+    out_two = (
+        gate_tok[:, None] * leading_contraction(pick, produced)
+        + contract_last(shared_hidden, sdown_own)
+    ).astype(BF)
+
+    out_two, cot_held = meet(out_two, cot_held)
+    cot_all = box.gather_step(cot_held, len(box.dims) - 1)
+    out_held = box.scatter_step(out_two, len(box.dims) - 1)
+    cot_rows = matmul(pick, cot_all)
+    grad_in = (gate_row[:, None] * cot_rows).astype(BF)
+    grad_hidden = matmul(grad_in, down_expert)
+    grad_hidden, out_held = meet(grad_hidden, out_held)
+    for dim in reversed(range(1, len(box.dims) - 1)):
+        out_held = box.scatter_step(out_held, dim)
+    grad_eg = (grad_hidden * up_val * slope).astype(BF)
+    grad_eu = (grad_hidden * act).astype(BF)
+    grad_rows = (contract_last(grad_eg, gate_expert) + contract_last(grad_eu, up_expert)).astype(BF)
+    gg_row = jnp.sum(cot_rows * produced.astype(F32), -1)
+    gg_tok = jnp.sum(jnp.where(chosen, gg_row[:, None], 0.0), 0)
+    grad_sh = matmul(cot_all, sdown_own)
+    grad_sg = (grad_sh * su * sslope).astype(BF)
+    grad_su = (grad_sh * sact).astype(BF)
+    grad_two_part = (
+        leading_contraction(pick, grad_rows)
+        + contract_last(grad_sg, sgate_own)
+        + contract_last(grad_su, sup_own)
+    ).astype(BF)
+    gg_part = jnp.where(column, gg_tok[:, None], 0.0)
+    grad_two_part, out_held = meet(grad_two_part, out_held)
+    output = residual + box.scatter_step(out_held, 0)
+    d_gate = leading_contraction(rows_in, grad_eg).astype(BF)
+    d_up = leading_contraction(rows_in, grad_eu).astype(BF)
+    d_down = leading_contraction(grad_in, expert_hidden).astype(BF)
+    d_experts = [
+        lax.psum_scatter(v, "fsdp", scatter_dimension=0, tiled=True).astype(F32)[None]
+        for v in (d_gate, d_up, d_down)
+    ]
+    d_rest = jnp.concatenate(
+        [
+            leading_contraction(two_all, grad_sg)[:, :fs],
+            leading_contraction(two_all, grad_su)[:, :fs],
+            leading_contraction(cot_all, shared_hidden)[:, :fs],
+        ],
+        1,
+    ).astype(BF)
+    d_rest = pad_last(d_rest, up_to(3 * fs)).reshape(count, 2, shard, -1)
+    grad_two_part, gg_part, d_rest, d_gate, d_up, d_down, output = meet(
+        grad_two_part, gg_part, d_rest, d_gate, d_up, d_down, output
+    )
+    rest_mine, rest_got = halves_sent(d_rest)
+    grad_two, grad_gates = reduce_blocks(
+        3,
+        grad_two_part.reshape(count, rows, D),
+        (gg_part.reshape(count, rows, -1), Scatter(count, gg_part.reshape(count, rows, -1), 1)),
+    )
+
+    probs = probs_all[:rows]
+    grad_logits = probs * (grad_gates - jnp.sum(probs * grad_gates, -1, keepdims=True))
+    grad_logits = grad_logits.astype(BF)
+    grad_two = grad_two + contract_last(grad_logits, router_full)
+    d_router = leading_contraction(normed_two, grad_logits)
+    d_second = jnp.sum(grad_two * residual * residual_scale, 0)
+    grad_residual = cotangent[0] + norm_back(residual, residual_scale, gain_second, grad_two)
+
+    attended = grad_residual.astype(BF)
+    grad_mixed = to_head(matmul(attended, output_full).astype(BF))
+    by_owner = jnp.take(attended.reshape(rows, count, -1), owners, axis=1).reshape(rows, -1)
+    grad_mixed, rest_mine, rest_got = meet(grad_mixed, rest_mine, rest_got)
+    d_rest = (rest_mine.astype(F32) + rest_got.astype(F32)).astype(BF)
+    d_rest = lax.all_to_all(d_rest, "ctx", split_axis=0, concat_axis=0, tiled=True).astype(F32)
+
+    d_output = leading_contraction(by_owner, mixed).astype(BF)
+    d_output = box.scatter_step(d_output, len(box.dims) - 1)
+    delta = jnp.sum(grad_mixed.astype(F32) * mixed_f, -1, keepdims=True)
+    probs_a = jnp.where(visible, jnp.exp(contract_last(query, keys) * scale - logsum), 0.0)
+    grad_probs = contract_last(grad_mixed, values)
+    grad_scores = (probs_a * (grad_probs - delta)).astype(BF)
+    grad_scores, d_output = meet(grad_scores, d_output)
+    for dim in reversed(range(1, len(box.dims) - 1)):
+        d_output = box.scatter_step(d_output, dim)
+    grad_query = matmul(grad_scores, keys) * scale
+    grad_keys = leading_contraction(grad_scores, query) * scale
+    grad_values = leading_contraction(probs_a.astype(BF), grad_mixed)
+    grad_expanded = jnp.concatenate([grad_keys[:, :NOPE], grad_values], -1).astype(BF)
+    grad_latent = contract_last(grad_expanded, expand_own)
+    d_expand = leading_contraction(latent, grad_expanded)
+    d_latent = jnp.sum(grad_latent * low_part * latent_scale, 0)
+    grad_comp = jnp.concatenate(
+        [
+            norm_back(low_part, latent_scale, gain_latent, grad_latent),
+            turn(grad_keys[:, NOPE:], cosine, -sine),
+        ],
+        -1,
+    ).astype(BF)
+    grad_qraw = jnp.concatenate(
+        [grad_query[:, :NOPE], turn(grad_query[:, NOPE:], cosine[:asked], -sine[:asked])], -1
+    ).astype(BF)
+    grad_comp, d_output = meet(grad_comp, d_output)
+    d_output = box.scatter_step(d_output, 0)
+    d_query = leading_contraction(normed_all[:asked], grad_qraw)
+    d_compress = leading_contraction(normed_all, grad_comp)
+    d_first = (
+        jnp.sum(d_query * query_own.astype(F32), 1) + jnp.sum(d_compress * compress_full.astype(F32), 1)
+    ) / gain_first
+
+    d_q = halves_summed(d_query.reshape(count, 2, shard, -1)).astype(BF)
+    d_e = halves_summed(d_expand.reshape(count, 2, -1, d_expand.shape[-1])).astype(BF)
+    d_lat = jnp.pad(d_latent.reshape(all_devices, lat_rows), ((0, 0), (0, shard - lat_rows)))
+    d_small = jnp.concatenate(
+        [d_compress, d_router, d_first[:, None], d_second[:, None], d_lat.reshape(-1)[:, None]], 1
+    ).astype(BF)
+    d_small = pad_last(d_small, up_to(small_cols)).reshape(count, 2, shard, -1)
+    d_small = jnp.take(d_small, owners, axis=0)
+    d_small = jnp.where(half == 0, d_small, d_small[:, ::-1])
+    d_small = jnp.transpose(d_small, (1, 0, 2, 3)).reshape(2 * count, shard, -1)
+    from_query = contract_last(grad_qraw, query_own)
+    if repeat > 1:
+        from_query = jnp.pad(from_query, ((0, group - asked), (0, 0)))
+    grad_norm_part = (from_query + contract_last(grad_comp, compress_full)).astype(BF)
+    grad_norm_part, d_output, d_rest = meet(grad_norm_part, d_output, d_rest)
+    output_mine, output_got = halves_sent(d_output.reshape(1, 2, shard, -1))
+    grad_norm, d_small, d_q, d_e = reduce_blocks(
+        5,
+        grad_norm_part.reshape(count, rows, D),
+        (d_small, Scatter(count, d_small, 1, both=True)),
+        (d_q, Deal(count, d_q)),
+        (d_e, Deal(count, d_e)),
+    )
+    output_mine, output_got = after(grad_norm, output_mine, output_got)
+    d_output = (output_mine.astype(F32) + output_got.astype(F32))[0]
+    grad_tokens = grad_residual + norm_back(hidden, norm_scale(hidden), gain_first, grad_norm)
+
+    def joined(parts, times):
+        if times > 1:
+            parts = jnp.sum(parts.astype(F32).reshape(count // times, times, *parts.shape[1:]), 1)
+        return jnp.transpose(parts.astype(F32), (1, 0, 2)).reshape(parts.shape[1], -1)
+
+    return (
+        output[None],
+        grad_tokens[None],
+        d_small[:, edge + experts],
+        d_small[:lat_rows, edge + experts + 2],
+        joined(d_q, repeat),
+        d_small[:, :edge],
+        joined(d_e, repeat),
+        d_output,
+        d_small[:, edge + experts + 1],
+        d_small[:, edge : edge + experts],
+        joined(d_rest[:, :, :fs], 1),
+        joined(d_rest[:, :, fs : 2 * fs], 1),
+        joined(d_rest[:, :, 2 * fs : 3 * fs], 1),
+        *d_experts,
+    )
 
 
 def shifted(shard, axis, by):
     devices = lax.axis_size(axis)
     return lax.ppermute(shard, axis, [(i, (i + by) % devices) for i in range(devices)])
-
-
-def matmul(left, right):
-    return jnp.dot(left, right, preferred_element_type=jnp.float32)
-
-
-def contract_last(left, right):
-    return lax.dot_general(
-        left, right, (((1,), (1,)), ((), ())), preferred_element_type=jnp.float32
-    )
-
-
-def leading_contraction(left, right):
-    return lax.dot_general(
-        left, right, (((0,), (0,)), ((), ())), preferred_element_type=jnp.float32
-    )
 
 
 def rms_norm(value, gain):
@@ -52,15 +933,6 @@
     return jnp.concatenate([first * cosine - second * sine, first * sine + second * cosine], -1)
 
 
-def placement(lengths_row, order_row):
-    ends = jnp.cumsum(lengths_row)
-    starts = ends - lengths_row
-    sequence = jnp.sum((order_row[:, None] >= ends[None, :]).astype(jnp.int32), 1)
-    chosen = sequence[:, None] == jnp.arange(lengths_row.shape[0], dtype=jnp.int32)[None, :]
-    offset = jnp.sum(jnp.where(chosen, starts[None, :], 0), 1)
-    return (sequence, order_row - offset)
-
-
 def expert_slots(route_rows, experts):
     flat = route_rows.reshape(-1)
     onehot = (flat[:, None] == jnp.arange(experts, dtype=jnp.int32)[None, :]).astype(jnp.int32)
@@ -76,7 +948,7 @@
     return jax.nn.softmax(value, -1)
 
 
-def local(
+def local_gathered(
     tokens,
     cotangent,
     lengths,
@@ -384,43 +1256,16 @@
 
 
 def solution(mesh):
-    in_specs = (
-        P("fsdp", "ctx", None),
-        P("fsdp", "ctx", None),
-        P("fsdp", None),
-        P("fsdp", None),
-        P("fsdp", "ctx", None),
-        P(("ctx", "fsdp")),
-        P(("ctx", "fsdp")),
-        P(("ctx", "fsdp"), None),
-        P(("ctx", "fsdp"), None),
-        P(("ctx", "fsdp"), None),
-        P(("ctx", "fsdp"), None),
-        P(("ctx", "fsdp")),
-        P(("ctx", "fsdp"), None),
-        P(("ctx", "fsdp"), None),
-        P(("ctx", "fsdp"), None),
-        P(("ctx", "fsdp"), None),
-        P("ctx", "fsdp", None),
-        P("ctx", "fsdp", None),
-        P("ctx", "fsdp", None),
-    )
-    out_specs = (
-        P("fsdp", "ctx", None),
-        P("fsdp", "ctx", None),
-        P(("ctx", "fsdp")),
-        P(("ctx", "fsdp")),
-        P(("ctx", "fsdp"), None),
-        P(("ctx", "fsdp"), None),
-        P(("ctx", "fsdp"), None),
-        P(("ctx", "fsdp"), None),
-        P(("ctx", "fsdp")),
-        P(("ctx", "fsdp"), None),
-        P(("ctx", "fsdp"), None),
-        P(("ctx", "fsdp"), None),
-        P(("ctx", "fsdp"), None),
-        P("ctx", "fsdp", None),
-        P("ctx", "fsdp", None),
-        P("ctx", "fsdp", None),
-    )
-    return jax.shard_map(local, mesh=mesh, in_specs=in_specs, out_specs=out_specs, check_vma=False)
+    token_spec = P("fsdp", "ctx", None)
+    vector = P(("ctx", "fsdp"))
+    matrix = P(("ctx", "fsdp"), None)
+    expert = P("ctx", "fsdp", None)
+    weights = (vector, vector, matrix, matrix, matrix, matrix, vector, matrix, matrix, matrix, matrix)
+    weights = weights + (expert,) * 3
+    return jax.shard_map(
+        local if mesh.shape["ctx"] == HEADS else local_gathered,
+        mesh=mesh,
+        in_specs=(token_spec, token_spec, P("fsdp", None), P("fsdp", None), token_spec) + weights,
+        out_specs=(token_spec, token_spec) + weights,
+        check_vma=False,
+    )

time: 4350 us -> 1120 us (0.26)
  waiting for transfers between devices: 3030 us -> 103 us
  Pallas kernels: 0 us -> 361 us
  local copies, waits for them, and re-layouts: 458 us -> 100 us
  blocking collectives: 149 us -> 0 us
  matrix products: 404 us -> 331 us
  starting transfers between devices: 115 us -> 51.8 us
    reduce_scatter x9 -> x3, waiting for transfers between devices: 1760 us -> 0.01 us  [local(): lax.psum_scatter(v, 'fsdp', scatter_dimension=0, tiled=True).astype(F32)]
    unnamed x25 -> x8, waiting for transfers between devices: 493 us -> 0.13 us
    pallas_call x0 -> x6, Pallas kernels: none -> 361 us  [exchange(): pl.pallas_call(functools.partial(exchange_kernel, count, plans, early), o...]
    scatter x2 -> x0, local copies, waits for them, and re-layouts: 276 us -> none  [local(): jnp.zeros((experts, capacity, D), jnp.bfloat16).at[flat, slot]]
    ppermute x64 -> x25, waiting for transfers between devices: 308 us -> 63.8 us  [the longest x20 59.6 us: shift(): lax.ppermute(value, 'ctx', [(i, target(i)) for i in range(self.count)])]
    all_gather x12 -> x5, waiting for transfers between devices: 252 us -> 35.8 us  [the longest x1 16.2 us: local(): lax.all_gather(output_cast.astype(BF), both, axis=0, tiled=True)]
    all_to_all x4 -> x2, waiting for transfers between devices: 217 us -> 2.83 us  [the longest x1 2.83 us: local(): lax.all_to_all(d_rest, 'ctx', split_axis=0, concat_axis=0, tiled=True)]
    dot_general x93 -> x15, matrix products: 232 us -> 107 us  [matmul(): return jnp.dot(left, right, preferred_element_type=F32)]
  transfers between devices with their start and end apart: 91 -> 35, of which waited for: 46 -> 12; matrix products, arithmetic and copies ran while one was open for 23% -> 48% of each run, Pallas kernels for 0% -> 33%
where the time goes in v1:
time: 1120 us; the launch traced here: 1110 us
  Pallas kernels  361 us (32%)
  matrix products  331 us (30%)
  other arithmetic  146 us (13%)
  waiting for transfers between devices  103 us (9%)
  local copies, waits for them, and re-layouts  100 us (9%)
  starting transfers between devices  51.8 us (5%)
  between operations  16.6 us (1%)
    pallas_call x6, Pallas kernels, exchange(): pl.pallas_call(functools.partial(exchange_kernel, count, plans, early), o...  361 us
    dot_general x15, matrix products, leading_contraction(): lax.dot_general(left, right, (((0,), (0,)), ((), ())), preferred_element_...  119 us
    dot_general x15, matrix products, matmul(): return jnp.dot(left, right, preferred_element_type=F32)  107 us
    dot_general x12, matrix products, contract_last(): lax.dot_general(left, right, (((1,), (1,)), ((), ())), preferred_element_...  105 us
    ppermute x20, waiting for transfers between devices, shift(): lax.ppermute(value, 'ctx', [(i, target(i)) for i in range(self.count)])  59.6 us
    ppermute x20, starting transfers between devices, shift(): lax.ppermute(value, 'ctx', [(i, target(i)) for i in range(self.count)])  33.1 us
  transfers between devices with their start and end apart: 35, of which 12 were waited for; matrix products, arithmetic and copies ran while one was open for 48% of the time, Pallas kernels for 33%

profile of v1, /device:TPU:0, one launch (start us, length us, event | category | flops | bytes accessed | tf_op | source)
XLA Modules:
  0.0 1109.1 jit_solution(1163279871047184738)
XLA Ops:
  19.1 89.6 %shard_map.306 = (bf16[16,2,64,192]{3,2,1,0:T(8,128)(2,1)}, bf16[16,2,16,256]{3,2,1,0:T(8,128)(2,1)}, bf16[16,128,2048]{2,1,0:T(8,128)(2,1)}) custom-call(bf16[16,64,192]{2,1,0:T(8,128)(2,1)} %bitcast.261, bf16[16,16,256]{2,1,0:T(8,128)(2,1)} %bitcast.272, bf16[128,2048]{1,0:T(8,128)(2,1)} %bitcast.237), custom_call_target="tpu_custom_call" | custom-call | bytes 104857600 | tf_op jit(solution)/shard_map/pallas_call | solution.py:512
  116.2 5.4 collective-permute-start.1
  153.7 8.7 multiply_convert_fusion.1
  162.5 8.8 fusion.2
  171.3 9.3 fusion.126
  196.5 6.1 fusion.3
  202.7 7.7 fusion.5
  210.4 7.1 fusion.133
  217.5 18.7 %shard_map.307 = bf16[16,128,128]{2,1,0:T(8,128)(2,1)} custom-call(bf16[16,128,128]{2,1,0:T(8,128)(2,1)} %bitcast.274), custom_call_target="tpu_custom_call" | custom-call | bytes 104857600 | tf_op jit(solution)/shard_map/pallas_call | solution.py:512
  243.0 16.2 %all-gather.9.cloned.1.call-done = bf16[2048,2048]{1,0:T(8,128)(2,1)} async-done(((bf16[64,2048]{1,0:T(8,128)(2,1)}), bf16[2048,2048]{1,0:T(8,128)(2,1)}) %all-gather.9.cloned.1.call-update) | async-done | bytes 8388624 | tf_op jit(solution)/shard_map/all_gather | solution.py:654
  259.2 6.5 multiply_reduce_fusion.9
  267.6 59.2 %shard_map.308 = bf16[16,128,2048]{2,1,0:T(8,128)(2,1)} custom-call(bf16[128,2048]{1,0:T(8,128)(2,1)} %multiply_convert_fusion.10.refs_0_), custom_call_target="tpu_custom_call" | custom-call | bytes 104857600 | tf_op jit(solution)/shard_map/pallas_call | solution.py:512
  326.8 7.6 all-gather.11.cloned.1.call-done
  338.9 12.8 %fusion.20 = bf16[1024,2048]{1,0:T(8,128)(2,1)} fusion(bf16[2048,2048]{1,0:T(8,128)(2,1)} %bitcast.215, s32[2048]{0:T(1024)S(1)} %copy-done.95), kind=kOutput, calls=%fused_computation.58 | convolution fusion | flops 8594128896 | bytes 12591104 | tf_op jit(solution)/shard_map/dot_general | solution.py:24
  362.2 8.1 multiply_convert_fusion.9
  370.3 6.6 fusion.138
  377.0 8.7 fusion.39
  389.2 9.2 multiply_convert_fusion.5
  398.3 12.0 %all-gather.13.cloned.1.call-done = bf16[2048,1408]{1,0:T(8,128)(2,1)} async-done(((bf16[1024,1408]{1,0:T(8,128)(2,1)}), bf16[2048,1408]{1,0:T(8,128)(2,1)}) %all-gather.13.cloned.1.call-update) | async-done | bytes 5767184 | tf_op jit(solution)/shard_map/all_gather | solution.py:656
  410.3 11.1 %convolution_convert_fusion.4 = bf16[1024,2048]{1,0:T(8,128)(2,1)} fusion(bf16[1024,1408]{1,0:T(8,128)(2,1)} %get-tuple-element.315, bf16[2048,1408]{1,0:T(8,128)(2,1)} %all-gather.13.cloned.1.call-done), kind=kOutput, calls=%fused_computation.59 | convolution fusion | flops 5907677184 | bytes 12845056 | tf_op jit(solution)/shard_map/dot_general | solution.py:28
  421.4 13.9 %add_convert_fusion.2 = bf16[2048,2048]{1,0:T(8,128)(2,1)S(1)} fusion(f32[2048,2048]{1,0:T(8,128)} %fusion.39, f32[2048]{0:T(1024)S(1)} %broadcast_select_fusion.1, bf16[1024,2048]{1,0:T(8,128)(2,1)} %convolution_convert_fusion.4, s32[2048]{0:T(1024)S(1)} %copy-done.95), kind=kOutput, calls=%fused_computation.12 | convolution fusion | flops 8604614656 | bytes 29376512 | tf_op jit(solution)/shard_map/dot_general | solution.py:32
  447.2 13.6 %multiply_reduce_fusion = (f32[1024]{0:T(1024)S(1)}, f32[1024,2048]{1,0:T(8,128)}) fusion(bf16[1024,2048]{1,0:T(8,128)(2,1)S(1)} %copy-done.123, bf16[2048,2048]{1,0:T(8,128)(2,1)} %constant_dynamic-update-slice_fusion.11, s32[2048]{0:T(1024)S(1)} %copy-done.95), kind=kOutput, calls=%fused_computation.23 | convolution fusion | flops 8598322176 | bytes 20983808 | tf_op jit(solution)/shard_map/dot_general | solution.py:24
  468.2 11.1 %fusion.123 = f32[1024,1408]{1,0:T(8,128)S(1)} fusion(bf16[2048,1408]{1,0:T(8,128)(2,1)} %all-gather.13.cloned.1.call-done, f32[1024,2048]{1,0:T(8,128)} %get-tuple-element.318, f32[1024]{0:T(1024)S(1)} %get-tuple-element.249), kind=kOutput, calls=%fused_computation.291 | convolution fusion | flops 5909774336 | bytes 19927040 | tf_op jit(solution)/shard_map/dot_general | solution.py:24
  485.0 8.7 convolution_convert_fusion.2
  507.2 6.4 fusion.142
  519.6 9.0 fusion.139
  528.5 8.8 convolution_convert_fusion.1
  537.4 5.8 fusion.140
  544.2 9.6 fusion.44
  553.8 23.4 %fusion.7 = f32[2048,2048]{1,0:T(8,128)} fusion(f32[1024,2048]{1,0:T(8,128)} %fusion.139, bf16[1024,1408]{1,0:T(8,128)(2,1)} %get-tuple-element.256, bf16[2048,1408]{1,0:T(8,128)(2,1)} %all-gather.11.cloned.1.call-done, pred[1024,2048]{1,0:T(32,128)(4,1)S(1)} %copy-done.48), kind=kOutput, calls=%fused_computation.29 | convolution fusion | flops 14499708928 | bytes 35913728 | tf_op jit(solution)/shard_map/dot_general | solution.py:32
  577.1 15.8 %add_convert_fusion.1 = bf16[2048,2048]{1,0:T(8,128)(2,1)} fusion(f32[2048,2048]{1,0:T(8,128)} %fusion.7, f32[2048,2048]{1,0:T(8,128)} %fusion.44, bf16[2048,256]{1,0:T(8,128)(2,1)} %copy-done.52, bf16[2048,176]{1,0:T(8,128)(2,1)S(1)} %copy-done.24), kind=kOutput, calls=%fused_computation.11 | convolution fusion | flops 2160066560 | bytes 43712512 | tf_op jit(solution)/shard_map/dot_general | solution.py:28
  592.9 12.0 %convolution_convert_fusion = bf16[2048,1408]{1,0:T(8,128)(2,1)} fusion(bf16[1024,1408]{1,0:T(8,128)(2,1)} %get-tuple-element.315, f32[1024,2048]{1,0:T(8,128)} %get-tuple-element.318, f32[1024]{0:T(1024)S(1)} %get-tuple-element.249), kind=kOutput, calls=%fused_computation.35 | convolution fusion | flops 5912657920 | bytes 17043456 | tf_op jit(solution)/shard_map/dot_general | solution.py:32
  626.5 21.4 %collective-permute-done.14 = bf16[128,2048]{1,0:T(8,128)(2,1)} collective-permute-done((bf16[128,2048]{1,0:T(8,128)(2,1)}, bf16[128,2048]{1,0:T(8,128)(2,1)}, u32[]{:S(2)}, u32[]{:S(2)}) %collective-permute-start.14) | collective-permute-done | bytes 524320 | tf_op jit(solution)/shard_map/ppermute | solution.py:83
  651.2 77.4 %shard_map.309 = (f32[128,16]{1,0:T(8,128)}, f32[128,2048]{1,0:T(8,128)}) custom-call(f32[16,128,16]{2,1,0:T(8,128)} %bitcast.251, bf16[16,128,2048]{2,1,0:T(8,128)(2,1)} %bitcast.226), custom_call_target="tpu_custom_call" | custom-call | bytes 104857600 | tf_op jit(solution)/shard_map/pallas_call | solution.py:512
  754.2 12.7 %shard_map.310 = bf16[16,128,128]{2,1,0:T(8,128)(2,1)} custom-call(bf16[16,128,128]{2,1,0:T(8,128)(2,1)} %bitcast.268), custom_call_target="tpu_custom_call" | custom-call | bytes 104857600 | tf_op jit(solution)/shard_map/pallas_call | solution.py:512
  772.4 8.0 all-to-all-start.1
  780.5 11.8 %fusion.22 = bf16[2048,128]{0,1:T(8,128)(2,1)} fusion(bf16[2048,128]{1,0:T(8,128)(2,1)} %bitcast.256, f32[2048,2048]{0,1:T(8,128)} %copy-done.6, f32[2048]{0:T(1024)S(1)} %log_add_fusion, s32[2048]{0:T(1024)S(1)} %copy-done.86, s32[2048]{0:T(1024)S(1)} %copy-done.75), kind=kOutput, calls=%fused_computation.73 | convolution fusion | flops 1103364096 | bytes 17850368 | tf_op jit(solution)/shard_map/dot_general | solution.py:32
  792.7 12.3 %multiply_convert_fusion = bf16[2048,2048]{0,1:T(8,128)(2,1)} fusion(f32[2048,2048]{0,1:T(8,128)} %copy-done.6, bf16[2048,128]{1,0:T(8,128)(2,1)S(1)} %bitcast.258, f32[2048]{0:T(1024)S(1)} %multiply_reduce_fusion.7, f32[2048]{0:T(1024)S(1)} %log_add_fusion, s32[2048]{0:T(1024)S(1)} %copy-done.86, s32[2048]{0:T(1024)S(1)} %copy-done.75, ...), kind=kOutput, calls=%fused_computation.9 | convolution fusion | flops 1111490560 | bytes 26263552 | tf_op jit(solution)/shard_map/dot_general | solution.py:28
  809.6 5.4 add_convert_fusion.3
  815.1 6.8 convolution_multiply_fusion
  821.9 6.4 convolution_multiply_fusion.1
  864.8 16.5 %collective-permute-done.18 = bf16[512,2048]{1,0:T(8,128)(2,1)} collective-permute-done((bf16[512,2048]{1,0:T(8,128)(2,1)}, bf16[512,2048]{1,0:T(8,128)(2,1)}, u32[]{:S(2)}, u32[]{:S(2)}) %collective-permute-start.18) | collective-permute-done | bytes 2097184 | tf_op jit(solution)/shard_map/ppermute | solution.py:83
  885.8 9.8 multiply_reduce_fusion.1
  901.0 6.3 concatenate.85
  925.4 10.3 fusion.124
  935.7 9.3 add_convert_fusion
  945.0 12.2 %collective-permute-done.22 = bf16[128,2048]{1,0:T(8,128)(2,1)} collective-permute-done((bf16[128,2048]{1,0:T(8,128)(2,1)}, bf16[128,2048]{1,0:T(8,128)(2,1)}, u32[]{:S(2)}, u32[]{:S(2)}) %collective-permute-start.22) | collective-permute-done | bytes 524320 | tf_op jit(solution)/shard_map/ppermute | solution.py:83
  960.9 102.9 %shard_map.311 = (f32[64,640]{1,0:T(8,128)}, bf16[16,64,192]{2,1,0:T(8,128)(2,1)}, bf16[16,16,256]{2,1,0:T(8,128)(2,1)}, f32[128,2048]{1,0:T(8,128)}) custom-call(bf16[32,64,640]{2,1,0:T(8,128)(2,1)} %bitcast.232, bf16[16,64,192]{2,1,0:T(8,128)(2,1)} %fusion.34.refs_1_, bf16[16,16,256]{2,1,0:T(8,128)(2,1)} %fusion.92.refs_2_, bf16[16,128,2048]{2,1,0:T(8,128)(2,1)} %bitcast.225), custom_call_target="tpu_custom_call" | custom-call | bytes 104857600 | tf_op jit(solution)/shard_map/pallas_call | solution.py:512
  (565 shorter events, 305.5 us)
Async XLA Ops:
  7.2 136.1 %copy-start = (s32[1,2048]{1,0:T(1,128)S(1)}, s32[1,2048]{1,0:T(1,128)}, u32[]{:S(2)}) copy-start(s32[1,2048]{1,0:T(1,128)} %param.22) | copy-start | bytes 24580
  7.2 144.5 %all-gather.7.cloned.1.call-start = ((), (), s32[]{:S(2)}) async-start(), calls=%async_computation.5 | async-start | bytes 2703360 | tf_op jit(solution)/shard_map/all_gather | solution.py:627
  12.1 184.4 %all-gather.15.cloned.1.call-start = ((), (), s32[]{:S(2)}) async-start(), calls=%async_computation.12 | async-start | bytes 8650752 | tf_op jit(solution)/shard_map/all_gather | solution.py:628
  16.7 92.0 %copy-start.66 = (f32[64,2048]{1,0:T(8,128)S(1)}, f32[64,2048]{1,0:T(8,128)}, u32[]{:S(2)}) copy-start(f32[64,2048]{1,0:T(8,128)} %param.29) | copy-start | bytes 1572868
  16.8 242.4 %all-gather.9.cloned.1.call-start = ((), (), s32[]{:S(2)}) async-start(), calls=%async_computation.6 | async-start | bytes 8650752 | tf_op jit(solution)/shard_map/all_gather | solution.py:654
  109.6 224.9 %all-gather.11.cloned.1.call-start = ((), (), s32[]{:S(2)}) async-start(), calls=%async_computation.7 | async-start | bytes 8650752 | tf_op jit(solution)/shard_map/all_gather | solution.py:655
  115.1 29.7 %collective-permute-start = (s32[128,6]{0,1:T(8,128)S(1)}, s32[128,6]{0,1:T(8,128)S(1)}, u32[]{:S(2)}, u32[]{:S(2)}) collective-permute-start(s32[128,6]{0,1:T(8,128)S(1)} %bitcast.283), channel_id=1, source_target_pairs={{0,8},{2,10},{4,12},{6,14},{8,16},{10,18},{12,20},{14,22},{16,24},... | collective-permute-start | bytes 9224 | tf_op jit(solution)/shard_map/ppermute | solution.py:83
  116.2 28.6 %collective-permute-start.1 = (s32[128,6]{0,1:T(8,128)S(1)}, s32[128,6]{0,1:T(8,128)S(1)}, u32[]{:S(2)}, u32[]{:S(2)}) collective-permute-start(s32[128,6]{0,1:T(8,128)S(1)} %bitcast.284), channel_id=1, source_target_pairs={{0,16},{2,18},{4,20},{6,22},{8,24},{10,26},{12,28},{14,30},{16,0},... | collective-permute-start | bytes 9224 | tf_op jit(solution)/shard_map/ppermute | solution.py:83
  121.6 23.3 %collective-permute-start.2 = (s32[128,6]{0,1:T(8,128)S(1)}, s32[128,6]{0,1:T(8,128)S(1)}, u32[]{:S(2)}, u32[]{:S(2)}) collective-permute-start(s32[128,6]{0,1:T(8,128)S(1)} %bitcast.285), channel_id=1, source_target_pairs={{0,24},{2,26},{4,28},{6,30},{8,0},{10,2},{12,4},{14,6},{16,8},{18,... | collective-permute-start | bytes 9224 | tf_op jit(solution)/shard_map/ppermute | solution.py:83
  128.1 52.5 %all-to-all-start = ((bf16[16,64,640]{2,1,0:T(8,128)(2,1)}), bf16[16,64,640]{2,1,0:T(8,128)(2,1)}, u32[]{:S(2)}, u32[]{:S(2)}) async-start(bf16[16,64,640]{2,1,0:T(8,128)(2,1)} %pad.37.clone), calls=%async_computation | async-start | bytes 2621440 | tf_op jit(solution)/shard_map/all_to_all | solution.py:667
  132.5 277.8 %all-gather.13.cloned.1.call-start = ((), (), s32[]{:S(2)}) async-start(), calls=%async_computation.8 | async-start | bytes 8650752 | tf_op jit(solution)/shard_map/all_gather | solution.py:656
  137.1 950.0 %reduce-scatter.4.cloned.1.call-start = ((), (), s32[]{:S(2)}) async-start(), calls=%async_computation.9 | async-start | bytes 8650752 | tf_op jit(solution)/shard_map/reduce_scatter | solution.py:795
  144.0 66.3 %copy-start.74 = (s32[2048]{0:T(1024)}, s32[2048]{0:T(1024)S(1)}, u32[]{:S(2)}) copy-start(s32[2048]{0:T(1024)S(1)} %convert_reduce_fusion.1) | copy-start | bytes 24580
  144.8 4.4 collective-permute-start.3
  149.2 1.2 collective-permute-start.4
  191.2 47.1 %collective-permute-start.8 = (bf16[16,64,640]{2,1,0:T(8,128)(2,1)}, bf16[16,64,640]{2,1,0:T(8,128)(2,1)}, u32[]{:S(2)}, u32[]{:S(2)}) collective-permute-start(bf16[16,64,640]{2,1,0:T(8,128)(2,1)} %all-to-all-done), channel_id=1, source_target_pairs={{0,1},{1,0},{2,3},{3,2},{4,5},{5,4},{6,7},{7,6},{8,9},{9,8},{10,11... | collective-permute-start | bytes 3932168 | tf_op jit(solution)/shard_map/ppermute | solution.py:594
  196.4 69.3 %copy-start.79 = (f32[2048]{0:T(1024)}, f32[2048]{0:T(1024)S(1)}, u32[]{:S(2)}) copy-start(f32[2048]{0:T(1024)S(1)} %convert_reduce_fusion) | copy-start | bytes 24580
  240.6 111.1 %copy-start.8 = (bf16[16,2,64,640]{3,2,1,0:T(8,128)(2,1)}, bf16[16,2,64,640]{3,2,1,0:T(8,128)(2,1)S(1)}, u32[]{:S(2)}) copy-start(bf16[16,2,64,640]{3,2,1,0:T(8,128)(2,1)S(1)} %pad_maximum_fusion.1) | copy-start | bytes 7864324
  267.6 66.8 %copy-start.49 = (bf16[128,2048]{1,0:T(8,128)(2,1)S(1)}, bf16[128,2048]{1,0:T(8,128)(2,1)}, u32[]{:S(2)}) copy-start(bf16[128,2048]{1,0:T(8,128)(2,1)} %bitcast_convert_fusion.4) | copy-start | bytes 1572868
  267.6 71.3 %copy-start.95 = (s32[2048]{0:T(1024)S(1)}, s32[2048]{0:T(1024)}, u32[]{:S(2)}) copy-start(s32[2048]{0:T(1024)} %bitcast_select_fusion) | copy-start | bytes 24580
  334.4 51.3 %collective-permute-start.7 = (bf16[128,2048]{1,0:T(8,128)(2,1)S(1)}, bf16[128,2048]{1,0:T(8,128)(2,1)}, u32[]{:S(2)}, u32[]{:S(2)}) collective-permute-start(bf16[128,2048]{1,0:T(8,128)(2,1)S(1)} %copy-done.49), channel_id=1, source_target_pairs={{0,24},{2,26},{4,28},{6,30},{8,0},{10,2},{12,4},{14,6},{16,8},{18,... | collective-permute-start | bytes 1572872 | tf_op jit(solution)/shard_map/ppermute | solution.py:83
  337.8 47.9 %collective-permute-start.6 = (bf16[128,2048]{1,0:T(8,128)(2,1)S(1)}, bf16[128,2048]{1,0:T(8,128)(2,1)}, u32[]{:S(2)}, u32[]{:S(2)}) collective-permute-start(bf16[128,2048]{1,0:T(8,128)(2,1)S(1)} %copy-done.49), channel_id=1, source_target_pairs={{0,16},{2,18},{4,20},{6,22},{8,24},{10,26},{12,28},{14,30},{16,0},... | collective-permute-start | bytes 1572872 | tf_op jit(solution)/shard_map/ppermute | solution.py:83
  337.8 47.9 %collective-permute-start.5 = (bf16[128,2048]{1,0:T(8,128)(2,1)S(1)}, bf16[128,2048]{1,0:T(8,128)(2,1)}, u32[]{:S(2)}, u32[]{:S(2)}) collective-permute-start(bf16[128,2048]{1,0:T(8,128)(2,1)S(1)} %copy-done.49), channel_id=1, source_target_pairs={{0,8},{2,10},{4,12},{6,14},{8,16},{10,18},{12,20},{14,22},{16,24},... | collective-permute-start | bytes 1572872 | tf_op jit(solution)/shard_map/ppermute | solution.py:83
  387.6 47.8 %collective-permute-start.9 = (bf16[512,2048]{1,0:T(8,128)(2,1)S(1)}, bf16[512,2048]{1,0:T(8,128)(2,1)}, u32[]{:S(2)}, u32[]{:S(2)}) collective-permute-start(bf16[512,2048]{1,0:T(8,128)(2,1)S(1)} %pad_maximum_fusion.4), channel_id=1, source_target_pairs={{0,4},{2,6},{4,0},{6,2},{8,12},{10,14},{12,8},{14,10},{16,20},{18,... | collective-permute-start | bytes 6291464 | tf_op jit(solution)/shard_map/ppermute | solution.py:83
  437.7 7.2 collective-permute-start.10
  438.4 25.5 %collective-permute-start.11 = (bf16[1024,2048]{1,0:T(8,128)(2,1)S(1)}, bf16[1024,2048]{1,0:T(8,128)(2,1)S(1)}, u32[]{:S(2)}, u32[]{:S(2)}) collective-permute-start(bf16[1024,2048]{1,0:T(8,128)(2,1)S(1)} %split.49), channel_id=1, source_target_pairs={{0,2},{2,0},{4,6},{6,4},{8,10},{10,8},{12,14},{14,12},{16,18},{18,... | collective-permute-start | bytes 12582920 | tf_op jit(solution)/shard_map/ppermute | solution.py:83
  493.7 598.2 %reduce-scatter.6.cloned.1.call-start = ((), (), s32[]{:S(2)}) async-start(), calls=%async_computation.10 | async-start | bytes 8650752 | tf_op jit(solution)/shard_map/reduce_scatter | solution.py:795
  505.7 99.2 %collective-permute-start.12 = (bf16[512,2048]{1,0:T(8,128)(2,1)}, bf16[512,2048]{1,0:T(8,128)(2,1)}, u32[]{:S(2)}, u32[]{:S(2)}) collective-permute-start(bf16[512,2048]{1,0:T(8,128)(2,1)} %split.51), channel_id=1, source_target_pairs={{0,4},{2,6},{4,0},{6,2},{8,12},{10,14},{12,8},{14,10},{16,20},{18,... | collective-permute-start | bytes 6291464 | tf_op jit(solution)/shard_map/ppermute | solution.py:83
  537.4 559.3 %reduce-scatter.8.cloned.1.call-start = ((), (), s32[]{:S(2)}) async-start(), calls=%async_computation.11 | async-start | bytes 8650752 | tf_op jit(solution)/shard_map/reduce_scatter | solution.py:795
  609.4 17.1 %collective-permute-start.15 = (bf16[128,2048]{1,0:T(8,128)(2,1)}, bf16[128,2048]{1,0:T(8,128)(2,1)}, u32[]{:S(2)}, u32[]{:S(2)}) collective-permute-start(bf16[128,2048]{1,0:T(8,128)(2,1)} %get-tuple-element.279), channel_id=1, source_target_pairs={{0,8},{2,10},{4,12},{6,14},{8,16},{10,18},{12,20},{14,22},{16,24},... | collective-permute-start | bytes 1572872 | tf_op jit(solution)/shard_map/ppermute | solution.py:83
  611.1 36.9 %collective-permute-start.14 = (bf16[128,2048]{1,0:T(8,128)(2,1)}, bf16[128,2048]{1,0:T(8,128)(2,1)}, u32[]{:S(2)}, u32[]{:S(2)}) collective-permute-start(bf16[128,2048]{1,0:T(8,128)(2,1)} %get-tuple-element.280), channel_id=1, source_target_pairs={{0,16},{2,18},{4,20},{6,22},{8,24},{10,26},{12,28},{14,30},{16,0},... | collective-permute-start | bytes 1572872 | tf_op jit(solution)/shard_map/ppermute | solution.py:83
  613.5 34.5 %collective-permute-start.13 = (bf16[128,2048]{1,0:T(8,128)(2,1)S(1)}, bf16[128,2048]{1,0:T(8,128)(2,1)}, u32[]{:S(2)}, u32[]{:S(2)}) collective-permute-start(bf16[128,2048]{1,0:T(8,128)(2,1)S(1)} %get-tuple-element.278), channel_id=1, source_target_pairs={{0,24},{2,26},{4,28},{6,30},{8,0},{10,2},{12,4},{14,6},{16,8},{18,... | collective-permute-start | bytes 1572872 | tf_op jit(solution)/shard_map/ppermute | solution.py:83
  651.2 78.6 %copy-start.80 = (f32[2048]{0:T(1024)S(1)}, f32[2048]{0:T(1024)}, u32[]{:S(2)}) copy-start(f32[2048]{0:T(1024)} %copy-done.79) | copy-start | bytes 24580
  651.2 78.6 %copy-start.106 = (f32[128]{0:T(128)S(1)}, f32[128]{0:T(128)}, u32[]{:S(2)}) copy-start(f32[128]{0:T(128)} %copy-done.105) | copy-start | bytes 1540
  651.2 80.8 %copy-start.116 = (f32[128]{0:T(128)S(1)}, f32[128]{0:T(128)}, u32[]{:S(2)}) copy-start(f32[128]{0:T(128)} %copy-done.115) | copy-start | bytes 1540
  733.3 36.1 %collective-permute-start.16 = (bf16[16,64,640]{2,1,0:T(8,128)(2,1)}, bf16[16,64,640]{2,1,0:T(8,128)(2,1)}, u32[]{:S(2)}, u32[]{:S(2)}) collective-permute-start(bf16[16,64,640]{2,1,0:T(8,128)(2,1)} %get-tuple-element.267), channel_id=1, source_target_pairs={{0,1},{1,0},{2,3},{3,2},{4,5},{5,4},{6,7},{7,6},{8,9},{9,8},{10,11... | collective-permute-start | bytes 3932168 | tf_op jit(solution)/shard_map/ppermute | solution.py:594
  746.4 63.2 %collective-permute-start.17 = (bf16[1024,2048]{1,0:T(8,128)(2,1)}, bf16[1024,2048]{1,0:T(8,128)(2,1)}, u32[]{:S(2)}, u32[]{:S(2)}) collective-permute-start(bf16[1024,2048]{1,0:T(8,128)(2,1)} %split.65), channel_id=1, source_target_pairs={{0,2},{2,0},{4,6},{6,4},{8,10},{10,8},{12,14},{14,12},{16,18},{18,... | collective-permute-start | bytes 12582920 | tf_op jit(solution)/shard_map/ppermute | solution.py:83
  772.4 35.4 %all-to-all-start.1 = ((bf16[16,64,640]{2,1,0:T(8,128)(2,1)}), bf16[16,64,640]{2,1,0:T(8,128)(2,1)S(1)}, u32[]{:S(2)}, u32[]{:S(2)}) async-start(bf16[16,64,640]{2,1,0:T(8,128)(2,1)} %add_convert_fusion.9), calls=%async_computation.1 | async-start | bytes 2621440 | tf_op jit(solution)/shard_map/all_to_all | solution.py:830
  832.3 49.0 %collective-permute-start.18 = (bf16[512,2048]{1,0:T(8,128)(2,1)}, bf16[512,2048]{1,0:T(8,128)(2,1)}, u32[]{:S(2)}, u32[]{:S(2)}) collective-permute-start(bf16[512,2048]{1,0:T(8,128)(2,1)} %split.59), channel_id=1, source_target_pairs={{0,4},{2,6},{4,0},{6,2},{8,12},{10,14},{12,8},{14,10},{16,20},{18,... | collective-permute-start | bytes 6291464 | tf_op jit(solution)/shard_map/ppermute | solution.py:83
  843.3 19.0 %collective-permute-start.19 = (bf16[16,64,192]{2,1,0:T(8,128)(2,1)}, bf16[16,64,192]{2,1,0:T(8,128)(2,1)}, u32[]{:S(2)}, u32[]{:S(2)}) collective-permute-start(bf16[16,64,192]{2,1,0:T(8,128)(2,1)} %fusion.48), channel_id=1, source_target_pairs={{0,1},{1,0},{2,3},{3,2},{4,5},{5,4},{6,7},{7,6},{8,9},{9,8},{10,11... | collective-permute-start | bytes 1179656 | tf_op jit(solution)/shard_map/ppermute | solution.py:594
  848.6 12.1 %collective-permute-start.20 = (bf16[16,16,256]{2,1,0:T(8,128)(2,1)}, bf16[16,16,256]{2,1,0:T(8,128)(2,1)}, u32[]{:S(2)}, u32[]{:S(2)}) collective-permute-start(bf16[16,16,256]{2,1,0:T(8,128)(2,1)} %fusion.94), channel_id=1, source_target_pairs={{0,1},{1,0},{2,3},{3,2},{4,5},{5,4},{6,7},{7,6},{8,9},{9,8},{10,11... | collective-permute-start | bytes 393224 | tf_op jit(solution)/shard_map/ppermute | solution.py:594
  917.8 27.2 %collective-permute-start.23 = (bf16[128,2048]{1,0:T(8,128)(2,1)}, bf16[128,2048]{1,0:T(8,128)(2,1)S(1)}, u32[]{:S(2)}, u32[]{:S(2)}) collective-permute-start(bf16[128,2048]{1,0:T(8,128)(2,1)} %get-tuple-element.276), channel_id=1, source_target_pairs={{0,8},{2,10},{4,12},{6,14},{8,16},{10,18},{12,20},{14,22},{16,24},... | collective-permute-start | bytes 1572872 | tf_op jit(solution)/shard_map/ppermute | solution.py:83
  921.6 35.6 %collective-permute-start.22 = (bf16[128,2048]{1,0:T(8,128)(2,1)}, bf16[128,2048]{1,0:T(8,128)(2,1)}, u32[]{:S(2)}, u32[]{:S(2)}) collective-permute-start(bf16[128,2048]{1,0:T(8,128)(2,1)} %get-tuple-element.277), channel_id=1, source_target_pairs={{0,16},{2,18},{4,20},{6,22},{8,24},{10,26},{12,28},{14,30},{16,0},... | collective-permute-start | bytes 1572872 | tf_op jit(solution)/shard_map/ppermute | solution.py:83
  922.9 34.3 %collective-permute-start.21 = (bf16[128,2048]{1,0:T(8,128)(2,1)}, bf16[128,2048]{1,0:T(8,128)(2,1)}, u32[]{:S(2)}, u32[]{:S(2)}) collective-permute-start(bf16[128,2048]{1,0:T(8,128)(2,1)} %get-tuple-element.275), channel_id=1, source_target_pairs={{0,24},{2,26},{4,28},{6,30},{8,0},{10,2},{12,4},{14,6},{16,8},{18,... | collective-permute-start | bytes 1572872 | tf_op jit(solution)/shard_map/ppermute | solution.py:83
  958.7 105.2 %copy-start.31 = (f32[128,2048]{1,0:T(8,128)}, f32[128,2048]{1,0:T(8,128)S(1)}, u32[]{:S(2)}) copy-start(f32[128,2048]{1,0:T(8,128)S(1)} %convert_add_fusion) | copy-start | bytes 3145732
  959.5 125.9 %collective-permute-start.24 = (bf16[1,64,2048]{2,1,0:T(8,128)(2,1)}, bf16[1,64,2048]{2,1,0:T(8,128)(2,1)}, u32[]{:S(2)}, u32[]{:S(2)}) collective-permute-start(bf16[1,64,2048]{2,1,0:T(8,128)(2,1)} %fusion.91), channel_id=1, source_target_pairs={{0,1},{1,0},{2,3},{3,2},{4,5},{5,4},{6,7},{7,6},{8,9},{9,8},{10,11... | collective-permute-start | bytes 786440 | tf_op jit(solution)/shard_map/ppermute | solution.py:594
  960.9 104.6 %copy-start.17 = (bf16[1,128,2048]{2,1,0:T(8,128)(2,1)S(1)}, bf16[1,128,2048]{2,1,0:T(8,128)(2,1)}, u32[]{:S(2)}) copy-start(bf16[1,128,2048]{2,1,0:T(8,128)(2,1)} %param.19) | copy-start | bytes 1572868
  960.9 104.6 %copy-start.73 = (f32[2048,1]{0,1:T(1,128)S(1)}, f32[2048,1]{0,1:T(1,128)}, u32[]{:S(2)}) copy-start(f32[2048,1]{0,1:T(1,128)} %copy-done.72) | copy-start | bytes 24580
  (134 other events, 1195.2 us)
Sparse Core Ops, SparseCore 0:
  12.2 78.1 all-gather.6
  92.6 74.7 all-gather.14
  170.9 88.2 all-gather.8
  261.1 73.2 all-gather.10
  335.8 74.4 all-gather.12
  493.8 71.3 reduce-scatter.3
  568.2 71.3 reduce-scatter.5
  641.9 71.3 reduce-scatter.7

commit v2 on v1

--- a/solution.py
+++ b/solution.py
@@ -91,34 +91,28 @@
             owner = (offset[:, None] + owner[None, :]).reshape(-1)
         return owner
 
-    def gather_step(self, held, dim):
-        shifted = [self.shift(held, dim, k) for k in range(1, self.dims[dim])]
-        return jnp.concatenate([held] + shifted, 0)
+    def spread(self, held, dim):
+        return [held] + [self.shift(held, dim, k) for k in range(1, self.dims[dim])]
 
     def gather(self, held):
         for dim in range(len(self.dims)):
-            held = self.gather_step(held, dim)
+            held = jnp.concatenate(self.spread(held, dim), 0)
         return held
 
-    def scatter_step(self, held, dim):
+    def share(self, held, dim):
         parts = jnp.split(held, self.dims[dim], 0)
-        total = parts[0].astype(F32)
-        for k in range(1, self.dims[dim]):
-            total = total + self.shift(parts[k], dim, -k).astype(F32)
-        return total if dim == 0 else total.astype(held.dtype)
-
-    def scatter(self, held):
-        for dim in reversed(range(len(self.dims))):
-            held = self.scatter_step(held, dim)
-        return held
-
-
-def after(event, *values):
-    return lax.optimization_barrier((event,) + values)[1:]
-
-
-def meet(*values):
-    return lax.optimization_barrier(values)
+        return parts[:1] + [self.shift(parts[k], dim, -k) for k in range(1, self.dims[dim])]
+
+
+def joined(parts):
+    return jnp.concatenate(parts, 0)
+
+
+def summed(parts, dtype):
+    total = parts[0].astype(F32)
+    for part in parts[1:]:
+        total = total + part.astype(F32)
+    return total.astype(dtype)
 
 
 MESH = pl.DeviceIdType.MESH
@@ -131,7 +125,9 @@
         stride //= side
         found.append(("ctx", side, stride, held))
         held *= side
-    return found + ([("fsdp", 2, 1, held)] if both else [])
+    if both:
+        found = [("fsdp", 2, 1, 1)] + [(axis, n, by, held * 2) for axis, n, by, held in found]
+    return found
 
 
 def moved(me, side, stride, by):
@@ -160,7 +156,7 @@
 class Gather:
     def __init__(self, count, value, chunks):
         self.count, self.chunks = count, chunks
-        self.out = jax.ShapeDtypeStruct((count,) + value.shape, value.dtype)
+        self.taken, self.outs = 1, [jax.ShapeDtypeStruct((count,) + value.shape, value.dtype)]
         self.scratch = [DMA, DMA((count, chunks)), DMA((count, chunks))]
         self.space, self.out_space = pl.ANY, pl.ANY
         self.reach = "box"
@@ -223,7 +219,7 @@
 class GatherAll:
     def __init__(self, count, value):
         self.count = count
-        self.out = jax.ShapeDtypeStruct((count, 2) + value.shape, value.dtype)
+        self.taken, self.outs = 1, [jax.ShapeDtypeStruct((count, 2) + value.shape, value.dtype)]
         self.scratch = [DMA, DMA((count, 2)), DMA((count, 2))]
         self.space, self.out_space = pl.ANY, pl.ANY
         self.reach = "box+half"
@@ -313,7 +309,7 @@
         self.pick = pick or (lambda me, to: to)
         self.place = place or (lambda me, to: me)
         shape = value.shape[:1] + ((2,) if both else ()) + value.shape[1:]
-        self.out = jax.ShapeDtypeStruct(shape, value.dtype)
+        self.taken, self.outs = 1, [jax.ShapeDtypeStruct(shape, value.dtype)]
         self.scratch = [DMA, DMA((count, 2)), DMA((count, 2))]
         self.space, self.out_space = pl.ANY, pl.ANY
         self.reach = "all+half" if both else "all"
@@ -389,13 +385,76 @@
         self.own.wait()
 
 
+class DealSum:
+    def __init__(self, count, value):
+        self.count = count
+        shape = value.shape[:1] + value.shape[2:]
+        self.taken, self.outs = 1, [jax.ShapeDtypeStruct(shape, value.dtype)]
+        self.scratch = [pltpu.VMEM(shape, value.dtype), pltpu.VMEM(shape, value.dtype)]
+        self.scratch += [DMA, DMA((count, 2)), DMA((count, 2))]
+        self.space, self.out_space = pltpu.VMEM, pl.ANY
+        self.reach = "all+half"
+
+    def bind(self, me, half, x_ref, out_ref, landed, total, own_sem, send_sem, recv_sem):
+        self.me, self.half, self.x, self.o = me, half, x_ref, out_ref
+        self.landed, self.total = landed, total
+        self.send, self.recv = send_sem, recv_sem
+        self.own = pltpu.make_async_copy(total.at[me], out_ref.at[me], own_sem)
+        self.sent = []
+
+    def cross(self, part):
+        return remote(
+            self.x.at[part, 1 - self.half], self.landed.at[part], self.send.at[part, 1],
+            self.recv.at[part, 1], "fsdp", 1 - self.half,
+        )
+
+    def copy(self, by):
+        to = (self.me + by) % self.count
+        return remote(
+            self.total.at[to], self.o.at[self.me], self.send.at[by, 0], self.recv.at[by, 0],
+            "ctx", to,
+        )
+
+    def start(self):
+        for part in range(self.count):
+            copy = self.cross(part)
+            copy.start()
+            self.sent.append(copy)
+
+    def add(self):
+        for part in range(self.count):
+            self.cross(part).wait_recv()
+            mine = self.x[part, self.half].astype(F32) + self.landed[part].astype(F32)
+            self.total[part] = mine.astype(self.total.dtype)
+        self.own.start()
+        for by in range(1, self.count):
+            copy = self.copy(by)
+            copy.start()
+            self.sent.append(copy)
+
+    def steps(self):
+        return [self.add]
+
+    def finish(self):
+        for by in range(1, self.count):
+            source = (self.me + self.count - by) % self.count
+            slot = self.o.at[source]
+            remote(
+                slot, slot, self.send.at[by, 0], self.recv.at[by, 0], "ctx",
+                (self.me + by) % self.count,
+            ).wait_recv()
+        for copy in self.sent:
+            copy.wait_send()
+        self.own.wait()
+
+
 class Scatter:
     def __init__(self, count, value, chunks, both=False):
         self.count, self.chunks, self.both = count, chunks, both
-        tail = value.shape[1:]
-        self.out = jax.ShapeDtypeStruct(tail, F32)
+        tail = value.shape[2:] if both else value.shape[1:]
+        self.taken, self.outs = 1, [jax.ShapeDtypeStruct(tail, F32)]
         dims = sides(count, both)
-        blocks = value.shape[0]
+        blocks = count * 2 if both else count
         self.scratch = [
             pltpu.VMEM(((side - 1) * held,) + tail, value.dtype) for _, side, _, held in dims
         ]
@@ -406,7 +465,7 @@
 
     def bind(self, me, half, x_ref, out_ref, *scratch):
         self.me, self.half, self.o = me, half, out_ref
-        self.blocks = x_ref.shape[0]
+        self.blocks = self.count * 2 if self.both else self.count
         self.dims = sides(self.count, self.both)
         levels = len(self.dims)
         self.landed = scratch[:levels]
@@ -423,7 +482,7 @@
         part = self.part(chunk)
         here = self.me if axis == "ctx" else self.half
         return remote(
-            self.held[dim].at[block, part],
+            self.held[dim].at[self.at(dim, block) + (part,)],
             self.landed[dim].at[block - held, part],
             self.send.at[block, chunk],
             self.recv.at[block, chunk],
@@ -431,6 +490,14 @@
             moved(here, side, stride, -(block // held)),
         )
 
+    def at(self, dim, block):
+        if not self.both or dim < len(self.dims) - 1:
+            return (block,)
+        owner = self.me
+        for _, side, stride, held in self.dims[1:]:
+            owner = moved(owner, side, stride, -(block // held % side))
+        return (owner, self.half if block % 2 == 0 else 1 - self.half)
+
     def ready(self, dim, block, chunk):
         if block >= self.dims[dim][3]:
             copy = self.copy(dim, block, chunk)
@@ -441,7 +508,7 @@
         _, side, _, held = self.dims[dim]
         part = self.part(chunk)
         for block in reversed(range(held)):
-            total = self.held[dim][block, part].astype(F32)
+            total = self.held[dim][self.at(dim, block) + (part,)].astype(F32)
             for by in range(1, side):
                 self.copy(dim, by * held + block, chunk).wait_recv()
                 total = total + self.landed[dim][(by - 1) * held + block, part].astype(F32)
@@ -471,10 +538,69 @@
             copy.wait_send()
 
 
-def exchange_kernel(count, plans, early, *refs):
+class Products:
+    def __init__(self, values, pairs):
+        self.values, self.pairs = values, pairs
+        self.taken = len(values)
+        self.outs = [
+            jax.ShapeDtypeStruct((values[a].shape[1], values[b].shape[1]), BF) for a, b in pairs
+        ]
+        widest = max(out.shape[1] for out in self.outs)
+        self.scratch = [pltpu.VMEM(v.shape, v.dtype) for v in values]
+        self.scratch += [pltpu.VMEM((2, TILE, widest), BF), DMA((len(values),)), DMA((2,))]
+        self.space, self.out_space = pl.ANY, pl.ANY
+        self.reach = ""
+
+    def bind(self, me, half, *refs):
+        n, m = len(self.values), len(self.pairs)
+        self.held = refs[n + m : n + m + n]
+        self.tile, self.in_sem, self.out_sem = refs[n + m + n :]
+        self.o = refs[n : n + m]
+        self.loads = [
+            pltpu.make_async_copy(refs[i], self.held[i], self.in_sem.at[i]) for i in range(n)
+        ]
+        self.stores = []
+        self.loaded = set()
+
+    def start(self):
+        for load in self.loads:
+            load.start()
+
+    def step(self, pair, row):
+        for i in self.pairs[pair]:
+            if i not in self.loaded:
+                self.loads[i].wait()
+                self.loaded.add(i)
+        left, right = (self.held[i] for i in self.pairs[pair])
+        slot = len(self.stores) % 2
+        if len(self.stores) >= 2:
+            self.stores[-2].wait()
+        part = pl.ds(row * TILE, TILE)
+        out = self.o[pair]
+        place = self.tile.at[slot, :, pl.ds(0, out.shape[1])]
+        place[...] = leading_contraction(left[:, part], right[...]).astype(BF)
+        store = pltpu.make_async_copy(place, out.at[part], self.out_sem.at[slot])
+        store.start()
+        self.stores.append(store)
+
+    def steps(self):
+        return [
+            functools.partial(self.step, pair, row)
+            for pair in range(len(self.pairs))
+            for row in range(self.outs[pair].shape[0] // TILE)
+        ]
+
+    def finish(self):
+        for store in self.stores[-2:]:
+            store.wait()
+
+
+def exchange_kernel(count, plans, spans, needed, carried, *refs):
     me, half = lax.axis_index("ctx"), lax.axis_index("fsdp")
-    ins, refs = refs[: len(plans)], refs[len(plans) :]
-    outs, refs = refs[: len(plans)], refs[len(plans) :]
+    taken = sum(plan.taken for plan in plans)
+    ins, refs = refs[:taken], refs[taken + needed + carried :]
+    given = sum(len(plan.outs) for plan in plans)
+    outs, refs = refs[:given], refs[given + carried :]
     barrier = pltpu.get_barrier_semaphore()
     peers = []
     if any("all" in plan.reach for plan in plans):
@@ -487,39 +613,448 @@
     for axis, target in peers:
         pl.semaphore_signal(barrier, inc=1, device_id={axis: target}, device_id_type=MESH)
     pl.semaphore_wait(barrier, len(peers))
-    for plan, x_ref, out_ref in zip(plans, ins, outs):
+    for plan in plans:
         mine, refs = refs[: len(plan.scratch)], refs[len(plan.scratch) :]
-        plan.bind(me, half, x_ref, out_ref, *mine)
+        plan.bind(me, half, *ins[: plan.taken], *outs[: len(plan.outs)], *mine)
+        ins, outs = ins[plan.taken :], outs[len(plan.outs) :]
         plan.start()
-    for plan in plans[:early]:
-        for step in plan.steps():
-            step()
-    queues = [plan.steps() for plan in plans[early:]]
-    longest = max(len(queue) for queue in queues)
-    done = [0] * len(queues)
-    for turn in range(longest):
-        for i, queue in enumerate(queues):
-            upto = (turn + 1) * len(queue) // longest
-            for step in queue[done[i] : upto]:
-                step()
-            done[i] = upto
+    timed = []
+    for plan, (first, last) in zip(plans, spans):
+        steps = plan.steps()
+        for i, step in enumerate(steps):
+            timed.append((first + (last - first) * (i + 1) / len(steps), step))
+    for _, step in sorted(timed, key=lambda entry: entry[0]):
+        step()
     for plan in plans:
         plan.finish()
 
 
-def exchange(count, collective, values, plans, early=0):
+def exchange(count, collective, values, plans, spans=None, needs=(), carry=()):
+    spans = spans or [(0.0, 1.0)] * len(plans)
     scratch = [ref for plan in plans for ref in plan.scratch]
+    values = [v for value in values for v in (value if isinstance(value, list) else [value])]
+    outs = [out for plan in plans for out in plan.outs]
+    first = len(values) + len(needs)
+    spot = pl.BlockSpec(memory_space=pl.ANY)
+    in_specs = [pl.BlockSpec(memory_space=p.space) for p in plans for _ in range(p.taken)]
+    out_specs = [pl.BlockSpec(memory_space=p.out_space) for p in plans for _ in p.outs]
     return pl.pallas_call(
-        functools.partial(exchange_kernel, count, plans, early),
-        out_shape=tuple(plan.out for plan in plans),
-        in_specs=[pl.BlockSpec(memory_space=plan.space) for plan in plans],
-        out_specs=tuple(pl.BlockSpec(memory_space=plan.out_space) for plan in plans),
+        functools.partial(exchange_kernel, count, plans, spans, len(needs), len(carry)),
+        out_shape=tuple(outs) + tuple(jax.ShapeDtypeStruct(v.shape, v.dtype) for v in carry),
+        in_specs=in_specs + [spot] * (len(needs) + len(carry)),
+        out_specs=tuple(out_specs + [spot] * len(carry)),
+        input_output_aliases={first + i: len(outs) + i for i in range(len(carry))},
         scratch_shapes=scratch,
         compiler_params=pltpu.CompilerParams(
-            collective_id=collective, has_side_effects=True, vmem_limit_bytes=56 << 20
+            collective_id=collective, has_side_effects=True, vmem_limit_bytes=60 << 20
         ),
         cost_estimate=pl.CostEstimate(flops=0, bytes_accessed=100 << 20, transcendentals=0),
-    )(*values)
+    )(*values, *needs, *carry)
+
+
+TILE = 256
+
+
+def hot_rows(slots, first):
+    count = slots.shape[1]
+    return (lax.broadcasted_iota(jnp.int32, (TILE, count), 0) + first == slots).astype(BF)
+
+
+def hot_cols(slots, first):
+    count = slots.shape[0]
+    return (lax.broadcasted_iota(jnp.int32, (count, TILE), 1) + first == slots).astype(BF)
+
+
+def meets(starts, tokens, slots):
+    return (starts[tokens] < (slots + 1) * TILE) & (starts[tokens + 1] > slots * TILE)
+
+
+def split_of(info, width):
+    own = pl.multiple_of(info * (width // 2), 128)
+    other = pl.multiple_of((1 - info) * (width // 2), 128)
+    return pl.ds(own, width // 2), pl.ds(other, width // 2)
+
+
+def pick_rows(starts, slot_ref, source_ref, total_ref, tile):
+    total_ref[...] = jnp.zeros_like(total_ref)
+    for j in range(source_ref.shape[0] // TILE):
+
+        @pl.when(meets(starts, j, tile))
+        def _():
+            part = pl.ds(j * TILE, TILE)
+            total_ref[...] += matmul(hot_rows(slot_ref[:, part], tile * TILE), source_ref[part])
+
+
+def expert_in_kernel(info, starts, slot, two, g0, u0, rows, gate, up, hidden, total):
+    pick_rows(starts, slot, two, total, pl.program_id(0))
+    rows[...] = total[...].astype(BF)
+    gate[...] = matmul(rows[...], g0[...])
+    up[...] = matmul(rows[...], u0[...])
+    value = gate[...]
+    hidden[...] = (value / (1.0 + jnp.exp(-value)) * up[...]).astype(BF)
+
+
+def expert_out_kernel(
+    info, starts, hidden, d0, d1, slot, weight, shared, sdown, produced, out, held, total
+):
+    step, tiles = pl.program_id(0), held.shape[0] // TILE
+
+    @pl.when(step < tiles)
+    def _():
+        own, other = split_of(info[0], held.shape[1])
+        produced[:, own] = contract_last(hidden[...], d0[...]).astype(BF)
+        produced[:, other] = contract_last(hidden[...], d1[...]).astype(BF)
+        held[pl.ds(pl.multiple_of(step * TILE, TILE), TILE)] = produced[...]
+
+    @pl.when(step >= tiles)
+    def _():
+        token = step - tiles
+        total[...] = jnp.zeros_like(total)
+        for i in range(tiles):
+
+            @pl.when(meets(starts, token, i))
+            def _():
+                total[...] += matmul(hot_cols(slot[...], i * TILE), held[pl.ds(i * TILE, TILE)])
+
+        out[...] = (weight[...] * total[...] + contract_last(shared[...], sdown[...])).astype(BF)
+
+
+def expert_back_kernel(
+    info, starts, slot, weight, cot, produced, gate, up, g0, u0, d0, d1,
+    grad_in, grad_gate, grad_up, grad_rows, dots, total,
+):
+    tile = pl.program_id(0)
+    total[...] = jnp.zeros_like(total)
+    dots[...] = jnp.zeros_like(dots)
+    for j in range(cot.shape[0] // TILE):
+
+        @pl.when(meets(starts, j, tile))
+        def _():
+            part = pl.ds(j * TILE, TILE)
+            hot = hot_rows(slot[:, part], tile * TILE)
+            total[...] += matmul(hot, cot[part])
+            dots[...] += jnp.sum(hot.astype(F32) * weight[:, part], 1, keepdims=True)
+
+    grad_in[...] = (dots[...] * total[...]).astype(BF)
+    dots[...] = jnp.sum(total[...] * produced[...].astype(F32), 1, keepdims=True)
+    own, other = split_of(info[0], grad_in.shape[1])
+    grad_hidden = matmul(grad_in[:, own], d0[...]) + matmul(grad_in[:, other], d1[...])
+    act, slope = swiglu_parts(gate[...], up[...])
+    grad_gate[...] = (grad_hidden * up[...] * slope).astype(BF)
+    grad_up[...] = (grad_hidden * act).astype(BF)
+    back = contract_last(grad_gate[...], g0[...]) + contract_last(grad_up[...], u0[...])
+    grad_rows[...] = back.astype(BF)
+
+
+def shared_in_kernel(two, sgate, sup, gate, up, hidden):
+    gate[...] = matmul(two[...], sgate[...])
+    up[...] = matmul(two[...], sup[...])
+    value = gate[...]
+    hidden[...] = (value / (1.0 + jnp.exp(-value)) * up[...]).astype(BF)
+
+
+def tokens_back_kernel(
+    info, starts, slot, dots, grad_rows, cot, gate, up, sgate, sup, sdown,
+    out, grad_gate, grad_up, gates, total,
+):
+    token = pl.program_id(0)
+    grad_hidden = matmul(cot[...], sdown[...])
+    act, slope = swiglu_parts(gate[...], up[...])
+    grad_gate[...] = (grad_hidden * up[...] * slope).astype(BF)
+    grad_up[...] = (grad_hidden * act).astype(BF)
+    total[...] = contract_last(grad_gate[...], sgate[...]) + contract_last(grad_up[...], sup[...])
+    gates[...] = jnp.zeros_like(gates)
+    mine = lax.broadcasted_iota(jnp.int32, gates.shape, 1) == info[1]
+    for i in range(grad_rows.shape[0] // TILE):
+
+        @pl.when(meets(starts, token, i))
+        def _():
+            part = pl.ds(i * TILE, TILE)
+            hot = hot_cols(slot[...], i * TILE)
+            total[...] += matmul(hot, grad_rows[part])
+            found = jnp.sum(hot.astype(F32) * dots[:, part], 1, keepdims=True)
+            gates[...] += jnp.where(mine, found, 0.0)
+
+    out[...] = total[...].astype(BF)
+
+
+def whole(value):
+    return pl.BlockSpec(value.shape, lambda *_: (0,) * value.ndim, pipeline_mode=pl.Buffered(1))
+
+
+def tiled(value, index=lambda step: step):
+    return pl.BlockSpec((TILE,) + value.shape[1:], lambda step, *_: (index(step), 0))
+
+
+def run(kernel, steps, scalars, values, specs, outs, out_specs, scratch, flops, needs=(), carry=()):
+    moved_bytes = sum(v.size * v.dtype.itemsize for v in list(values) + list(outs))
+    first = len(scalars) + len(values)
+    fenced = first + len(needs) + len(carry)
+
+    def body(*refs):
+        made = refs[fenced : fenced + len(outs)]
+        kernel(*refs[:first], *made, *refs[fenced + len(outs) + len(carry) :])
+
+    spot = pl.BlockSpec(memory_space=pl.ANY)
+    specs = list(specs) + [spot] * (len(needs) + len(carry))
+    out_specs = tuple(out_specs) + (spot,) * len(carry)
+    handed = tuple(jax.ShapeDtypeStruct(v.shape, v.dtype) for v in carry)
+    return pl.pallas_call(
+        body,
+        grid_spec=pltpu.PrefetchScalarGridSpec(
+            num_scalar_prefetch=len(scalars),
+            grid=(steps,),
+            in_specs=specs,
+            out_specs=out_specs,
+            scratch_shapes=scratch,
+        ),
+        out_shape=tuple(outs) + handed,
+        input_output_aliases={first + len(needs) + i: len(outs) + i for i in range(len(carry))},
+        compiler_params=pltpu.CompilerParams(vmem_limit_bytes=60 << 20),
+        cost_estimate=pl.CostEstimate(flops=flops, bytes_accessed=moved_bytes, transcendentals=0),
+    )(*scalars, *values, *needs, *carry)
+
+
+def like(rows, columns, dtype):
+    return jax.ShapeDtypeStruct((rows, columns), dtype)
+
+
+def expert_in(info, starts, slot_row, two, gates, ups, carry):
+    capacity, width, hidden = slot_row[1], two.shape[1], gates.shape[1]
+    slot_row = slot_row[0]
+    outs = (
+        like(capacity, width, BF),
+        like(capacity, hidden, F32),
+        like(capacity, hidden, F32),
+        like(capacity, hidden, BF),
+    )
+    values = [slot_row, two, gates, ups]
+    return run(
+        expert_in_kernel, capacity // TILE, (info, starts), values, [whole(v) for v in values],
+        outs, tuple(tiled(o) for o in outs), [pltpu.VMEM((TILE, width), F32)],
+        capacity * width * hidden * 4,
+        carry=carry,
+    )
+
+
+def expert_out(info, starts, hidden, downs, slot_col, weight_col, shared, sdown, needs):
+    capacity, tokens, width = hidden.shape[0], slot_col.shape[0], sdown.shape[0]
+    first = capacity // TILE
+    outs = (like(capacity, width, BF), like(tokens, width, BF))
+    rows_at = lambda step: jnp.minimum(step, first - 1)
+    tokens_at = lambda step: jnp.maximum(step - first, 0)
+    values = [hidden, *downs, slot_col, weight_col, shared, sdown]
+    specs = [tiled(hidden, rows_at), whole(downs[0]), whole(downs[1])]
+    specs += [tiled(slot_col, tokens_at), tiled(weight_col, tokens_at), tiled(shared, tokens_at)]
+    specs += [whole(sdown)]
+    return run(
+        expert_out_kernel, first + tokens // TILE, (info, starts), values, specs, outs,
+        (tiled(outs[0], rows_at), tiled(outs[1], tokens_at)),
+        [pltpu.VMEM((capacity, width), BF), pltpu.VMEM((TILE, width), F32)],
+        capacity * width * hidden.shape[1] * 3,
+        needs,
+    )
+
+
+def expert_back(
+    info, starts, slot_row, weight_row, cot, produced, gate, up, gates, ups, downs, needs
+):
+    capacity, hidden = gate.shape
+    width = cot.shape[1]
+    outs = (
+        like(capacity, width, BF),
+        like(capacity, hidden, BF),
+        like(capacity, hidden, BF),
+        like(capacity, width, BF),
+        like(capacity, 1, F32),
+    )
+    values = [slot_row, weight_row, cot, produced, gate, up, gates, ups, *downs]
+    specs = [whole(v) for v in values]
+    specs[3:6] = [tiled(produced), tiled(gate), tiled(up)]
+    return run(
+        expert_back_kernel, capacity // TILE, (info, starts), values, specs, outs,
+        tuple(tiled(o) for o in outs), [pltpu.VMEM((TILE, width), F32)],
+        capacity * width * hidden * 6,
+        needs,
+    )
+
+
+def shared_in(two, sgate, sup):
+    tokens, hidden = two.shape[0], sgate.shape[1]
+    outs = (like(tokens, hidden, F32), like(tokens, hidden, F32), like(tokens, hidden, BF))
+    return run(
+        shared_in_kernel, tokens // TILE, (), [two, sgate, sup],
+        [tiled(two), whole(sgate), whole(sup)], outs, tuple(tiled(o) for o in outs), [],
+        tokens * two.shape[1] * hidden * 4,
+    )
+
+
+def tokens_back(info, starts, slot_col, dots_row, grad_rows, cot, gate, up, sgate, sup, sdown, experts):
+    tokens, width = cot.shape
+    hidden = gate.shape[1]
+    outs = (
+        like(tokens, width, BF),
+        like(tokens, hidden, BF),
+        like(tokens, hidden, BF),
+        like(tokens, experts, F32),
+    )
+    values = [slot_col, dots_row, grad_rows, cot, gate, up, sgate, sup, sdown]
+    specs = [whole(v) for v in values]
+    specs[0] = tiled(slot_col)
+    specs[3:6] = [tiled(cot), tiled(gate), tiled(up)]
+    return run(
+        tokens_back_kernel, tokens // TILE, (info, starts), values, specs, outs,
+        tuple(tiled(o) for o in outs), [pltpu.VMEM((TILE, width), F32)],
+        tokens * width * hidden * 8,
+    )
+
+
+def columns_kernel(rest, query, expand, d_query, d_output, d_gate, d_up, d_down, d_expand):
+    parts = rest.shape[0]
+    fs = d_gate.shape[1] // parts
+    for part in range(parts):
+        for i, out in enumerate((d_gate, d_up, d_down)):
+            block = rest[part, :, i * fs : (i + 1) * fs]
+            out[:, part * fs : (part + 1) * fs] = block.astype(F32)
+        width = NOPE + ROPE
+        d_query[:, part * width : (part + 1) * width] = query[part, :, :width].astype(F32)
+        block = query[part, :, width : width + VDIM]
+        d_output[:, part * VDIM : (part + 1) * VDIM] = block.astype(F32)
+        width = NOPE + VDIM
+        d_expand[:, part * width : (part + 1) * width] = expand[part].astype(F32)
+
+
+def columns_of(rest, query, expand, fs):
+    count, shard = query.shape[:2]
+    outs = (
+        like(shard, count * (NOPE + ROPE), F32),
+        like(shard, count * VDIM, F32),
+        like(shard, count * fs, F32),
+        like(shard, count * fs, F32),
+        like(shard, count * fs, F32),
+        like(expand.shape[1], count * (NOPE + VDIM), F32),
+    )
+    values = [rest, query, expand]
+    specs = [whole(v) for v in values]
+    return run(
+        columns_kernel, 1, (), values, specs, outs, tuple(whole(o) for o in outs), [], 0
+    )
+
+
+def turned(value, cosine, sine):
+    half = value.shape[1] // 2
+    return value * cosine + jnp.concatenate([value[:, half:], value[:, :half]], 1) * sine
+
+
+def before_kernel(
+    token, gain, gain_latent, wq, wc, we, cosine, sine, normed, query, keys, values, latent, low
+):
+    hidden = token[...].astype(F32)
+    normed[...] = (hidden * norm_scale(hidden) * gain[...]).astype(BF)
+    raw = matmul(normed[...], wq[...])
+    query[:, :NOPE] = raw[:, :NOPE].astype(BF)
+    query[:, NOPE:] = turned(raw[:, NOPE:], cosine[...], sine[...]).astype(BF)
+    compressed = matmul(normed[...], wc[...])
+    low[...] = compressed[:, :LATENT]
+    part = low[...]
+    latent[...] = (part * norm_scale(part) * gain_latent[...]).astype(BF)
+    expanded = matmul(latent[...], we[...])
+    keys[:, :NOPE] = expanded[:, :NOPE].astype(BF)
+    rope = compressed[:, LATENT : LATENT + ROPE]
+    keys[:, NOPE:] = turned(rope, cosine[...], sine[...]).astype(BF)
+    values[...] = expanded[:, NOPE:].astype(BF)
+
+
+def before_attention(token, gain, gain_latent, wq, wc, we, cosine, sine):
+    tokens, width = token.shape
+    outs = (
+        like(tokens, width, BF),
+        like(tokens, NOPE + ROPE, BF),
+        like(tokens, NOPE + ROPE, BF),
+        like(tokens, VDIM, BF),
+        like(tokens, LATENT, BF),
+        like(tokens, LATENT, F32),
+    )
+    values = [token, gain, gain_latent, wq, wc, we, cosine, sine]
+    specs = [whole(v) for v in values]
+    specs[0], specs[6], specs[7] = tiled(token), tiled(cosine), tiled(sine)
+    return run(
+        before_kernel, tokens // TILE, (), values, specs, outs, tuple(tiled(o) for o in outs), [],
+        tokens * width * 2000,
+    )
+
+
+def behind_kernel(
+    gq, gk, gv, normed, latent, low, gain_latent, latent_col, gain_col, wq, wc, we, cosine, sine,
+    extra, out, d_query, d_small, d_expand, d_latent, sum_q, sum_c, sum_e,
+):
+    step = pl.program_id(0)
+
+    @pl.when(step == 0)
+    def _():
+        sum_q[...] = jnp.zeros_like(sum_q)
+        sum_c[...] = jnp.zeros_like(sum_c)
+        sum_e[...] = jnp.zeros_like(sum_e)
+
+    scale = (NOPE + ROPE) ** (-0.5)
+    query, keys = gq[...] * scale, gk[...] * scale
+    back = -sine[...]
+    grad_q = jnp.concatenate(
+        [query[:, :NOPE], turned(query[:, NOPE:], cosine[...], back)], 1
+    ).astype(BF)
+    grad_e = jnp.concatenate([keys[:, :NOPE], gv[...]], 1).astype(BF)
+    grad_latent = contract_last(grad_e, we[...])
+    part = low[...]
+    grad_low = norm_back(part, norm_scale(part), gain_latent[...], grad_latent)
+    rope = turned(keys[:, NOPE:], cosine[...], back)
+    fill = jnp.zeros((rope.shape[0], wc.shape[1] - LATENT - ROPE), F32)
+    grad_c = jnp.concatenate([grad_low, rope, fill], 1).astype(BF)
+    out[...] = (contract_last(grad_q, wq[...]) + contract_last(grad_c, wc[...])).astype(BF)
+    sum_q[...] += leading_contraction(normed[...], grad_q)
+    sum_c[...] += leading_contraction(normed[...], grad_c)
+    sum_e[...] += leading_contraction(latent[...], grad_e)
+
+    @pl.when(step == pl.num_programs(0) - 1)
+    def _():
+        first = jnp.sum(sum_q[...] * wq[...].astype(F32), 1, keepdims=True)
+        first = first + jnp.sum(sum_c[...] * wc[...].astype(F32), 1, keepdims=True)
+        d_query[...] = sum_q[...].astype(BF)
+        edge = LATENT + ROPE
+        lanes = lax.broadcasted_iota(jnp.int32, extra.shape, 1)
+        more = extra[...] + jnp.where(lanes == 0, first / gain_col[...], 0.0)
+        d_small[:, :edge] = sum_c[:, :edge].astype(BF)
+        d_small[:, edge:] = more.astype(BF)
+        d_expand[...] = sum_e[...].astype(BF)
+        second = jnp.sum(sum_e[...] * we[...].astype(F32), 1, keepdims=True) / latent_col[...]
+        d_latent[...] = second
+
+
+def behind_attention(
+    gq, gk, gv, normed, latent, low, gain_latent, gain_col, wq, wc, we, cosine, sine, extra, needs
+):
+    tokens, width = normed.shape
+    outs = (
+        like(tokens, width, BF),
+        like(width, wq.shape[1], BF),
+        like(width, wc.shape[1], BF),
+        like(LATENT, we.shape[1], BF),
+        like(LATENT, 1, F32),
+    )
+    values = [gq, gk, gv, normed, latent, low]
+    values += [gain_latent, gain_latent.reshape(-1, 1), gain_col, wq, wc, we, cosine, sine, extra]
+    specs = [tiled(v) for v in values[:6]] + [whole(v) for v in values[6:]]
+    specs[12], specs[13] = tiled(cosine), tiled(sine)
+    return run(
+        behind_kernel, tokens // TILE, (), values, specs, outs,
+        (tiled(outs[0]),) + tuple(whole(o) for o in outs[1:]),
+        [
+            pltpu.VMEM((width, wq.shape[1]), F32),
+            pltpu.VMEM((width, wc.shape[1]), F32),
+            pltpu.VMEM((LATENT, we.shape[1]), F32),
+        ],
+        tokens * width * 4000,
+        needs,
+    )
 
 
 def placement(lengths_row, order_row):
@@ -580,32 +1115,20 @@
     all_devices = count * lax.axis_size("fsdp")
 
     half = lax.axis_index("fsdp")
-    small_vmem = count * rows * D * 2 <= 12 << 20
-
-    def reduce_blocks(collective, value, *more):
-        if small_vmem:
-            plans = [plan for _, plan in more] + [Scatter(count, value, 4)]
-            got = exchange(count, collective, [v for v, _ in more] + [value], plans)
-            return (got[-1],) + tuple(got[:-1])
-        rest = exchange(count, collective, [v for v, _ in more], [p for _, p in more]) if more else ()
-        return (box.scatter(value)[0],) + tuple(rest)
+
+    def reduce_blocks(collective, value, more, needs=(), carry=()):
+        plans = [Scatter(count, value, 4)] + [plan for _, plan, _ in more]
+        spans = [(0.0, 1.0)] + [span for _, _, span in more]
+        values = [value] + [v for v, _, _ in more]
+        return exchange(count, collective, values, plans, spans, needs, carry)
 
     def across(value):
         return lax.ppermute(value, "fsdp", [(0, 1), (1, 0)])
-
-    def both_halves(value):
-        other = across(value)
-        first, second = jnp.where(half == 0, value, other), jnp.where(half == 0, other, value)
-        return jnp.stack([first, second], 1)
 
     def halves_sent(parts):
         own = lax.dynamic_index_in_dim(parts, half, 1, keepdims=False)
         other = lax.dynamic_index_in_dim(parts, 1 - half, 1, keepdims=False)
         return own, across(other.astype(BF))
-
-    def halves_summed(parts):
-        own, got = halves_sent(parts)
-        return own.astype(F32) + got.astype(F32)
 
     owners = box.owners()
 
@@ -614,9 +1137,9 @@
     small = jnp.concatenate(
         [
             compress_weight,
-            router_weight,
             first_gain[:, None],
             second_gain[:, None],
+            router_weight,
             jnp.pad(latent_gain, (0, shard - lat_rows))[:, None],
         ],
         1,
@@ -625,8 +1148,8 @@
     query_parts = spread(query_weight, count, repeat)
     expand_parts = spread(expand_weight, count, repeat)
     small_all = lax.all_gather(small, both, axis=0, tiled=True)
-    gate_expert = lax.all_gather(expert_gate[0].astype(BF), "fsdp", axis=0, tiled=True)
-    query_own, expand_own, token_all = exchange(
+    gates = lax.all_gather(expert_gate[0].astype(BF), "fsdp", axis=0, tiled=True)
+    query_own, expand_own, token_all, cot_low = exchange(
         count,
         0,
         [query_parts, expand_parts, tokens[0]],
@@ -635,65 +1158,48 @@
             Deal(count, expand_parts, both=True),
             Gather(count, tokens[0], 4),
         ],
-        early=2,
+        spans=[(-2, -1), (-1, 0), (0, 1)],
+        carry=[cotangent[0].astype(BF)],
     )
     token_all = token_all.reshape(group, D)
     query_own = query_own.reshape(D, -1)
     expand_own = expand_own.reshape(LATENT, -1)
     edge = compress_weight.shape[1]
     compress_full = small_all[:, :edge]
-    router_full = small_all[:, edge : edge + experts]
-    gain_first = small_all[:, edge + experts].astype(F32)
-    gain_second = small_all[:, edge + experts + 1].astype(F32)
+    router_full = small_all[:, edge + 2 : edge + 2 + experts]
+    gain_first = small_all[:, edge].astype(F32)
+    gain_second = small_all[:, edge + 1].astype(F32)
     gain_latent = small_all[:, edge + experts + 2].reshape(all_devices, shard)[:, :lat_rows]
     gain_latent = gain_latent.reshape(-1).astype(F32)
 
-    output_cast, up_cast, down_cast = after(
-        token_all, output_weight, expert_up[0], expert_down[0]
-    )
+    output_cast = output_weight
     output_full = lax.all_gather(output_cast.astype(BF), both, axis=0, tiled=True)
-    up_expert = lax.all_gather(up_cast.astype(BF), "fsdp", axis=0, tiled=True)
-    down_expert = lax.all_gather(down_cast.astype(BF), "fsdp", axis=0, tiled=True)
-
-    cot_low, route_own, gate_cols, up_cols, down_cols = after(
-        token_all, cotangent[0].astype(BF), routes[0], shared_gate, shared_up, shared_down
-    )
+    route_own, gate_cols, up_cols, down_cols = routes[0], shared_gate, shared_up, shared_down
     fs = shared_gate.shape[1] // count
     fp = up_to(fs)
     rest = jnp.concatenate(
         [spread(gate_cols, count, 1), spread(up_cols, count, 1), spread(down_cols, count, 1)], -1
     )
     rest = pad_last(rest, up_to(3 * fs))
-    rest = lax.all_to_all(rest, "ctx", split_axis=0, concat_axis=0, tiled=True)
+    cot_parts = box.spread(cot_low, 0)
+
     order_all = jnp.take(token_order[0].reshape(count, rows), owners, axis=0).reshape(-1)
     sequence, position = placement(lengths[0], order_all)
     turns = ROPE // 2
     freq = 10000.0 ** (-jnp.arange(turns, dtype=F32) / turns)
     angle = position.astype(F32)[:, None] * freq[None, :]
-    cosine, sine = jnp.cos(angle), jnp.sin(angle)
-
-    hidden_all = token_all.astype(F32)
-    normed_all = (hidden_all * norm_scale(hidden_all) * gain_first).astype(BF)
-    query_raw = matmul(normed_all[:asked], query_own)
-    query = jnp.concatenate(
-        [query_raw[:, :NOPE], turn(query_raw[:, NOPE:], cosine[:asked], sine[:asked])], -1
-    ).astype(BF)
-    compressed = matmul(normed_all, compress_full)
-    compressed, rest = meet(compressed, rest)
-    rest = both_halves(rest).reshape(D, -1)
-    rest_own = rest
-    sgate_own = pad_last(rest_own[:, :fs], fp)
-    sup_own = pad_last(rest_own[:, fs : 2 * fs], fp)
-    sdown_own = pad_last(rest_own[:, 2 * fs : 3 * fs], fp)
-    low_part = compressed[:, :LATENT]
-    latent_scale = norm_scale(low_part)
-    latent = (low_part * latent_scale * gain_latent).astype(BF)
-    expanded = matmul(latent, expand_own)
-    keys = jnp.concatenate(
-        [expanded[:, :NOPE], turn(compressed[:, LATENT:], cosine, sine)], -1
-    ).astype(BF)
-    values = expanded[:, NOPE:].astype(BF)
-    keys, gate_expert = meet(keys, gate_expert)
+    cosine = jnp.tile(jnp.cos(angle), (1, 2))
+    sine = jnp.sin(angle)
+    sine = jnp.concatenate([-sine, sine], 1)
+
+    normed_all, query, keys, values, latent, low_part = before_attention(
+        token_all, gain_first[None, :], gain_latent[None, :], query_own, small_all, expand_own,
+        cosine, sine,
+    )
+    up_cast, down_cast = expert_up[0], expert_down[0]
+    ups = lax.all_gather(up_cast.astype(BF), "fsdp", axis=0, tiled=True)
+    down_own = down_cast.astype(BF)
+    downs = (down_own, across(down_own))
     scale = width ** (-0.5)
     visible = (sequence[:asked, None] == sequence[None, :]) & (
         position[None, :] <= position[:asked, None]
@@ -705,114 +1211,93 @@
     mixed_f = matmul(weights.astype(BF), values) / total
     logsum = peak + jnp.log(total)
 
-    def to_owner(value):
+    def to_owner(value, needs, carried):
         if repeat > 1:
             value = jnp.pad(value, ((0, group - asked), (0, 0)))
         value = value.reshape(count, rows, -1)
         plan = Deal(count, value, pick=lambda me, to: offset_of(count, me, to))
-        (got,) = exchange(count, 1, [value], [plan])
+        got, rest_own, carried = exchange(
+            count, 1, [value, rest], [plan, Deal(count, rest, both=True)],
+            spans=[(0, 1), (1, 2)], needs=needs, carry=[carried],
+        )
         if repeat > 1:
             got = jnp.sum(got.reshape(HEADS, repeat, rows, -1).astype(F32), 1).astype(BF)
-        return jnp.transpose(got, (1, 0, 2)).reshape(rows, -1)
-
-    def to_head(value):
-        value = jnp.transpose(value.reshape(rows, HEADS, -1), (1, 0, 2))
-        if repeat > 1:
-            value = jnp.repeat(value, repeat, 0)
-        plan = Deal(count, value, place=lambda me, to: offset_of(count, to, me))
-        (got,) = exchange(count, 4, [value], [plan])
-        return got.reshape(group, -1)[:asked]
-
-    mixed = to_owner(mixed_f.astype(BF))
+        return jnp.transpose(got, (1, 0, 2)).reshape(rows, -1), rest_own, carried
+
+    route_all = box.gather(route_own)
+    mine = jnp.any(route_all == me, -1)
+    capacity = rows * TOP * 4 // (3 * experts) * count
+    counted = jnp.cumsum(mine.astype(jnp.int32))
+    slot = jnp.where(mine, counted - 1, -1)
+    starts = jnp.concatenate([jnp.zeros((1,), jnp.int32), counted[TILE - 1 :: TILE]])
+    column = jnp.arange(experts, dtype=jnp.int32)[None, :] == me
+    info = jnp.stack([half, me]).astype(jnp.int32)
+    mixed, rest_own, cot_parts[0] = to_owner(mixed_f.astype(BF), [slot, gates], cot_parts[0])
+    cot_held = joined(cot_parts)
     hidden = tokens[0].astype(F32)
     residual = hidden + contract_last(mixed, output_full)
 
     residual_scale = norm_scale(residual)
     normed_two = (residual * residual_scale * gain_second).astype(BF)
-    (two_all,) = exchange(count, 2, [normed_two], [Gather(count, normed_two, 4)])
+    two_all, cot_held = exchange(
+        count, 2, [normed_two], [Gather(count, normed_two, 4)], carry=[cot_held]
+    )
     two_all = two_all.reshape(group, D)
-    route_all = box.gather(route_own)
-    two_all, up_expert, cot_low = meet(two_all, up_expert, cot_low)
-    cot_held = box.gather_step(cot_low, 0)
+    cot_parts = box.spread(cot_held, 1)
     probs_all = jax.nn.softmax(matmul(two_all, router_full), -1)
-    mine = jnp.any(route_all == me, -1)
-    capacity = rows * TOP * 4 // (3 * experts) * count
-    slot = jnp.where(mine, jnp.cumsum(mine.astype(jnp.int32)) - 1, -1)
-    slots = jnp.arange(capacity, dtype=jnp.int32)
-    chosen = slots[:, None] == slot[None, :]
-    pick = chosen.astype(BF)
-    column = jnp.arange(experts, dtype=jnp.int32)[None, :] == me
-    gate_tok = jnp.where(mine, jnp.sum(jnp.where(column, probs_all, 0.0), -1), 0.0)
-    gate_row = jnp.sum(jnp.where(chosen, gate_tok[None, :], 0.0), 1)
-    rows_in = matmul(pick, two_all).astype(BF)
-
-    gate_val = matmul(rows_in, gate_expert)
-    up_val = matmul(rows_in, up_expert)
-    gate_val, cot_held = meet(gate_val, cot_held)
-    for dim in range(1, len(box.dims) - 1):
-        cot_held = box.gather_step(cot_held, dim)
-    act, slope = swiglu_parts(gate_val, up_val)
-    expert_hidden = (act * up_val).astype(BF)
-    produced = contract_last(expert_hidden, down_expert).astype(BF)
-    sg = matmul(two_all, sgate_own)
-    su = matmul(two_all, sup_own)
-    sact, sslope = swiglu_parts(sg, su)
-    shared_hidden = (sact * su).astype(BF)
-    out_two = (
-        gate_tok[:, None] * leading_contraction(pick, produced)
-        + contract_last(shared_hidden, sdown_own)
-    ).astype(BF)
-
-    out_two, cot_held = meet(out_two, cot_held)
-    cot_all = box.gather_step(cot_held, len(box.dims) - 1)
-    out_held = box.scatter_step(out_two, len(box.dims) - 1)
-    cot_rows = matmul(pick, cot_all)
-    grad_in = (gate_row[:, None] * cot_rows).astype(BF)
-    grad_hidden = matmul(grad_in, down_expert)
-    grad_hidden, out_held = meet(grad_hidden, out_held)
-    for dim in reversed(range(1, len(box.dims) - 1)):
-        out_held = box.scatter_step(out_held, dim)
-    grad_eg = (grad_hidden * up_val * slope).astype(BF)
-    grad_eu = (grad_hidden * act).astype(BF)
-    grad_rows = (contract_last(grad_eg, gate_expert) + contract_last(grad_eu, up_expert)).astype(BF)
-    gg_row = jnp.sum(cot_rows * produced.astype(F32), -1)
-    gg_tok = jnp.sum(jnp.where(chosen, gg_row[:, None], 0.0), 0)
-    grad_sh = matmul(cot_all, sdown_own)
-    grad_sg = (grad_sh * su * sslope).astype(BF)
-    grad_su = (grad_sh * sact).astype(BF)
-    grad_two_part = (
-        leading_contraction(pick, grad_rows)
-        + contract_last(grad_sg, sgate_own)
-        + contract_last(grad_su, sup_own)
-    ).astype(BF)
-    gg_part = jnp.where(column, gg_tok[:, None], 0.0)
-    grad_two_part, out_held = meet(grad_two_part, out_held)
-    output = residual + box.scatter_step(out_held, 0)
-    d_gate = leading_contraction(rows_in, grad_eg).astype(BF)
-    d_up = leading_contraction(rows_in, grad_eu).astype(BF)
+    gate_col = jnp.sum(jnp.where(column & mine[:, None], probs_all, 0.0), -1, keepdims=True)
+    rows_in, gate_val, up_val, expert_hidden, cot_parts[0] = expert_in(
+        info, starts, (slot[None, :], capacity), two_all, gates, ups, [cot_parts[0]]
+    )
+    cot_held = joined(cot_parts)
+    cot_all = joined(box.spread(cot_held, 2))
+    rest_own = rest_own.reshape(D, -1)
+    sgate_own = pad_last(rest_own[:, :fs], fp)
+    sup_own = pad_last(rest_own[:, fs : 2 * fs], fp)
+    sdown_own = pad_last(rest_own[:, 2 * fs : 3 * fs], fp)
+    sg, su, shared_hidden = shared_in(two_all, sgate_own, sup_own)
+    produced, out_two = expert_out(
+        info, starts, expert_hidden, downs, slot[:, None], gate_col, shared_hidden, sdown_own,
+        [cot_held],
+    )
+
+    out_held = summed(box.share(out_two, 2), BF)
+    grad_in, grad_eg, grad_eu, grad_rows, dots = expert_back(
+        info, starts, slot[None, :], gate_col.reshape(1, group), cot_all, produced, gate_val, up_val,
+        gates, ups, downs, [out_held],
+    )
+    out_held = summed(box.share(out_held, 1), BF)
+    grad_two_part, grad_sg, grad_su, gg_part = tokens_back(
+        info, starts, slot[:, None], dots.reshape(1, capacity), grad_rows, cot_all, sg, su,
+        sgate_own, sup_own, sdown_own, experts,
+    )
+    d_rest = [
+        leading_contraction(two_all, grad_sg)[:, :fs],
+        leading_contraction(two_all, grad_su)[:, :fs],
+        leading_contraction(cot_all, shared_hidden)[:, :fs],
+    ]
+    d_rest = pad_last(jnp.concatenate(d_rest, 1).astype(BF), up_to(3 * fs))
+    d_rest = d_rest.reshape(count, 2, shard, -1)
+    rest_mine, rest_got = halves_sent(d_rest)
     d_down = leading_contraction(grad_in, expert_hidden).astype(BF)
+    products = Products(
+        [rows_in, grad_eg, grad_eu], [(0, 1), (0, 2)]
+    )
+    gg_part = gg_part.reshape(count, rows, -1)
+    grad_two, d_gate, d_up, grad_gates = reduce_blocks(
+        3,
+        grad_two_part.reshape(count, rows, D),
+        [
+            (products.values, products, (0.0, 1.0)),
+            (gg_part, Scatter(count, gg_part, 1), (0.3, 0.9)),
+        ],
+        [out_held, d_down],
+    )
+
     d_experts = [
         lax.psum_scatter(v, "fsdp", scatter_dimension=0, tiled=True).astype(F32)[None]
         for v in (d_gate, d_up, d_down)
     ]
-    d_rest = jnp.concatenate(
-        [
-            leading_contraction(two_all, grad_sg)[:, :fs],
-            leading_contraction(two_all, grad_su)[:, :fs],
-            leading_contraction(cot_all, shared_hidden)[:, :fs],
-        ],
-        1,
-    ).astype(BF)
-    d_rest = pad_last(d_rest, up_to(3 * fs)).reshape(count, 2, shard, -1)
-    grad_two_part, gg_part, d_rest, d_gate, d_up, d_down, output = meet(
-        grad_two_part, gg_part, d_rest, d_gate, d_up, d_down, output
-    )
-    rest_mine, rest_got = halves_sent(d_rest)
-    grad_two, grad_gates = reduce_blocks(
-        3,
-        grad_two_part.reshape(count, rows, D),
-        (gg_part.reshape(count, rows, -1), Scatter(count, gg_part.reshape(count, rows, -1), 1)),
-    )
 
     probs = probs_all[:rows]
     grad_logits = probs * (grad_gates - jnp.sum(probs * grad_gates, -1, keepdims=True))
@@ -823,92 +1308,65 @@
     grad_residual = cotangent[0] + norm_back(residual, residual_scale, gain_second, grad_two)
 
     attended = grad_residual.astype(BF)
-    grad_mixed = to_head(matmul(attended, output_full).astype(BF))
-    by_owner = jnp.take(attended.reshape(rows, count, -1), owners, axis=1).reshape(rows, -1)
-    grad_mixed, rest_mine, rest_got = meet(grad_mixed, rest_mine, rest_got)
+    output_own = lax.dynamic_slice_in_dim(output_full, me * VDIM, VDIM, 1)
+    attended_all, out_held, rest_mine = exchange(
+        count, 4, [attended], [Gather(count, attended, 4)], carry=[out_held, rest_mine]
+    )
     d_rest = (rest_mine.astype(F32) + rest_got.astype(F32)).astype(BF)
-    d_rest = lax.all_to_all(d_rest, "ctx", split_axis=0, concat_axis=0, tiled=True).astype(F32)
-
-    d_output = leading_contraction(by_owner, mixed).astype(BF)
-    d_output = box.scatter_step(d_output, len(box.dims) - 1)
+    out_parts = box.share(out_held, 0)
+    d_rest = lax.all_to_all(d_rest, "ctx", split_axis=0, concat_axis=0, tiled=True)
+    attended_all = attended_all.reshape(group, D)
+    mixed_own = mixed_f.astype(BF)
+    d_output = leading_contraction(attended_all, mixed_own)
+    grad_mixed = matmul(attended_all, output_own).astype(BF)
     delta = jnp.sum(grad_mixed.astype(F32) * mixed_f, -1, keepdims=True)
     probs_a = jnp.where(visible, jnp.exp(contract_last(query, keys) * scale - logsum), 0.0)
     grad_probs = contract_last(grad_mixed, values)
     grad_scores = (probs_a * (grad_probs - delta)).astype(BF)
-    grad_scores, d_output = meet(grad_scores, d_output)
-    for dim in reversed(range(1, len(box.dims) - 1)):
-        d_output = box.scatter_step(d_output, dim)
-    grad_query = matmul(grad_scores, keys) * scale
-    grad_keys = leading_contraction(grad_scores, query) * scale
+    output = residual + summed(out_parts, F32)
+    grad_query = matmul(grad_scores, keys)
+    grad_keys = leading_contraction(grad_scores, query)
     grad_values = leading_contraction(probs_a.astype(BF), grad_mixed)
-    grad_expanded = jnp.concatenate([grad_keys[:, :NOPE], grad_values], -1).astype(BF)
-    grad_latent = contract_last(grad_expanded, expand_own)
-    d_expand = leading_contraction(latent, grad_expanded)
-    d_latent = jnp.sum(grad_latent * low_part * latent_scale, 0)
-    grad_comp = jnp.concatenate(
-        [
-            norm_back(low_part, latent_scale, gain_latent, grad_latent),
-            turn(grad_keys[:, NOPE:], cosine, -sine),
-        ],
-        -1,
-    ).astype(BF)
-    grad_qraw = jnp.concatenate(
-        [grad_query[:, :NOPE], turn(grad_query[:, NOPE:], cosine[:asked], -sine[:asked])], -1
-    ).astype(BF)
-    grad_comp, d_output = meet(grad_comp, d_output)
-    d_output = box.scatter_step(d_output, 0)
-    d_query = leading_contraction(normed_all[:asked], grad_qraw)
-    d_compress = leading_contraction(normed_all, grad_comp)
-    d_first = (
-        jnp.sum(d_query * query_own.astype(F32), 1) + jnp.sum(d_compress * compress_full.astype(F32), 1)
-    ) / gain_first
-
-    d_q = halves_summed(d_query.reshape(count, 2, shard, -1)).astype(BF)
-    d_e = halves_summed(d_expand.reshape(count, 2, -1, d_expand.shape[-1])).astype(BF)
-    d_lat = jnp.pad(d_latent.reshape(all_devices, lat_rows), ((0, 0), (0, shard - lat_rows)))
-    d_small = jnp.concatenate(
-        [d_compress, d_router, d_first[:, None], d_second[:, None], d_lat.reshape(-1)[:, None]], 1
-    ).astype(BF)
-    d_small = pad_last(d_small, up_to(small_cols)).reshape(count, 2, shard, -1)
-    d_small = jnp.take(d_small, owners, axis=0)
-    d_small = jnp.where(half == 0, d_small, d_small[:, ::-1])
-    d_small = jnp.transpose(d_small, (1, 0, 2, 3)).reshape(2 * count, shard, -1)
-    from_query = contract_last(grad_qraw, query_own)
-    if repeat > 1:
-        from_query = jnp.pad(from_query, ((0, group - asked), (0, 0)))
-    grad_norm_part = (from_query + contract_last(grad_comp, compress_full)).astype(BF)
-    grad_norm_part, d_output, d_rest = meet(grad_norm_part, d_output, d_rest)
-    output_mine, output_got = halves_sent(d_output.reshape(1, 2, shard, -1))
-    grad_norm, d_small, d_q, d_e = reduce_blocks(
+    extra = jnp.concatenate([jnp.zeros_like(d_second)[:, None], d_second[:, None], d_router], 1)
+    extra = pad_last(extra, up_to(small_cols) - edge)
+    grad_norm_part, d_query, d_small, d_expand, d_latent = behind_attention(
+        grad_query, grad_keys, grad_values, normed_all, latent, low_part, gain_latent[None, :],
+        gain_first[:, None], query_own, small_all, expand_own, cosine, sine, extra,
+        [output],
+    )
+
+    d_latent = jnp.pad(d_latent.reshape(all_devices, lat_rows), ((0, 0), (0, shard - lat_rows)))
+    d_query = jnp.concatenate([d_query, d_output.astype(BF), d_latent.reshape(-1, 1).astype(BF)], 1)
+    d_q = d_query.reshape(count, 2, shard, -1)
+    d_e = d_expand.reshape(count, 2, -1, d_expand.shape[-1])
+    d_small = d_small.reshape(count, 2, shard, -1)
+    grad_norm, d_q, d_e, d_small = reduce_blocks(
         5,
         grad_norm_part.reshape(count, rows, D),
-        (d_small, Scatter(count, d_small, 1, both=True)),
-        (d_q, Deal(count, d_q)),
-        (d_e, Deal(count, d_e)),
-    )
-    output_mine, output_got = after(grad_norm, output_mine, output_got)
-    d_output = (output_mine.astype(F32) + output_got.astype(F32))[0]
+        [
+            (d_q, DealSum(count, d_q), (0.5, 0.55)),
+            (d_e, DealSum(count, d_e), (0.5, 0.56)),
+            (d_small, Scatter(count, d_small, 1, both=True), (0.25, 1.1)),
+        ],
+        [d_rest],
+    )
     grad_tokens = grad_residual + norm_back(hidden, norm_scale(hidden), gain_first, grad_norm)
 
-    def joined(parts, times):
-        if times > 1:
-            parts = jnp.sum(parts.astype(F32).reshape(count // times, times, *parts.shape[1:]), 1)
-        return jnp.transpose(parts.astype(F32), (1, 0, 2)).reshape(parts.shape[1], -1)
-
+    d_query, d_output, d_sgate, d_sup, d_sdown, d_expand = columns_of(d_rest, d_q, d_e, fs)
     return (
         output[None],
         grad_tokens[None],
-        d_small[:, edge + experts],
-        d_small[:lat_rows, edge + experts + 2],
-        joined(d_q, repeat),
+        d_small[:, edge],
+        jnp.sum(d_q[:, :lat_rows, width + VDIM].astype(F32), 0),
+        d_query,
         d_small[:, :edge],
-        joined(d_e, repeat),
+        d_expand,
         d_output,
-        d_small[:, edge + experts + 1],
-        d_small[:, edge : edge + experts],
-        joined(d_rest[:, :, :fs], 1),
-        joined(d_rest[:, :, fs : 2 * fs], 1),
-        joined(d_rest[:, :, 2 * fs : 3 * fs], 1),
+        d_small[:, edge + 1],
+        d_small[:, edge + 2 : edge + 2 + experts],
+        d_sgate,
+        d_sup,
+        d_sdown,
         *d_experts,
     )
 

time: 1120 us -> 1010 us (0.902)
  Pallas kernels: 361 us -> 646 us
  matrix products: 331 us -> 85.1 us
  other arithmetic: 146 us -> 96.5 us
  local copies, waits for them, and re-layouts: 100 us -> 56.4 us
  waiting for transfers between devices: 103 us -> 73.3 us
  starting transfers between devices: 51.8 us -> 32.4 us
    pallas_call x6 -> x14, Pallas kernels: 361 us -> 646 us  [the longest x6 460 us: exchange(): pl.pallas_call(functools.partial(exchange_kernel, count, plans, spans, le...]
    dot_general x15 -> x4, matrix products: 107 us -> 18.1 us  [matmul(): return jnp.dot(left, right, preferred_element_type=F32)]
    dot_general x12 -> x4, matrix products: 105 us -> 24 us  [contract_last(): lax.dot_general(left, right, (((1,), (1,)), ((), ())), preferred_element_...]
    dot_general x15 -> x8, matrix products: 119 us -> 43 us  [leading_contraction(): lax.dot_general(left, right, (((0,), (0,)), ((), ())), preferred_element_...]
    convert_element_type x15 -> x8, other arithmetic: 54.3 us -> 24.6 us  [the longest x2 7.7 us: summed(): return total.astype(dtype)]
    all_gather x2 -> x1, waiting for transfers between devices: 19.6 us -> 0.01 us  [local(): ups = lax.all_gather(up_cast.astype(BF), 'fsdp', axis=0, tiled=True)]
    reshape x9 -> x0, local copies, waits for them, and re-layouts: 11.9 us -> none  [the longest x6 6.82 us: joined(): jnp.transpose(parts.astype(F32), (1, 0, 2)).reshape(parts.shape[1], -1)]
    ppermute x20 -> x15, starting transfers between devices: 33.1 us -> 21.3 us  [shift(): lax.ppermute(value, 'ctx', [(i, target(i)) for i in range(self.count)])]
  transfers between devices with their start and end apart: 35 -> 25, of which waited for: 12 -> 6; matrix products, arithmetic and copies ran while one was open for 48% -> 21% of each run, Pallas kernels for 33% -> 58%
where the time goes in v2:
time: 1010 us
  Pallas kernels  646 us (64%)
  other arithmetic  96.5 us (10%)
  matrix products  85.1 us (8%)
  waiting for transfers between devices  73.3 us (7%)
  local copies, waits for them, and re-layouts  56.4 us (6%)
  starting transfers between devices  32.4 us (3%)
  between operations  15.4 us (2%)
    pallas_call x6, Pallas kernels, exchange(): pl.pallas_call(functools.partial(exchange_kernel, count, plans, spans, le...  460 us
    pallas_call x8, Pallas kernels, run(): pl.pallas_call(body, grid_spec=pltpu.PrefetchScalarGridSpec(num_scalar_pr...  186 us
    ppermute x15, waiting for transfers between devices, shift(): lax.ppermute(value, 'ctx', [(i, target(i)) for i in range(self.count)])  53.6 us
    dot_general x8, matrix products, leading_contraction(): lax.dot_general(left, right, (((0,), (0,)), ((), ())), preferred_element_...  43 us
    dot_general x4, matrix products, contract_last(): lax.dot_general(left, right, (((1,), (1,)), ((), ())), preferred_element_...  24 us
    ppermute x15, starting transfers between devices, shift(): lax.ppermute(value, 'ctx', [(i, target(i)) for i in range(self.count)])  21.3 us
  transfers between devices with their start and end apart: 25, of which 6 were waited for; matrix products, arithmetic and copies ran while one was open for 21% of the time, Pallas kernels for 58%

profile of v2, /device:TPU:0, one launch (start us, length us, event | category | flops | bytes accessed | tf_op | source)
XLA Modules:
  0.0 1005.3 jit_solution(18022899535601865599)
XLA Ops:
  12.2 4.6 convert_element_type.243
  18.2 5.0 collective-permute-start.2
  27.5 90.0 %shard_map.306 = (bf16[16,2,64,192]{3,2,1,0:T(8,128)(2,1)}, bf16[16,2,16,256]{3,2,1,0:T(8,128)(2,1)}, bf16[16,128,2048]{2,1,0:T(8,128)(2,1)}, bf16[128,2048]{1,0:T(8,128)(2,1)}) custom-call(bf16[16,64,192]{2,1,0:T(8,128)(2,1)} %bitcast.153, bf16[16,16,256]{2,1,0:T(8,128)(2,1)} %bitcast.163, ...), custom_call_target="tpu_custom_call", output_to_operand_aliasing={{3}: (3, {})} | custom-call | bytes 104857600 | tf_op jit(solution)/shard_map/pallas_call | solution.py:641
  117.5 4.1 collective-permute-start.7
  121.6 4.5 convert_element_type.249
  133.0 4.5 convert_bitcast_fusion.refs_3_.refs_10_
  137.9 3.7 fusion.28
  164.7 18.4 %shard_map.307 = (bf16[2048,2048]{1,0:T(8,128)(2,1)}, bf16[2048,192]{1,0:T(8,128)(2,1)}, bf16[2048,192]{1,0:T(8,128)(2,1)}, bf16[2048,128]{1,0:T(8,128)(2,1)}, b...) custom-call(bf16[2048,2048]{1,0:T(8,128)(2,1)} %bitcast.175, f32[1,2048]{1,0:T(1,128)} %bitcast.166, ...), custom_call_target="tpu_custom_call" | custom-call | flops 8388608000 | bytes 29894656 | tf_op jit(solution)/shard_map/pallas_call | solution.py:802
  183.0 5.9 fusion
  189.0 8.0 fusion.2
  197.0 7.1 fusion.50
  204.1 68.6 %shard_map.308 = (bf16[16,128,128]{2,1,0:T(8,128)(2,1)}, bf16[16,2,64,640]{3,2,1,0:T(8,128)(2,1)}, bf16[128,2048]{1,0:T(8,128)(2,1)}) custom-call(bf16[16,128,128]{2,1,0:T(8,128)(2,1)} %bitcast.159, bf16[16,64,640]{2,1,0:T(8,128)(2,1)} %fusion.15.refs_1_, s32[2048]{0:T(1024)} %get-tuple-element.220.refs_2_, ...), custom_call_target="tpu_custom_call", output_to_operand_aliasing={{2}: (4, {})} | custom-call | bytes 104857600 | tf_op jit(solution)/shard_map/pallas_call | solution.py:641
  277.1 19.5 %all-gather.9.cloned.1.call-done = bf16[2048,2048]{1,0:T(8,128)(2,1)} async-done(((bf16[64,2048]{1,0:T(8,128)(2,1)}), bf16[2048,2048]{1,0:T(8,128)(2,1)}) %all-gather.9.cloned.1.call-update) | async-done | bytes 8388624 | tf_op jit(solution)/shard_map/all_gather | solution.py:1176
  296.6 6.4 multiply_reduce_fusion.3
  304.0 67.3 %shard_map.309 = (bf16[16,128,2048]{2,1,0:T(8,128)(2,1)}, bf16[512,2048]{1,0:T(8,128)(2,1)}) custom-call(bf16[128,2048]{1,0:T(8,128)(2,1)} %multiply_convert_fusion.1.refs_0_, bf16[512,2048]{1,0:T(8,128)(2,1)} %pad_maximum_fusion.1.refs_1_), custom_call_target="tpu_custom_call", output_to_operand_aliasing={{1}: (1, {})} | custom-call | bytes 104857600 | tf_op jit(solution)/shard_map/pallas_call | solution.py:641
  379.8 3.6 fusion.51
  387.7 11.0 %shard_map.311 = (f32[2048,256]{1,0:T(8,128)}, f32[2048,256]{1,0:T(8,128)}, bf16[2048,256]{1,0:T(8,128)(2,1)}) custom-call(bf16[2048,2048]{1,0:T(8,128)(2,1)} %bitcast.133, bf16[2048,256]{1,0:T(8,128)(2,1)} %slice_select_fusion.refs_1_.refs_8_, bf16[2048,256]{1,0:T(8,128)(2,1)} %pad.40.refs_2_.refs_9_), custom_call_target="tpu_custom_call" | custom-call | flops 4294967296 | bytes 15728640 | tf_op jit(solution)/shard_map/pallas_call | solution.py:802
  398.7 21.0 %collective-permute-done.8 = bf16[512,2048]{1,0:T(8,128)(2,1)} collective-permute-done((bf16[512,2048]{1,0:T(8,128)(2,1)}, bf16[512,2048]{1,0:T(8,128)(2,1)}, u32[]{:S(2)}, u32[]{:S(2)}) %collective-permute-start.8) | collective-permute-done | bytes 2097184 | tf_op jit(solution)/shard_map/ppermute | solution.py:83
  419.7 28.8 %shard_map.310 = (bf16[1024,2048]{1,0:T(8,128)(2,1)}, f32[1024,1408]{1,0:T(8,128)}, f32[1024,1408]{1,0:T(8,128)}, bf16[1024,1408]{1,0:T(8,128)(2,1)}, bf16[512,2048]{1,0:T(8,128)(2,1)}) custom-call(s32[2]{0:T(128)} %pad_add_fusion.1.refs_0_, s32[9]{0:T(128)} %pad_add_fusion.2.refs_1_, ...), custom_call_target="tpu_custom_call", output_to_operand_aliasing={{4}: (6, {})} | custom-call | flops 11811160064 | bytes 38543360 | tf_op jit(solution)/shard_map/pallas_call | solution.py:802
  448.5 4.3 constant_dynamic-update-slice_fusion.12
  452.8 4.1 constant_dynamic-update-slice_fusion.11
  457.0 24.4 %shard_map.312 = (bf16[1024,2048]{1,0:T(8,128)(2,1)}, bf16[2048,2048]{1,0:T(8,128)(2,1)}) custom-call(s32[2]{0:T(128)} %pad_add_fusion.1.refs_0_, s32[9]{0:T(128)} %pad_add_fusion.2.refs_1_, bf16[1024,1408]{1,0:T(8,128)(2,1)} %get-tuple-element.84.refs_2_, bf16[1024,1408]{1,0:T(8,128)(2,1)} %convert_bitcast_fusion.refs_3_.refs_10_, ...), custom_call_target="tpu_custom_call" | custom-call | flops 8858370048 | bytes 23347200 | tf_op jit(solution)/shard_map/pallas_call | solution.py:802
  484.6 11.9 %collective-permute-done.11 = bf16[1024,2048]{1,0:T(8,128)(2,1)S(1)} collective-permute-done((bf16[1024,2048]{1,0:T(8,128)(2,1)S(1)}, bf16[1024,2048]{1,0:T(8,128)(2,1)S(1)}, u32[]{:S(2)}, u32[]{:S(2)}) %collective-permute-start.11) | collective-permute-done | bytes 4194336 | tf_op jit(solution)/shard_map/ppermute | solution.py:83
  496.4 4.0 add_convert_fusion.refs_12_
  502.7 40.5 %shard_map.313 = (bf16[1024,2048]{1,0:T(8,128)(2,1)}, bf16[1024,1408]{1,0:T(8,128)(2,1)}, bf16[1024,1408]{1,0:T(8,128)(2,1)}, bf16[1024,2048]{1,0:T(8,128)(2,1)}, f32[1024,1]{1,0:T(8,128)}) custom-call(s32[2]{0:T(128)} %pad_add_fusion.1.refs_0_, s32[9]{0:T(128)} %pad_add_fusion.2.refs_1_, s32[1,2048]{1,0:T(1,128)} %reshape_select_fusion.1.refs_2_, ...), custom_call_target="tpu_custom_call" | custom-call | flops 17716740096 | bytes 55595008 | tf_op jit(solution)/shard_map/pallas_call | solution.py:802
  543.2 11.0 %convolution_convert_fusion.refs_6_ = bf16[2048,1408]{1,0:T(8,128)(2,1)} fusion(bf16[1024,2048]{1,0:T(8,128)(2,1)} %get-tuple-element.100, bf16[1024,1408]{1,0:T(8,128)(2,1)} %get-tuple-element.84.refs_2_), kind=kOutput, calls=%fused_computation.13 | convolution fusion | flops 5908463616 | bytes 12845056 | tf_op jit(solution)/shard_map/dot_general | solution.py:32
  554.3 3.2 split.33
  559.3 26.2 %shard_map.314 = (bf16[2048,2048]{1,0:T(8,128)(2,1)}, bf16[2048,256]{1,0:T(8,128)(2,1)}, bf16[2048,256]{1,0:T(8,128)(2,1)}, f32[2048,16]{1,0:T(8,128)}) custom-call(s32[2]{0:T(128)} %pad_add_fusion.1.refs_0_, s32[9]{0:T(128)} %pad_add_fusion.2.refs_1_, s32[2048,1]{1,0:T(8,128)} %reshape_select_fusion.refs_5_.refs_2_, f32[1,1024]{1,0:T(1,128)} %bitcast.173, ...), custom_call_target="tpu_custom_call" | custom-call | flops 8589934592 | bytes 30552064 | tf_op jit(solution)/shard_map/pallas_call | solution.py:802
  585.5 19.0 %collective-permute-done.12 = bf16[512,2048]{1,0:T(8,128)(2,1)S(1)} collective-permute-done((bf16[512,2048]{1,0:T(8,128)(2,1)}, bf16[512,2048]{1,0:T(8,128)(2,1)S(1)}, u32[]{:S(2)}, u32[]{:S(2)}) %collective-permute-start.12) | collective-permute-done | bytes 2097184 | tf_op jit(solution)/shard_map/ppermute | solution.py:83
  604.4 3.7 add_convert_fusion.1.refs_5_.refs_1_
  608.2 73.1 %shard_map.315 = (f32[128,2048]{1,0:T(8,128)}, bf16[2048,1408]{1,0:T(8,128)(2,1)}, bf16[2048,1408]{1,0:T(8,128)(2,1)}, f32[128,16]{1,0:T(8,128)}) custom-call(bf16[16,128,2048]{2,1,0:T(8,128)(2,1)} %bitcast.144, bf16[1024,2048]{1,0:T(8,128)(2,1)} %get-tuple-element.96.refs_1_, bf16[1024,1408]{1,0:T(8,128)(2,1)} %get-tuple-element.97.refs_2_, ...), custom_call_target="tpu_custom_call" | custom-call | bytes 104857600 | tf_op jit(solution)/shard_map/pallas_call | solution.py:641
  682.6 5.9 fusion.55
  688.6 6.2 fusion.54
  711.4 57.3 %shard_map.316 = (bf16[16,128,2048]{2,1,0:T(8,128)(2,1)}, bf16[512,2048]{1,0:T(8,128)(2,1)}, bf16[16,64,640]{2,1,0:T(8,128)(2,1)}) custom-call(bf16[128,2048]{1,0:T(8,128)(2,1)} %get-tuple-element.216.refs_0_, bf16[512,2048]{1,0:T(8,128)(2,1)} %add_convert_fusion.1.refs_5_.refs_1_, ...), custom_call_target="tpu_custom_call", output_to_operand_aliasing={{1}: (1, {}), {2}: (2, {})} | custom-call | bytes 104857600 | tf_op jit(solution)/shard_map/pallas_call | solution.py:641
  768.7 6.8 convolution_convert_fusion.1
  776.6 7.0 collective-permute-start.13
  787.0 3.6 multiply_reduce_fusion.1
  790.6 10.0 multiply_convert_fusion
  800.7 3.7 fusion.57.refs_1_
  804.4 3.8 fusion.56.refs_0_
  808.3 5.9 fusion.4.refs_2_
  815.3 7.3 all-to-all-start
  830.4 32.8 %shard_map.317 = (bf16[2048,2048]{1,0:T(8,128)(2,1)}, bf16[2048,192]{1,0:T(8,128)(2,1)}, bf16[2048,640]{1,0:T(8,128)(2,1)}, bf16[512,256]{1,0:T(8,128)(2,1)}, f32[512,1]{1,0:T(8,128)}) custom-call(f32[2048,192]{1,0:T(8,128)} %fusion.56.refs_0_, f32[2048,192]{1,0:T(8,128)} %fusion.57.refs_1_, f32[2048,128]{1,0:T(8,128)} %fusion.4.refs_2_, ...), custom_call_target="tpu_custom_call" | custom-call | flops 16777216000 | bytes 36190208 | tf_op jit(solution)/shard_map/pallas_call | solution.py:802
  867.8 103.8 %shard_map.318 = (f32[128,2048]{1,0:T(8,128)}, bf16[16,64,321]{2,1,0:T(8,128)(2,1)}, bf16[16,16,256]{2,1,0:T(8,128)(2,1)}, f32[64,640]{1,0:T(8,128)}) custom-call(bf16[16,128,2048]{2,1,0:T(8,128)(2,1)} %bitcast.143, bf16[16,2,64,321]{3,2,1,0:T(8,128)(2,1)} %pad_maximum_fusion.2.refs_1_, bf16[16,2,16,256]{3,2,1,0:T(8,128)(2,1)} %bitcast.165, ...), custom_call_target="tpu_custom_call" | custom-call | bytes 104857600 | tf_op jit(solution)/shard_map/pallas_call | solution.py:641
  973.3 4.1 shard_map.319
  983.3 4.7 bitcast_convert_fusion
  988.0 4.7 bitcast_convert_fusion.1
  992.8 4.8 bitcast_convert_fusion.2
  (282 shorter events, 110.3 us)
Async XLA Ops:
  7.2 121.0 %copy-start = (s32[1,2048]{1,0:T(1,128)S(1)}, s32[1,2048]{1,0:T(1,128)}, u32[]{:S(2)}) copy-start(s32[1,2048]{1,0:T(1,128)} %param.22) | copy-start | bytes 24580
  7.2 151.6 %all-gather.7.cloned.1.call-start = ((), (), s32[]{:S(2)}) async-start(), calls=%async_computation.4 | async-start | bytes 2703360 | tf_op jit(solution)/shard_map/all_gather | solution.py:1150
  12.1 12.2 %copy-start.25 = (f32[16,4096]{1,0:T(8,128)S(1)}, f32[16,4096]{1,0:T(8,128)}, u32[]{:S(2)}) copy-start(f32[16,4096]{1,0:T(8,128)} %param.28) | copy-start | bytes 786436
  12.1 191.9 %all-gather.11.cloned.1.call-start = ((), (), s32[]{:S(2)}) async-start(), calls=%async_computation.9 | async-start | bytes 8650752 | tf_op jit(solution)/shard_map/all_gather | solution.py:1151
  16.7 9.9 copy-start.12
  16.8 279.9 %all-gather.9.cloned.1.call-start = ((), (), s32[]{:S(2)}) async-start(), calls=%async_computation.5 | async-start | bytes 8650752 | tf_op jit(solution)/shard_map/all_gather | solution.py:1176
  17.6 381.1 %all-gather.13.cloned.1.call-start = ((), (), s32[]{:S(2)}) async-start(), calls=%async_computation.10 | async-start | bytes 8650752 | tf_op jit(solution)/shard_map/all_gather | solution.py:1200
  18.2 126.6 %collective-permute-start.2 = (s32[128,6]{0,1:T(8,128)}, s32[128,6]{0,1:T(8,128)}, u32[]{:S(2)}, u32[]{:S(2)}) collective-permute-start(s32[128,6]{0,1:T(8,128)} %bitcast.130), channel_id=1, source_target_pairs={{0,24},{2,26},{4,28},{6,30},{8,0},{10,2},{12,4},{14,6},{16,8},{18,... | collective-permute-start | bytes 9224 | tf_op jit(solution)/shard_map/ppermute | solution.py:83
  23.3 122.5 %collective-permute-start.1 = (s32[128,6]{0,1:T(8,128)}, s32[128,6]{0,1:T(8,128)}, u32[]{:S(2)}, u32[]{:S(2)}) collective-permute-start(s32[128,6]{0,1:T(8,128)} %bitcast.130), channel_id=1, source_target_pairs={{0,16},{2,18},{4,20},{6,22},{8,24},{10,26},{12,28},{14,30},{16,0},... | collective-permute-start | bytes 9224 | tf_op jit(solution)/shard_map/ppermute | solution.py:83
  23.3 124.5 %collective-permute-start = (s32[128,6]{0,1:T(8,128)}, s32[128,6]{0,1:T(8,128)}, u32[]{:S(2)}, u32[]{:S(2)}) collective-permute-start(s32[128,6]{0,1:T(8,128)} %bitcast.130), channel_id=1, source_target_pairs={{0,8},{2,10},{4,12},{6,14},{8,16},{10,18},{12,20},{14,22},{16,24},... | collective-permute-start | bytes 9224 | tf_op jit(solution)/shard_map/ppermute | solution.py:83
  117.5 10.5 %copy-start.36 = (s32[1,4]{1,0:T(1,128)S(1)}, s32[1,4]{1,0:T(1,128)}, u32[]{:S(2)}) copy-start(s32[1,4]{1,0:T(1,128)} %param.21) | copy-start | bytes 52
  117.5 12.1 %copy-start.17 = (f32[64,2816]{1,0:T(8,128)S(1)}, f32[64,2816]{1,0:T(8,128)}, u32[]{:S(2)}) copy-start(f32[64,2816]{1,0:T(8,128)} %param.32) | copy-start | bytes 2162692
  117.5 86.5 %collective-permute-start.7 = (bf16[128,2048]{1,0:T(8,128)(2,1)}, bf16[128,2048]{1,0:T(8,128)(2,1)}, u32[]{:S(2)}, u32[]{:S(2)}) collective-permute-start(bf16[128,2048]{1,0:T(8,128)(2,1)} %get-tuple-element.78.refs_4_), channel_id=1, source_target_pairs={{0,24},{2,26},{4,28},{6,30},{8,0},{10,2},{12,4},{14,6},{16,8},{18,... | collective-permute-start | bytes 1572872 | tf_op jit(solution)/shard_map/ppermute | solution.py:83
  121.6 82.4 %collective-permute-start.6 = (bf16[128,2048]{1,0:T(8,128)(2,1)}, bf16[128,2048]{1,0:T(8,128)(2,1)}, u32[]{:S(2)}, u32[]{:S(2)}) collective-permute-start(bf16[128,2048]{1,0:T(8,128)(2,1)} %get-tuple-element.78.refs_4_), channel_id=1, source_target_pairs={{0,16},{2,18},{4,20},{6,22},{8,24},{10,26},{12,28},{14,30},{16,0},... | collective-permute-start | bytes 1572872 | tf_op jit(solution)/shard_map/ppermute | solution.py:83
  126.1 857.2 %reduce-scatter.8.cloned.1.call-start = ((), (), s32[]{:S(2)}) async-start(), calls=%async_computation.8 | async-start | bytes 8650752 | tf_op jit(solution)/shard_map/reduce_scatter | solution.py:1298
  137.9 11.9 %copy-start.26 = (s32[2048,6]{0,1:T(8,128)S(1)}, s32[2048,6]{0,1:T(8,128)}, u32[]{:S(2)}) copy-start(s32[2048,6]{0,1:T(8,128)} %get-tuple-element.249) | copy-start | bytes 147460
  137.9 11.9 %copy-start.33 = (s32[1024,6]{0,1:T(8,128)S(1)}, s32[1024,6]{0,1:T(8,128)}, u32[]{:S(2)}) copy-start(s32[1024,6]{0,1:T(8,128)} %get-tuple-element.248) | copy-start | bytes 73732
  144.9 59.1 %collective-permute-start.5 = (bf16[128,2048]{1,0:T(8,128)(2,1)S(1)}, bf16[128,2048]{1,0:T(8,128)(2,1)S(1)}, u32[]{:S(2)}, u32[]{:S(2)}) collective-permute-start(bf16[128,2048]{1,0:T(8,128)(2,1)S(1)} %copy-done.7), channel_id=1, source_target_pairs={{0,8},{2,10},{4,12},{6,14},{8,16},{10,18},{12,20},{14,22},{16,24},... | collective-permute-start | bytes 1572872 | tf_op jit(solution)/shard_map/ppermute | solution.py:83
  145.8 311.2 %collective-permute-start.10 = (bf16[1024,1408]{1,0:T(8,128)(2,1)}, bf16[1024,1408]{1,0:T(8,128)(2,1)}, u32[]{:S(2)}, u32[]{:S(2)}) collective-permute-start(bf16[1024,1408]{1,0:T(8,128)(2,1)} %convert_bitcast_fusion.refs_3_.refs_10_), channel_id=1, source_target_pairs={{0,1},{1,0},{2,3},{3,2},{4,5},{5,4},{6,7},{7,6},{8,9},{9,8},{10,11... | collective-permute-start | bytes 8650760 | tf_op jit(solution)/shard_map/ppermute | solution.py:1126
  148.5 3.7 collective-permute-start.3
  152.2 2.3 collective-permute-start.4
  164.7 18.4 %copy-start.28 = (s32[2048]{0:T(1024)S(1)}, s32[2048]{0:T(1024)}, u32[]{:S(2)}) copy-start(s32[2048]{0:T(1024)} %get-tuple-element.223) | copy-start | bytes 24580
  272.7 23.9 %copy-start.8 = (bf16[1,128,2048]{2,1,0:T(8,128)(2,1)S(1)}, bf16[1,128,2048]{2,1,0:T(8,128)(2,1)}, u32[]{:S(2)}) copy-start(bf16[1,128,2048]{2,1,0:T(8,128)(2,1)} %param.19) | copy-start | bytes 1572868
  371.3 48.4 %collective-permute-start.8 = (bf16[512,2048]{1,0:T(8,128)(2,1)}, bf16[512,2048]{1,0:T(8,128)(2,1)}, u32[]{:S(2)}, u32[]{:S(2)}) collective-permute-start(bf16[512,2048]{1,0:T(8,128)(2,1)} %get-tuple-element.82.refs_6_), channel_id=1, source_target_pairs={{0,4},{2,6},{4,0},{6,2},{8,12},{10,14},{12,8},{14,10},{16,20},{18,... | collective-permute-start | bytes 6291464 | tf_op jit(solution)/shard_map/ppermute | solution.py:83
  386.4 12.3 %copy-start.29 = (f32[2048]{0:T(1024)}, f32[2048]{0:T(1024)S(1)}, u32[]{:S(2)}) copy-start(f32[2048]{0:T(1024)S(1)} %get-tuple-element.218) | copy-start | bytes 24580
  481.3 15.1 %copy-start.6 = (bf16[2048,2048]{1,0:T(8,128)(2,1)S(1)}, bf16[2048,2048]{1,0:T(8,128)(2,1)}, u32[]{:S(2)}) copy-start(bf16[2048,2048]{1,0:T(8,128)(2,1)} %get-tuple-element.90) | copy-start | bytes 25165828
  484.0 12.4 %collective-permute-start.11 = (bf16[1024,2048]{1,0:T(8,128)(2,1)S(1)}, bf16[1024,2048]{1,0:T(8,128)(2,1)S(1)}, u32[]{:S(2)}, u32[]{:S(2)}) collective-permute-start(bf16[1024,2048]{1,0:T(8,128)(2,1)S(1)} %split.25), channel_id=1, source_target_pairs={{0,2},{2,0},{4,6},{6,4},{8,10},{10,8},{12,14},{14,12},{16,18},{18,... | collective-permute-start | bytes 12582920 | tf_op jit(solution)/shard_map/ppermute | solution.py:83
  484.1 16.3 %collective-permute-start.9 = (bf16[1024,2048]{1,0:T(8,128)(2,1)}, bf16[1024,2048]{1,0:T(8,128)(2,1)S(1)}, u32[]{:S(2)}, u32[]{:S(2)}) collective-permute-start(bf16[1024,2048]{1,0:T(8,128)(2,1)} %get-tuple-element.233.refs_9_), channel_id=1, source_target_pairs={{0,2},{2,0},{4,6},{6,4},{8,10},{10,8},{12,14},{14,12},{16,18},{18,... | collective-permute-start | bytes 12582920 | tf_op jit(solution)/shard_map/ppermute | solution.py:83
  554.2 433.8 %reduce-scatter.6.cloned.1.call-start = ((), (), s32[]{:S(2)}) async-start(), calls=%async_computation.7 | async-start | bytes 8650752 | tf_op jit(solution)/shard_map/reduce_scatter | solution.py:1298
  557.4 47.0 %collective-permute-start.12 = (bf16[512,2048]{1,0:T(8,128)(2,1)}, bf16[512,2048]{1,0:T(8,128)(2,1)S(1)}, u32[]{:S(2)}, u32[]{:S(2)}) collective-permute-start(bf16[512,2048]{1,0:T(8,128)(2,1)} %split.33), channel_id=1, source_target_pairs={{0,4},{2,6},{4,0},{6,2},{8,12},{10,14},{12,8},{14,10},{16,20},{18,... | collective-permute-start | bytes 6291464 | tf_op jit(solution)/shard_map/ppermute | solution.py:83
  681.3 311.4 %reduce-scatter.4.cloned.1.call-start = ((), (), s32[]{:S(2)}) async-start(), calls=%async_computation.6 | async-start | bytes 8650752 | tf_op jit(solution)/shard_map/reduce_scatter | solution.py:1298
  682.6 12.2 %slice-start = ((s8[8388608]{0:T(1024)(128)(4,1)}), s8[4194304]{0:T(1024)(128)(4,1)S(1)}, s32[]{:S(2)}) async-start(s8[8388608]{0:T(1024)(128)(4,1)} %bitcast.137), calls=%async_computation.11 | async-start | bytes 8388608
  704.4 79.8 %collective-permute-start.16 = (bf16[16,64,640]{2,1,0:T(8,128)(2,1)}, bf16[16,64,640]{2,1,0:T(8,128)(2,1)}, u32[]{:S(2)}, u32[]{:S(2)}) collective-permute-start(bf16[16,64,640]{2,1,0:T(8,128)(2,1)} %get-tuple-element.224), channel_id=1, source_target_pairs={{0,1},{1,0},{2,3},{3,2},{4,5},{5,4},{6,7},{7,6},{8,9},{9,8},{10,11... | collective-permute-start | bytes 3932168 | tf_op jit(solution)/shard_map/ppermute | solution.py:1126
  708.6 60.1 %copy-start.21 = (bf16[2048,128]{1,0:T(8,128)(2,1)S(1)}, bf16[2048,128]{1,0:T(8,128)(2,1)}, u32[]{:S(2)}) copy-start(bf16[2048,128]{1,0:T(8,128)(2,1)} %get-tuple-element.254) | copy-start | bytes 1572868
  768.7 15.6 %copy-start.5 = (bf16[16,64,640]{2,1,0:T(8,128)(2,1)S(1)}, bf16[16,64,640]{2,1,0:T(8,128)(2,1)}, u32[]{:S(2)}) copy-start(bf16[16,64,640]{2,1,0:T(8,128)(2,1)} %get-tuple-element.115) | copy-start | bytes 3932164
  768.7 18.3 %copy-start.35 = (bf16[16,128,2048]{2,1,0:T(8,128)(2,1)S(1)}, bf16[16,128,2048]{2,1,0:T(8,128)(2,1)}, u32[]{:S(2)}) copy-start(bf16[16,128,2048]{2,1,0:T(8,128)(2,1)} %get-tuple-element.106) | copy-start | bytes 25165828
  775.5 11.5 %copy-start.37 = (f32[2048,128]{1,0:T(8,128)S(1)}, f32[2048,128]{1,0:T(8,128)}, u32[]{:S(2)}) copy-start(f32[2048,128]{1,0:T(8,128)} %get-tuple-element.255) | copy-start | bytes 3145732
  776.6 49.7 %collective-permute-start.13 = (bf16[128,2048]{1,0:T(8,128)(2,1)}, bf16[128,2048]{1,0:T(8,128)(2,1)}, u32[]{:S(2)}, u32[]{:S(2)}) collective-permute-start(bf16[128,2048]{1,0:T(8,128)(2,1)} %get-tuple-element.230), channel_id=1, source_target_pairs={{0,24},{2,26},{4,28},{6,30},{8,0},{10,2},{12,4},{14,6},{16,8},{18,... | collective-permute-start | bytes 1572872 | tf_op jit(solution)/shard_map/ppermute | solution.py:83
  783.7 42.7 %collective-permute-start.15 = (bf16[128,2048]{1,0:T(8,128)(2,1)}, bf16[128,2048]{1,0:T(8,128)(2,1)}, u32[]{:S(2)}, u32[]{:S(2)}) collective-permute-start(bf16[128,2048]{1,0:T(8,128)(2,1)} %get-tuple-element.231), channel_id=1, source_target_pairs={{0,8},{2,10},{4,12},{6,14},{8,16},{10,18},{12,20},{14,22},{16,24},... | collective-permute-start | bytes 1572872 | tf_op jit(solution)/shard_map/ppermute | solution.py:83
  783.7 44.0 %collective-permute-start.14 = (bf16[128,2048]{1,0:T(8,128)(2,1)}, bf16[128,2048]{1,0:T(8,128)(2,1)}, u32[]{:S(2)}, u32[]{:S(2)}) collective-permute-start(bf16[128,2048]{1,0:T(8,128)(2,1)} %get-tuple-element.232), channel_id=1, source_target_pairs={{0,16},{2,18},{4,20},{6,22},{8,24},{10,26},{12,28},{14,30},{16,0},... | collective-permute-start | bytes 1572872 | tf_op jit(solution)/shard_map/ppermute | solution.py:83
  790.6 10.0 copy-start.38
  815.3 52.5 %all-to-all-start = ((bf16[16,64,640]{2,1,0:T(8,128)(2,1)}), bf16[16,64,640]{2,1,0:T(8,128)(2,1)}, u32[]{:S(2)}, u32[]{:S(2)}) async-start(bf16[16,64,640]{2,1,0:T(8,128)(2,1)} %add_convert_fusion.2), calls=%async_computation | async-start | bytes 2621440 | tf_op jit(solution)/shard_map/all_to_all | solution.py:1317
  830.4 34.3 %copy-start.22 = (bf16[2048,128]{1,0:T(8,128)(2,1)S(1)}, bf16[2048,128]{1,0:T(8,128)(2,1)}, u32[]{:S(2)}) copy-start(bf16[2048,128]{1,0:T(8,128)(2,1)} %convolution_convert_fusion.1) | copy-start | bytes 1572868
  867.8 112.6 %copy-start.9 = (bf16[1,128,2048]{2,1,0:T(8,128)(2,1)S(1)}, bf16[1,128,2048]{2,1,0:T(8,128)(2,1)}, u32[]{:S(2)}) copy-start(bf16[1,128,2048]{2,1,0:T(8,128)(2,1)} %param.19) | copy-start | bytes 1572868
  867.8 112.6 %copy-start.27 = (f32[2048]{0:T(1024)S(1)}, f32[2048]{0:T(1024)}, u32[]{:S(2)}) copy-start(f32[2048]{0:T(1024)} %get-tuple-element.211) | copy-start | bytes 24580
  971.6 10.4 %copy-start.13 = (f32[128,2048]{1,0:T(8,128)S(1)}, f32[128,2048]{1,0:T(8,128)}, u32[]{:S(2)}) copy-start(f32[128,2048]{1,0:T(8,128)} %get-tuple-element.217) | copy-start | bytes 3145732
  971.6 10.4 %copy-start.14 = (f32[128,2048]{1,0:T(8,128)S(1)}, f32[128,2048]{1,0:T(8,128)}, u32[]{:S(2)}) copy-start(f32[128,2048]{1,0:T(8,128)} %get-tuple-element.116) | copy-start | bytes 3145732
  988.0 10.2 %copy-start.1 = (s32[1,2048]{1,0:T(1,128)S(1)}, s32[1,2048]{1,0:T(1,128)}, u32[]{:S(2)}) copy-start(s32[1,2048]{1,0:T(1,128)} %param.22) | copy-start | bytes 24580
  (29 other events, 162.8 us)
Sparse Core Ops, SparseCore 0:
  12.2 78.3 all-gather.6
  92.7 93.5 all-gather.10
  189.9 106.6 all-gather.8
  298.6 81.0 all-gather.12
  554.3 72.6 reduce-scatter.7
  681.4 99.1 reduce-scatter.5
  782.9 71.3 reduce-scatter.3

commit v3 on v2

--- a/solution.py
+++ b/solution.py
@@ -685,11 +685,12 @@
             total_ref[...] += matmul(hot_rows(slot_ref[:, part], tile * TILE), source_ref[part])
 
 
-def expert_in_kernel(info, starts, slot, two, g0, u0, rows, gate, up, hidden, total):
+def expert_in_kernel(info, starts, slot, two, g0, u0, u1, rows, gate, up, hidden, total):
     pick_rows(starts, slot, two, total, pl.program_id(0))
     rows[...] = total[...].astype(BF)
     gate[...] = matmul(rows[...], g0[...])
-    up[...] = matmul(rows[...], u0[...])
+    own, other = split_of(info[0], rows.shape[1])
+    up[...] = matmul(rows[:, own], u0[...]) + matmul(rows[:, other], u1[...])
     value = gate[...]
     hidden[...] = (value / (1.0 + jnp.exp(-value)) * up[...]).astype(BF)
 
@@ -720,7 +721,7 @@
 
 
 def expert_back_kernel(
-    info, starts, slot, weight, cot, produced, gate, up, g0, u0, d0, d1,
+    info, starts, slot, weight, cot, produced, gate, up, g0, u0, u1, d0, d1,
     grad_in, grad_gate, grad_up, grad_rows, dots, total,
 ):
     tile = pl.program_id(0)
@@ -742,8 +743,9 @@
     act, slope = swiglu_parts(gate[...], up[...])
     grad_gate[...] = (grad_hidden * up[...] * slope).astype(BF)
     grad_up[...] = (grad_hidden * act).astype(BF)
-    back = contract_last(grad_gate[...], g0[...]) + contract_last(grad_up[...], u0[...])
-    grad_rows[...] = back.astype(BF)
+    total[...] = contract_last(grad_gate[...], g0[...])
+    for part, ups in ((own, u0), (other, u1)):
+        grad_rows[:, part] = (total[:, part] + contract_last(grad_up[...], ups[...])).astype(BF)
 
 
 def shared_in_kernel(two, sgate, sup, gate, up, hidden):
@@ -828,7 +830,7 @@
         like(capacity, hidden, F32),
         like(capacity, hidden, BF),
     )
-    values = [slot_row, two, gates, ups]
+    values = [slot_row, two, gates, *ups]
     return run(
         expert_in_kernel, capacity // TILE, (info, starts), values, [whole(v) for v in values],
         outs, tuple(tiled(o) for o in outs), [pltpu.VMEM((TILE, width), F32)],
@@ -868,7 +870,7 @@
         like(capacity, width, BF),
         like(capacity, 1, F32),
     )
-    values = [slot_row, weight_row, cot, produced, gate, up, gates, ups, *downs]
+    values = [slot_row, weight_row, cot, produced, gate, up, gates, *ups, *downs]
     specs = [whole(v) for v in values]
     specs[3:6] = [tiled(produced), tiled(gate), tiled(up)]
     return run(
@@ -1149,17 +1151,24 @@
     expand_parts = spread(expand_weight, count, repeat)
     small_all = lax.all_gather(small, both, axis=0, tiled=True)
     gates = lax.all_gather(expert_gate[0].astype(BF), "fsdp", axis=0, tiled=True)
-    query_own, expand_own, token_all, cot_low = exchange(
+    fs = shared_gate.shape[1] // count
+    fp = up_to(fs)
+    rest = jnp.concatenate(
+        [spread(shared_gate, count, 1), spread(shared_up, count, 1), spread(shared_down, count, 1)], -1
+    )
+    rest = pad_last(rest, up_to(3 * fs))
+    query_own, expand_own, token_all, rest_own, cot_low, down_own = exchange(
         count,
         0,
-        [query_parts, expand_parts, tokens[0]],
+        [query_parts, expand_parts, tokens[0], rest],
         [
             Deal(count, query_parts, both=True),
             Deal(count, expand_parts, both=True),
             Gather(count, tokens[0], 4),
+            Deal(count, rest, both=True),
         ],
-        spans=[(-2, -1), (-1, 0), (0, 1)],
-        carry=[cotangent[0].astype(BF)],
+        spans=[(-2, -1), (-1, 0), (0, 1), (1, 2)],
+        carry=[cotangent[0].astype(BF), expert_down[0].astype(BF)],
     )
     token_all = token_all.reshape(group, D)
     query_own = query_own.reshape(D, -1)
@@ -1174,13 +1183,7 @@
 
     output_cast = output_weight
     output_full = lax.all_gather(output_cast.astype(BF), both, axis=0, tiled=True)
-    route_own, gate_cols, up_cols, down_cols = routes[0], shared_gate, shared_up, shared_down
-    fs = shared_gate.shape[1] // count
-    fp = up_to(fs)
-    rest = jnp.concatenate(
-        [spread(gate_cols, count, 1), spread(up_cols, count, 1), spread(down_cols, count, 1)], -1
-    )
-    rest = pad_last(rest, up_to(3 * fs))
+    route_own = routes[0]
     cot_parts = box.spread(cot_low, 0)
 
     order_all = jnp.take(token_order[0].reshape(count, rows), owners, axis=0).reshape(-1)
@@ -1196,9 +1199,9 @@
         token_all, gain_first[None, :], gain_latent[None, :], query_own, small_all, expand_own,
         cosine, sine,
     )
-    up_cast, down_cast = expert_up[0], expert_down[0]
-    ups = lax.all_gather(up_cast.astype(BF), "fsdp", axis=0, tiled=True)
-    down_own = down_cast.astype(BF)
+    up_cast = expert_up[0]
+    up_own = up_cast.astype(BF)
+    ups = (up_own, across(up_own))
     downs = (down_own, across(down_own))
     scale = width ** (-0.5)
     visible = (sequence[:asked, None] == sequence[None, :]) & (
@@ -1216,13 +1219,10 @@
             value = jnp.pad(value, ((0, group - asked), (0, 0)))
         value = value.reshape(count, rows, -1)
         plan = Deal(count, value, pick=lambda me, to: offset_of(count, me, to))
-        got, rest_own, carried = exchange(
-            count, 1, [value, rest], [plan, Deal(count, rest, both=True)],
-            spans=[(0, 1), (1, 2)], needs=needs, carry=[carried],
-        )
+        got, carried = exchange(count, 1, [value], [plan], needs=needs, carry=[carried])
         if repeat > 1:
             got = jnp.sum(got.reshape(HEADS, repeat, rows, -1).astype(F32), 1).astype(BF)
-        return jnp.transpose(got, (1, 0, 2)).reshape(rows, -1), rest_own, carried
+        return jnp.transpose(got, (1, 0, 2)).reshape(rows, -1), carried
 
     route_all = box.gather(route_own)
     mine = jnp.any(route_all == me, -1)
@@ -1232,7 +1232,7 @@
     starts = jnp.concatenate([jnp.zeros((1,), jnp.int32), counted[TILE - 1 :: TILE]])
     column = jnp.arange(experts, dtype=jnp.int32)[None, :] == me
     info = jnp.stack([half, me]).astype(jnp.int32)
-    mixed, rest_own, cot_parts[0] = to_owner(mixed_f.astype(BF), [slot, gates], cot_parts[0])
+    mixed, cot_parts[0] = to_owner(mixed_f.astype(BF), [slot], cot_parts[0])
     cot_held = joined(cot_parts)
     hidden = tokens[0].astype(F32)
     residual = hidden + contract_last(mixed, output_full)
@@ -1246,8 +1246,8 @@
     cot_parts = box.spread(cot_held, 1)
     probs_all = jax.nn.softmax(matmul(two_all, router_full), -1)
     gate_col = jnp.sum(jnp.where(column & mine[:, None], probs_all, 0.0), -1, keepdims=True)
-    rows_in, gate_val, up_val, expert_hidden, cot_parts[0] = expert_in(
-        info, starts, (slot[None, :], capacity), two_all, gates, ups, [cot_parts[0]]
+    rows_in, gate_val, up_val, expert_hidden = expert_in(
+        info, starts, (slot[None, :], capacity), two_all, gates, ups, []
     )
     cot_held = joined(cot_parts)
     cot_all = joined(box.spread(cot_held, 2))

time: 1010 us -> 992 us (0.982)
  waiting for transfers between devices: 73.3 us -> 38.8 us
    all_gather x1, waiting for transfers between devices: 19.5 us -> 0.01 us  [local(): lax.all_gather(output_cast.astype(BF), both, axis=0, tiled=True)]
    ppermute x15, waiting for transfers between devices: 53.6 us -> 38.6 us  [shift(): lax.ppermute(value, 'ctx', [(i, target(i)) for i in range(self.count)])]
  transfers between devices with their start and end apart: 25 -> 25, of which waited for: 6 -> 3; matrix products, arithmetic and copies ran while one was open for 21% -> 23% of each run, Pallas kernels for 58% -> 59%
where the time goes in v3:
time: 992 us; the launch traced here: 983 us
  Pallas kernels  649 us (65%)
  other arithmetic  100 us (10%)
  matrix products  87.5 us (9%)
  local copies, waits for them, and re-layouts  61.4 us (6%)
  waiting for transfers between devices  38.8 us (4%)
  starting transfers between devices  31.4 us (3%)
  between operations  15.2 us (2%)
    pallas_call x6, Pallas kernels, exchange(): pl.pallas_call(functools.partial(exchange_kernel, count, plans, spans, le...  463 us
    pallas_call x8, Pallas kernels, run(): pl.pallas_call(body, grid_spec=pltpu.PrefetchScalarGridSpec(num_scalar_pr...  186 us
    dot_general x8, matrix products, leading_contraction(): lax.dot_general(left, right, (((0,), (0,)), ((), ())), preferred_element_...  43 us
    ppermute x15, waiting for transfers between devices, shift(): lax.ppermute(value, 'ctx', [(i, target(i)) for i in range(self.count)])  38.6 us
    dot_general x4, matrix products, contract_last(): lax.dot_general(left, right, (((1,), (1,)), ((), ())), preferred_element_...  24 us
    ppermute x15, starting transfers between devices, shift(): lax.ppermute(value, 'ctx', [(i, target(i)) for i in range(self.count)])  21.6 us
    dot_general x4, matrix products, matmul(): return jnp.dot(left, right, preferred_element_type=F32)  20.4 us
  transfers between devices with their start and end apart: 25, of which 3 were waited for; matrix products, arithmetic and copies ran while one was open for 23% of the time, Pallas kernels for 59%

profile of v3, /device:TPU:0, one launch (start us, length us, event | category | flops | bytes accessed | tf_op | source)
XLA Modules:
  0.0 983.2 jit_solution(10031673889819698731)
XLA Ops:
  15.4 5.0 collective-permute-start.2
  34.7 2.8 fusion.15.refs_3_
  40.3 155.3 %shard_map.306 = (bf16[16,2,64,192]{3,2,1,0:T(8,128)(2,1)}, bf16[16,2,16,256]{3,2,1,0:T(8,128)(2,1)}, bf16[16,128,2048]{2,1,0:T(8,128)(2,1)}, bf16[16,2,64,640]{...) custom-call(bf16[16,64,192]{2,1,0:T(8,128)(2,1)} %bitcast.152, ...), custom_call_target="tpu_custom_call", output_to_operand_aliasing={{4}: (4, {}), {5}: (5, {})} | custom-call | bytes 104857600 | tf_op jit(solution)/shard_map/pallas_call | solution.py:641
  196.8 4.7 convert_element_type.248
  204.0 4.7 convert_bitcast_fusion.refs_5_.refs_9_
  211.8 3.7 fusion.28
  243.3 18.4 %shard_map.307 = (bf16[2048,2048]{1,0:T(8,128)(2,1)}, bf16[2048,192]{1,0:T(8,128)(2,1)}, bf16[2048,192]{1,0:T(8,128)(2,1)}, bf16[2048,128]{1,0:T(8,128)(2,1)}, b...) custom-call(bf16[2048,2048]{1,0:T(8,128)(2,1)} %bitcast.175, f32[1,2048]{1,0:T(1,128)} %bitcast.166, ...), custom_call_target="tpu_custom_call" | custom-call | flops 8388608000 | bytes 29894656 | tf_op jit(solution)/shard_map/pallas_call | solution.py:804
  261.6 5.9 fusion
  267.5 7.6 fusion.2
  275.2 7.1 fusion.50
  282.3 13.9 %shard_map.308 = (bf16[16,128,128]{2,1,0:T(8,128)(2,1)}, bf16[128,2048]{1,0:T(8,128)(2,1)}) custom-call(bf16[16,128,128]{2,1,0:T(8,128)(2,1)} %bitcast.162, s32[2048]{0:T(1024)} %get-tuple-element.220.refs_1_, bf16[128,2048]{1,0:T(8,128)(2,1)} %get-tuple-element.78.refs_2_), custom_call_target="tpu_custom_call", output_to_operand_aliasing={{1}: (2, {})} | custom-call | bytes 104857600 | tf_op jit(solution)/shard_map/pallas_call | solution.py:641
  297.6 3.0 pad_maximum_fusion.1.refs_1_
  300.6 6.4 multiply_reduce_fusion.3
  308.0 63.0 %shard_map.309 = (bf16[16,128,2048]{2,1,0:T(8,128)(2,1)}, bf16[512,2048]{1,0:T(8,128)(2,1)}) custom-call(bf16[128,2048]{1,0:T(8,128)(2,1)} %multiply_convert_fusion.1.refs_0_, bf16[512,2048]{1,0:T(8,128)(2,1)} %pad_maximum_fusion.1.refs_1_), custom_call_target="tpu_custom_call", output_to_operand_aliasing={{1}: (1, {})} | custom-call | bytes 104857600 | tf_op jit(solution)/shard_map/pallas_call | solution.py:641
  371.0 5.9 fusion.51
  380.5 3.1 select_reduce_fusion
  387.5 11.0 %shard_map.311 = (f32[2048,256]{1,0:T(8,128)}, f32[2048,256]{1,0:T(8,128)}, bf16[2048,256]{1,0:T(8,128)(2,1)}) custom-call(bf16[2048,2048]{1,0:T(8,128)(2,1)} %bitcast.135, bf16[2048,256]{1,0:T(8,128)(2,1)} %slice_select_fusion.refs_1_.refs_8_, bf16[2048,256]{1,0:T(8,128)(2,1)} %pad.40.refs_2_.refs_9_), custom_call_target="tpu_custom_call" | custom-call | flops 4294967296 | bytes 15728640 | tf_op jit(solution)/shard_map/pallas_call | solution.py:804
  398.5 28.9 %shard_map.310 = (bf16[1024,2048]{1,0:T(8,128)(2,1)}, f32[1024,1408]{1,0:T(8,128)}, f32[1024,1408]{1,0:T(8,128)}, bf16[1024,1408]{1,0:T(8,128)(2,1)}) custom-call(s32[2]{0:T(128)} %pad_add_fusion.1.refs_0_, s32[9]{0:T(128)} %pad_add_fusion.2.refs_1_, s32[1,2048]{1,0:T(1,128)} %reshape_select_fusion.1.refs_2_, bf16[2048,2048]{1,0:T(8,128)(2,1)} %bitcast.136, ...), custom_call_target="tpu_custom_call" | custom-call | flops 11811160064 | bytes 38543360 | tf_op jit(solution)/shard_map/pallas_call | solution.py:804
  427.4 4.2 constant_dynamic-update-slice_fusion.11
  431.6 24.5 %shard_map.312 = (bf16[1024,2048]{1,0:T(8,128)(2,1)}, bf16[2048,2048]{1,0:T(8,128)(2,1)}) custom-call(s32[2]{0:T(128)} %pad_add_fusion.1.refs_0_, s32[9]{0:T(128)} %pad_add_fusion.2.refs_1_, bf16[1024,1408]{1,0:T(8,128)(2,1)} %get-tuple-element.83.refs_2_, bf16[1024,1408]{1,0:T(8,128)(2,1)} %get-tuple-element.84.refs_3_.refs_11_, ...), custom_call_target="tpu_custom_call" | custom-call | flops 8858370048 | bytes 23347200 | tf_op jit(solution)/shard_map/pallas_call | solution.py:804
  459.3 11.9 %collective-permute-done.12 = bf16[1024,2048]{1,0:T(8,128)(2,1)S(1)} collective-permute-done((bf16[1024,2048]{1,0:T(8,128)(2,1)S(1)}, bf16[1024,2048]{1,0:T(8,128)(2,1)S(1)}, u32[]{:S(2)}, u32[]{:S(2)}) %collective-permute-start.12) | collective-permute-done | bytes 4194336 | tf_op jit(solution)/shard_map/ppermute | solution.py:83
  471.2 4.0 add_convert_fusion.refs_13_
  477.5 40.8 %shard_map.313 = (bf16[1024,2048]{1,0:T(8,128)(2,1)}, bf16[1024,1408]{1,0:T(8,128)(2,1)}, bf16[1024,1408]{1,0:T(8,128)(2,1)}, bf16[1024,2048]{1,0:T(8,128)(2,1)}, f32[1024,1]{1,0:T(8,128)}) custom-call(s32[2]{0:T(128)} %pad_add_fusion.1.refs_0_, s32[9]{0:T(128)} %pad_add_fusion.2.refs_1_, s32[1,2048]{1,0:T(1,128)} %reshape_select_fusion.1.refs_2_, ...), custom_call_target="tpu_custom_call" | custom-call | flops 17716740096 | bytes 55595008 | tf_op jit(solution)/shard_map/pallas_call | solution.py:804
  518.3 11.0 %convolution_convert_fusion.refs_6_ = bf16[2048,1408]{1,0:T(8,128)(2,1)} fusion(bf16[1024,2048]{1,0:T(8,128)(2,1)} %get-tuple-element.100, bf16[1024,1408]{1,0:T(8,128)(2,1)} %get-tuple-element.83.refs_2_), kind=kOutput, calls=%fused_computation.13 | convolution fusion | flops 5908463616 | bytes 12845056 | tf_op jit(solution)/shard_map/dot_general | solution.py:32
  529.4 3.2 split.33
  536.5 25.9 %shard_map.314 = (bf16[2048,2048]{1,0:T(8,128)(2,1)}, bf16[2048,256]{1,0:T(8,128)(2,1)}, bf16[2048,256]{1,0:T(8,128)(2,1)}, f32[2048,16]{1,0:T(8,128)}) custom-call(s32[2]{0:T(128)} %pad_add_fusion.1.refs_0_, s32[9]{0:T(128)} %pad_add_fusion.2.refs_1_, s32[2048,1]{1,0:T(8,128)} %reshape_select_fusion.refs_5_.refs_2_, f32[1,1024]{1,0:T(1,128)} %bitcast.173, ...), custom_call_target="tpu_custom_call" | custom-call | flops 8589934592 | bytes 30552064 | tf_op jit(solution)/shard_map/pallas_call | solution.py:804
  562.3 18.0 %collective-permute-done.13 = bf16[512,2048]{1,0:T(8,128)(2,1)S(1)} collective-permute-done((bf16[512,2048]{1,0:T(8,128)(2,1)}, bf16[512,2048]{1,0:T(8,128)(2,1)S(1)}, u32[]{:S(2)}, u32[]{:S(2)}) %collective-permute-start.13) | collective-permute-done | bytes 2097184 | tf_op jit(solution)/shard_map/ppermute | solution.py:83
  580.3 3.8 add_convert_fusion.1.refs_5_.refs_1_
  584.1 75.0 %shard_map.315 = (f32[128,2048]{1,0:T(8,128)}, bf16[2048,1408]{1,0:T(8,128)(2,1)}, bf16[2048,1408]{1,0:T(8,128)(2,1)}, f32[128,16]{1,0:T(8,128)}) custom-call(bf16[16,128,2048]{2,1,0:T(8,128)(2,1)} %bitcast.145, bf16[1024,2048]{1,0:T(8,128)(2,1)} %get-tuple-element.96.refs_1_, bf16[1024,1408]{1,0:T(8,128)(2,1)} %get-tuple-element.97.refs_2_, ...), custom_call_target="tpu_custom_call" | custom-call | bytes 104857600 | tf_op jit(solution)/shard_map/pallas_call | solution.py:641
  660.4 5.9 fusion.55
  666.3 6.2 fusion.54
  687.9 58.4 %shard_map.316 = (bf16[16,128,2048]{2,1,0:T(8,128)(2,1)}, bf16[512,2048]{1,0:T(8,128)(2,1)}, bf16[16,64,640]{2,1,0:T(8,128)(2,1)}) custom-call(bf16[128,2048]{1,0:T(8,128)(2,1)} %get-tuple-element.216.refs_0_, bf16[512,2048]{1,0:T(8,128)(2,1)} %add_convert_fusion.1.refs_5_.refs_1_, ...), custom_call_target="tpu_custom_call", output_to_operand_aliasing={{1}: (1, {}), {2}: (2, {})} | custom-call | bytes 104857600 | tf_op jit(solution)/shard_map/pallas_call | solution.py:641
  746.3 6.8 convolution_convert_fusion.1
  754.3 6.9 collective-permute-start.14
  764.4 3.6 multiply_reduce_fusion.1
  768.1 10.1 %multiply_convert_fusion = bf16[2048,2048]{0,1:T(8,128)(2,1)S(1)} fusion(f32[2048,2048]{0,1:T(8,128)} %copy-done.4, bf16[2048,128]{1,0:T(8,128)(2,1)S(1)} %get-tuple-element.262, bf16[2048,128]{1,0:T(8,128)(2,1)S(1)} %copy-done.37, f32[2048]{0:T(1024)S(1)} %get-tuple-element.261, f32[2048]{0:T(1024)S(1)} %log_add_fusion, s32[2048]{0:T(1024)S(1)} %get-tuple-element.223, ...), kind=kOutput, calls=%fused_computation.1 | convolution fusion | flops 1111490560 | bytes 26247168 | tf_op jit(solution)/shard_map/dot_general | solution.py:28
  778.2 3.7 fusion.57.refs_1_
  781.9 3.8 fusion.56.refs_0_
  785.8 5.9 fusion.4.refs_2_
  792.8 7.2 all-to-all-start
  803.7 8.8 collective-permute-done.15
  815.2 32.7 %shard_map.317 = (bf16[2048,2048]{1,0:T(8,128)(2,1)}, bf16[2048,192]{1,0:T(8,128)(2,1)}, bf16[2048,640]{1,0:T(8,128)(2,1)}, bf16[512,256]{1,0:T(8,128)(2,1)}, f32[512,1]{1,0:T(8,128)}) custom-call(f32[2048,192]{1,0:T(8,128)} %fusion.56.refs_0_, f32[2048,192]{1,0:T(8,128)} %fusion.57.refs_1_, f32[2048,128]{1,0:T(8,128)} %fusion.4.refs_2_, ...), custom_call_target="tpu_custom_call" | custom-call | flops 16777216000 | bytes 36190208 | tf_op jit(solution)/shard_map/pallas_call | solution.py:804
  849.4 3.1 pad_maximum_fusion.2.refs_1_
  852.5 97.1 %shard_map.318 = (f32[128,2048]{1,0:T(8,128)}, bf16[16,64,321]{2,1,0:T(8,128)(2,1)}, bf16[16,16,256]{2,1,0:T(8,128)(2,1)}, f32[64,640]{1,0:T(8,128)}) custom-call(bf16[16,128,2048]{2,1,0:T(8,128)(2,1)} %bitcast.144, bf16[16,2,64,321]{3,2,1,0:T(8,128)(2,1)} %pad_maximum_fusion.2.refs_1_, bf16[16,2,16,256]{3,2,1,0:T(8,128)(2,1)} %bitcast.165, ...), custom_call_target="tpu_custom_call" | custom-call | bytes 104857600 | tf_op jit(solution)/shard_map/pallas_call | solution.py:641
  951.3 4.1 shard_map.319
  961.3 4.7 bitcast_convert_fusion
  966.0 4.7 bitcast_convert_fusion.1
  970.8 4.8 bitcast_convert_fusion.2
  (272 shorter events, 117.3 us)
Async XLA Ops:
  7.2 196.0 %copy-start = (s32[1,2048]{1,0:T(1,128)S(1)}, s32[1,2048]{1,0:T(1,128)}, u32[]{:S(2)}) copy-start(s32[1,2048]{1,0:T(1,128)} %param.22) | copy-start | bytes 24580
  7.2 19.0 %copy-start.17 = (f32[64,2816]{1,0:T(8,128)S(1)}, f32[64,2816]{1,0:T(8,128)}, u32[]{:S(2)}) copy-start(f32[64,2816]{1,0:T(8,128)} %param.33) | copy-start | bytes 2162692
  7.2 20.8 %copy-start.18 = (f32[64,2816]{1,0:T(8,128)S(1)}, f32[64,2816]{1,0:T(8,128)}, u32[]{:S(2)}) copy-start(f32[64,2816]{1,0:T(8,128)} %param.34) | copy-start | bytes 2162692
  7.2 230.0 %all-gather.5.cloned.1.call-start = ((), (), s32[]{:S(2)}) async-start(), calls=%async_computation.4 | async-start | bytes 2703360 | tf_op jit(solution)/shard_map/all_gather | solution.py:1152
  12.2 288.4 %all-gather.7.cloned.1.call-start = ((), (), s32[]{:S(2)}) async-start(), calls=%async_computation.5 | async-start | bytes 8650752 | tf_op jit(solution)/shard_map/all_gather | solution.py:1185
  14.1 384.4 %all-gather.9.cloned.1.call-start = ((), (), s32[]{:S(2)}) async-start(), calls=%async_computation.9 | async-start | bytes 8650752 | tf_op jit(solution)/shard_map/all_gather | solution.py:1153
  15.4 201.9 %collective-permute-start.2 = (s32[128,6]{0,1:T(8,128)}, s32[128,6]{0,1:T(8,128)S(1)}, u32[]{:S(2)}, u32[]{:S(2)}) collective-permute-start(s32[128,6]{0,1:T(8,128)} %bitcast.131), channel_id=1, source_target_pairs={{0,24},{2,26},{4,28},{6,30},{8,0},{10,2},{12,4},{14,6},{16,8},{18,... | collective-permute-start | bytes 9224 | tf_op jit(solution)/shard_map/ppermute | solution.py:83
  20.4 199.3 %collective-permute-start.1 = (s32[128,6]{0,1:T(8,128)}, s32[128,6]{0,1:T(8,128)S(1)}, u32[]{:S(2)}, u32[]{:S(2)}) collective-permute-start(s32[128,6]{0,1:T(8,128)} %bitcast.131), channel_id=1, source_target_pairs={{0,16},{2,18},{4,20},{6,22},{8,24},{10,26},{12,28},{14,30},{16,0},... | collective-permute-start | bytes 9224 | tf_op jit(solution)/shard_map/ppermute | solution.py:83
  20.4 199.4 %collective-permute-start = (s32[128,6]{0,1:T(8,128)}, s32[128,6]{0,1:T(8,128)}, u32[]{:S(2)}, u32[]{:S(2)}) collective-permute-start(s32[128,6]{0,1:T(8,128)} %bitcast.131), channel_id=1, source_target_pairs={{0,8},{2,10},{4,12},{6,14},{8,16},{10,18},{12,20},{14,22},{16,24},... | collective-permute-start | bytes 9224 | tf_op jit(solution)/shard_map/ppermute | solution.py:83
  26.2 12.2 %slice-start.6 = ((s8[5767168]{0:T(1024)(128)(4,1)}), s8[1572864]{0:T(1024)(128)(4,1)S(1)}, s32[]{:S(2)}) async-start(s8[5767168]{0:T(1024)(128)(4,1)} %bitcast.147), calls=%async_computation.16 | async-start | bytes 3145728
  29.9 7.7 copy-start.12
  195.6 86.7 %collective-permute-start.7 = (bf16[128,2048]{1,0:T(8,128)(2,1)}, bf16[128,2048]{1,0:T(8,128)(2,1)S(1)}, u32[]{:S(2)}, u32[]{:S(2)}) collective-permute-start(bf16[128,2048]{1,0:T(8,128)(2,1)} %get-tuple-element.78.refs_2_), channel_id=1, source_target_pairs={{0,24},{2,26},{4,28},{6,30},{8,0},{10,2},{12,4},{14,6},{16,8},{18,... | collective-permute-start | bytes 1572872 | tf_op jit(solution)/shard_map/ppermute | solution.py:83
  196.8 85.5 %collective-permute-start.6 = (bf16[128,2048]{1,0:T(8,128)(2,1)}, bf16[128,2048]{1,0:T(8,128)(2,1)}, u32[]{:S(2)}, u32[]{:S(2)}) collective-permute-start(bf16[128,2048]{1,0:T(8,128)(2,1)} %get-tuple-element.78.refs_2_), channel_id=1, source_target_pairs={{0,16},{2,18},{4,20},{6,22},{8,24},{10,26},{12,28},{14,30},{16,0},... | collective-permute-start | bytes 1572872 | tf_op jit(solution)/shard_map/ppermute | solution.py:83
  201.5 759.8 %reduce-scatter.8.cloned.1.call-start = ((), (), s32[]{:S(2)}) async-start(), calls=%async_computation.8 | async-start | bytes 8650752 | tf_op jit(solution)/shard_map/reduce_scatter | solution.py:1298
  217.3 65.0 %collective-permute-start.5 = (bf16[128,2048]{1,0:T(8,128)(2,1)S(1)}, bf16[128,2048]{1,0:T(8,128)(2,1)}, u32[]{:S(2)}, u32[]{:S(2)}) collective-permute-start(bf16[128,2048]{1,0:T(8,128)(2,1)S(1)} %copy-done.7), channel_id=1, source_target_pairs={{0,8},{2,10},{4,12},{6,14},{8,16},{10,18},{12,20},{14,22},{16,24},... | collective-permute-start | bytes 1572872 | tf_op jit(solution)/shard_map/ppermute | solution.py:83
  219.7 178.7 %collective-permute-start.10 = (bf16[1024,1408]{1,0:T(8,128)(2,1)}, bf16[1024,1408]{1,0:T(8,128)(2,1)}, u32[]{:S(2)}, u32[]{:S(2)}) collective-permute-start(bf16[1024,1408]{1,0:T(8,128)(2,1)} %convert_bitcast_fusion.refs_5_.refs_9_), channel_id=1, source_target_pairs={{0,1},{1,0},{2,3},{3,2},{4,5},{5,4},{6,7},{7,6},{8,9},{9,8},{10,11... | collective-permute-start | bytes 8650760 | tf_op jit(solution)/shard_map/ppermute | solution.py:1128
  220.5 4.3 collective-permute-start.3
  225.5 5.8 collective-permute-start.4
  231.3 200.3 %collective-permute-start.11 = (bf16[1024,1408]{1,0:T(8,128)(2,1)}, bf16[1024,1408]{1,0:T(8,128)(2,1)}, u32[]{:S(2)}, u32[]{:S(2)}) collective-permute-start(bf16[1024,1408]{1,0:T(8,128)(2,1)} %get-tuple-element.84.refs_3_.refs_11_), channel_id=1, source_target_pairs={{0,1},{1,0},{2,3},{3,2},{4,5},{5,4},{6,7},{7,6},{8,9},{9,8},{10,11... | collective-permute-start | bytes 8650760 | tf_op jit(solution)/shard_map/ppermute | solution.py:1128
  267.5 7.7 copy-start.4
  267.5 7.7 copy-start.36
  282.3 18.3 %copy-start.8 = (bf16[1,128,2048]{2,1,0:T(8,128)(2,1)S(1)}, bf16[1,128,2048]{2,1,0:T(8,128)(2,1)}, u32[]{:S(2)}) copy-start(bf16[1,128,2048]{2,1,0:T(8,128)(2,1)} %param.19) | copy-start | bytes 1572868
  371.0 9.5 copy-start.27
  378.3 49.1 %collective-permute-start.8 = (bf16[512,2048]{1,0:T(8,128)(2,1)S(1)}, bf16[512,2048]{1,0:T(8,128)(2,1)}, u32[]{:S(2)}, u32[]{:S(2)}) collective-permute-start(bf16[512,2048]{1,0:T(8,128)(2,1)S(1)} %copy-done.3), channel_id=1, source_target_pairs={{0,4},{2,6},{4,0},{6,2},{8,12},{10,14},{12,8},{14,10},{16,20},{18,... | collective-permute-start | bytes 6291464 | tf_op jit(solution)/shard_map/ppermute | solution.py:83
  383.6 14.8 %copy-start.24 = (f32[2048]{0:T(1024)}, f32[2048]{0:T(1024)S(1)}, u32[]{:S(2)}) copy-start(f32[2048]{0:T(1024)S(1)} %get-tuple-element.218) | copy-start | bytes 24580
  456.1 15.1 %copy-start.6 = (bf16[2048,2048]{1,0:T(8,128)(2,1)S(1)}, bf16[2048,2048]{1,0:T(8,128)(2,1)}, u32[]{:S(2)}) copy-start(bf16[2048,2048]{1,0:T(8,128)(2,1)} %get-tuple-element.90) | copy-start | bytes 25165828
  458.8 12.4 %collective-permute-start.12 = (bf16[1024,2048]{1,0:T(8,128)(2,1)S(1)}, bf16[1024,2048]{1,0:T(8,128)(2,1)S(1)}, u32[]{:S(2)}, u32[]{:S(2)}) collective-permute-start(bf16[1024,2048]{1,0:T(8,128)(2,1)S(1)} %split.25), channel_id=1, source_target_pairs={{0,2},{2,0},{4,6},{6,4},{8,10},{10,8},{12,14},{14,12},{16,18},{18,... | collective-permute-start | bytes 12582920 | tf_op jit(solution)/shard_map/ppermute | solution.py:83
  458.8 16.4 %collective-permute-start.9 = (bf16[1024,2048]{1,0:T(8,128)(2,1)}, bf16[1024,2048]{1,0:T(8,128)(2,1)S(1)}, u32[]{:S(2)}, u32[]{:S(2)}) collective-permute-start(bf16[1024,2048]{1,0:T(8,128)(2,1)} %get-tuple-element.233.refs_9_), channel_id=1, source_target_pairs={{0,2},{2,0},{4,6},{6,4},{8,10},{10,8},{12,14},{14,12},{16,18},{18,... | collective-permute-start | bytes 12582920 | tf_op jit(solution)/shard_map/ppermute | solution.py:83
  529.3 436.7 %reduce-scatter.6.cloned.1.call-start = ((), (), s32[]{:S(2)}) async-start(), calls=%async_computation.7 | async-start | bytes 8650752 | tf_op jit(solution)/shard_map/reduce_scatter | solution.py:1298
  532.6 47.8 %collective-permute-start.13 = (bf16[512,2048]{1,0:T(8,128)(2,1)}, bf16[512,2048]{1,0:T(8,128)(2,1)S(1)}, u32[]{:S(2)}, u32[]{:S(2)}) collective-permute-start(bf16[512,2048]{1,0:T(8,128)(2,1)} %split.33), channel_id=1, source_target_pairs={{0,4},{2,6},{4,0},{6,2},{8,12},{10,14},{12,8},{14,10},{16,20},{18,... | collective-permute-start | bytes 6291464 | tf_op jit(solution)/shard_map/ppermute | solution.py:83
  659.1 311.7 %reduce-scatter.4.cloned.1.call-start = ((), (), s32[]{:S(2)}) async-start(), calls=%async_computation.6 | async-start | bytes 8650752 | tf_op jit(solution)/shard_map/reduce_scatter | solution.py:1298
  660.4 12.2 %slice-start = ((s8[8388608]{0:T(1024)(128)(4,1)}), s8[4194304]{0:T(1024)(128)(4,1)S(1)}, s32[]{:S(2)}) async-start(s8[8388608]{0:T(1024)(128)(4,1)} %bitcast.138), calls=%async_computation.10 | async-start | bytes 8388608
  682.0 79.7 %collective-permute-start.17 = (bf16[16,64,640]{2,1,0:T(8,128)(2,1)}, bf16[16,64,640]{2,1,0:T(8,128)(2,1)}, u32[]{:S(2)}, u32[]{:S(2)}) collective-permute-start(bf16[16,64,640]{2,1,0:T(8,128)(2,1)} %get-tuple-element.224), channel_id=1, source_target_pairs={{0,1},{1,0},{2,3},{3,2},{4,5},{5,4},{6,7},{7,6},{8,9},{9,8},{10,11... | collective-permute-start | bytes 3932168 | tf_op jit(solution)/shard_map/ppermute | solution.py:1128
  685.1 61.2 %copy-start.21 = (bf16[2048,128]{1,0:T(8,128)(2,1)S(1)}, bf16[2048,128]{1,0:T(8,128)(2,1)}, u32[]{:S(2)}) copy-start(bf16[2048,128]{1,0:T(8,128)(2,1)} %get-tuple-element.254) | copy-start | bytes 1572868
  746.3 15.4 %copy-start.5 = (bf16[16,64,640]{2,1,0:T(8,128)(2,1)S(1)}, bf16[16,64,640]{2,1,0:T(8,128)(2,1)}, u32[]{:S(2)}) copy-start(bf16[16,64,640]{2,1,0:T(8,128)(2,1)} %get-tuple-element.115) | copy-start | bytes 3932164
  746.3 18.1 %copy-start.28 = (bf16[16,128,2048]{2,1,0:T(8,128)(2,1)S(1)}, bf16[16,128,2048]{2,1,0:T(8,128)(2,1)}, u32[]{:S(2)}) copy-start(bf16[16,128,2048]{2,1,0:T(8,128)(2,1)} %get-tuple-element.106) | copy-start | bytes 25165828
  753.1 11.3 %copy-start.30 = (f32[2048,128]{1,0:T(8,128)S(1)}, f32[2048,128]{1,0:T(8,128)}, u32[]{:S(2)}) copy-start(f32[2048,128]{1,0:T(8,128)} %get-tuple-element.255) | copy-start | bytes 3145732
  754.3 49.5 %collective-permute-start.14 = (bf16[128,2048]{1,0:T(8,128)(2,1)}, bf16[128,2048]{1,0:T(8,128)(2,1)}, u32[]{:S(2)}, u32[]{:S(2)}) collective-permute-start(bf16[128,2048]{1,0:T(8,128)(2,1)} %get-tuple-element.230), channel_id=1, source_target_pairs={{0,24},{2,26},{4,28},{6,30},{8,0},{10,2},{12,4},{14,6},{16,8},{18,... | collective-permute-start | bytes 1572872 | tf_op jit(solution)/shard_map/ppermute | solution.py:83
  761.1 42.6 %collective-permute-start.16 = (bf16[128,2048]{1,0:T(8,128)(2,1)}, bf16[128,2048]{1,0:T(8,128)(2,1)}, u32[]{:S(2)}, u32[]{:S(2)}) collective-permute-start(bf16[128,2048]{1,0:T(8,128)(2,1)} %get-tuple-element.231), channel_id=1, source_target_pairs={{0,8},{2,10},{4,12},{6,14},{8,16},{10,18},{12,20},{14,22},{16,24},... | collective-permute-start | bytes 1572872 | tf_op jit(solution)/shard_map/ppermute | solution.py:83
  761.1 51.4 %collective-permute-start.15 = (bf16[128,2048]{1,0:T(8,128)(2,1)}, bf16[128,2048]{1,0:T(8,128)(2,1)}, u32[]{:S(2)}, u32[]{:S(2)}) collective-permute-start(bf16[128,2048]{1,0:T(8,128)(2,1)} %get-tuple-element.232), channel_id=1, source_target_pairs={{0,16},{2,18},{4,20},{6,22},{8,24},{10,26},{12,28},{14,30},{16,0},... | collective-permute-start | bytes 1572872 | tf_op jit(solution)/shard_map/ppermute | solution.py:83
  768.1 10.1 %copy-start.31 = (bf16[2048,192]{1,0:T(8,128)(2,1)S(1)}, bf16[2048,192]{1,0:T(8,128)(2,1)}, u32[]{:S(2)}) copy-start(bf16[2048,192]{1,0:T(8,128)(2,1)} %get-tuple-element.75) | copy-start | bytes 2359300
  792.8 59.7 %all-to-all-start = ((bf16[16,64,640]{2,1,0:T(8,128)(2,1)}), bf16[16,64,640]{2,1,0:T(8,128)(2,1)}, u32[]{:S(2)}, u32[]{:S(2)}) async-start(bf16[16,64,640]{2,1,0:T(8,128)(2,1)} %add_convert_fusion.2), calls=%async_computation | async-start | bytes 2621440 | tf_op jit(solution)/shard_map/all_to_all | solution.py:1317
  815.2 34.2 %copy-start.20 = (bf16[2048,128]{1,0:T(8,128)(2,1)S(1)}, bf16[2048,128]{1,0:T(8,128)(2,1)}, u32[]{:S(2)}) copy-start(bf16[2048,128]{1,0:T(8,128)(2,1)} %convolution_convert_fusion.1) | copy-start | bytes 1572868
  852.5 105.9 %copy-start.9 = (bf16[1,128,2048]{2,1,0:T(8,128)(2,1)S(1)}, bf16[1,128,2048]{2,1,0:T(8,128)(2,1)}, u32[]{:S(2)}) copy-start(bf16[1,128,2048]{2,1,0:T(8,128)(2,1)} %param.19) | copy-start | bytes 1572868
  852.5 105.9 %copy-start.23 = (f32[2048]{0:T(1024)S(1)}, f32[2048]{0:T(1024)}, u32[]{:S(2)}) copy-start(f32[2048]{0:T(1024)} %get-tuple-element.211) | copy-start | bytes 24580
  949.6 10.4 %copy-start.13 = (f32[128,2048]{1,0:T(8,128)S(1)}, f32[128,2048]{1,0:T(8,128)}, u32[]{:S(2)}) copy-start(f32[128,2048]{1,0:T(8,128)} %get-tuple-element.217) | copy-start | bytes 3145732
  949.6 10.4 %copy-start.14 = (f32[128,2048]{1,0:T(8,128)S(1)}, f32[128,2048]{1,0:T(8,128)}, u32[]{:S(2)}) copy-start(f32[128,2048]{1,0:T(8,128)} %get-tuple-element.116) | copy-start | bytes 3145732
  966.0 10.2 %copy-start.1 = (s32[1,2048]{1,0:T(1,128)S(1)}, s32[1,2048]{1,0:T(1,128)}, u32[]{:S(2)}) copy-start(s32[1,2048]{1,0:T(1,128)} %param.22) | copy-start | bytes 24580
  (24 other events, 127.1 us)
Sparse Core Ops, SparseCore 0:
  12.3 72.1 all-gather.4
  88.1 117.0 all-gather.6
  207.3 155.8 all-gather.8
  529.5 73.1 reduce-scatter.7
  659.2 98.4 reduce-scatter.5
  759.9 71.3 reduce-scatter.3
